TPU v7x, 32 devices: a whole 2x2x4 slice. The times are simulated.
32 devices in a mesh: cluster: 8 (over z, x), narrow: 4 (over y, core).
Axes of the slice: x: 2, y: 2, z: 4, core: 2. Of those that a mesh axis runs over, the one named last changes fastest.
Arguments:
- edge_feats: bfloat16 [65536, 512], P(('cluster', 'narrow')), may hold values from -6 to 6
- cotangent: bfloat16 [65536, 512], P(('cluster', 'narrow')), may hold values from -6 to 6
- down_weight: bfloat16 [512, 64], replicated, may hold values from -0.25 to 0.25
- up_weight: bfloat16 [64, 512], replicated, may hold values from -0.75 to 0.75
- inner_weight: bfloat16 [1, 512, 512], replicated, may hold values from -0.25 to 0.25
- outer_weight: bfloat16 [1, 512, 512], replicated, may hold values from -0.25 to 0.25
- angular: bfloat16 [1024, 8, 4096], P(('cluster', 'narrow')), may hold values from -0.375 to 0.375
- reverse: int32 [65536], P(('cluster', 'narrow')), may hold values from 0 to 65535, as said below
- sources: int32 [1024, 8], P(('cluster', 'narrow')), may hold values from 0 to 1023, as said below
- counts: int32 [1024], P(('cluster', 'narrow')), may hold values from 1 to 8
Outputs:
- output: bfloat16 [65536, 512], P(('cluster', 'narrow'))
- grad_x: bfloat16 [65536, 512], P(('cluster', 'narrow'))
Inputs may be any that keep to these rules, and one draw needn't show every extreme that they name: reverse is an involution without fixed points, and reverse[e] // 2048 == ((e + 32768) % 65536) // 2048. sources[k, s] // 128 == k // 128; among the slots of the blocks of one device (blocks m * 32 to (m + 1) * 32 - 1), exactly 64 name a block j with (j % 128) // 32 == i, for every i below 4; slots s >= counts[k] hold valid block numbers that are not used.
All inputs are finite; a program needn't handle non-finite values.
Results may differ from a plain program's by a relative error of at most 0.0075.
Values may be sent and summed in bfloat16 or wider, within the bound.
No kernel may reach another device: no remote copies, remote signals or barrier semaphores. Data moves between devices by JAX's collectives and lax.ppermute only.
A program may use at most 128 MiB of HBM per device.

v0:
```python
import jax
import jax.numpy as jnp
from jax import lax
from jax.sharding import PartitionSpec as P

ROOT_HALF = 0.7071067811865476


def swapped(array, axis, bit):
    return lax.ppermute(array, axis, [(i, i ^ 1 << bit) for i in range(lax.axis_size(axis))])


def silu_grad(pre_act):
    squash = jax.nn.sigmoid(pre_act)
    return squash * (1.0 + pre_act * (1.0 - squash))


def dot_trans(operand, matrix):
    return lax.dot_general(
        operand, matrix, (((1,), (1,)), ((), ())), preferred_element_type=jnp.float32
    )


def split_parts(values):
    high_part = values.astype(jnp.bfloat16)
    low_part = (values - high_part.astype(jnp.float32)).astype(jnp.bfloat16)
    return (high_part, low_part)


def on_device(
    edge_feats,
    cotangent,
    down_weight,
    up_weight,
    inner_weight,
    outer_weight,
    angular,
    reverse,
    sources,
    counts,
):
    lane_count = lax.axis_size("narrow")
    top_bit = lax.axis_size("cluster").bit_length() - 2
    local_blocks = counts.shape[0]
    local_edges = edge_feats.shape[0]
    block_edges = local_edges // local_blocks
    trip_width = down_weight.shape[1]
    slot_count = sources.shape[1]
    cluster_blocks = local_blocks * lane_count
    source_local = sources % cluster_blocks
    live_mask = lax.broadcasted_iota(jnp.int32, sources.shape, 1) < counts[:, None]
    rev_slot = reverse % local_edges
    angle_mats = angular.reshape(local_blocks, slot_count, block_edges, block_edges)

    def one_hot(row_count, out_type):
        columns = lax.broadcasted_iota(jnp.int32, (1, 1, row_count), 2)
        return ((source_local[:, :, None] == columns) & live_mask[:, :, None]).astype(out_type)

    pre_down = jnp.dot(edge_feats, down_weight, preferred_element_type=jnp.float32)
    trip_feat = jax.nn.silu(pre_down).astype(jnp.bfloat16)
    trip_blocks = trip_feat.reshape(local_blocks, block_edges * trip_width)
    shard_piece = lax.all_gather(trip_blocks, "narrow", axis=0, tiled=True)
    selector = one_hot(shard_piece.shape[0], jnp.bfloat16)
    picked = jnp.einsum("ksp,pf->ksf", selector, shard_piece, preferred_element_type=jnp.float32)
    picked = picked.astype(jnp.bfloat16).reshape(local_blocks, slot_count, block_edges, trip_width)
    trip_sum = jnp.einsum("ksij,ksjf->kif", angle_mats, picked, preferred_element_type=jnp.float32)
    trip_round = trip_sum.reshape(local_edges, trip_width).astype(jnp.bfloat16)
    pre_up = jnp.dot(trip_round, up_weight, preferred_element_type=jnp.float32)
    up_feat = jax.nn.silu(pre_up).astype(jnp.bfloat16)
    partner_trip = swapped(trip_round, "cluster", top_bit)
    partner_pre = jnp.dot(partner_trip[rev_slot], up_weight, preferred_element_type=jnp.float32)
    partner_up = jax.nn.silu(partner_pre).astype(jnp.bfloat16)
    message = (up_feat.astype(jnp.float32) + partner_up.astype(jnp.float32)) * ROOT_HALF
    hidden_state = (edge_feats.astype(jnp.float32) + message) * ROOT_HALF
    layer_index = 0
    state_round = hidden_state.astype(jnp.bfloat16)
    pre_in = jnp.dot(state_round, inner_weight[layer_index], preferred_element_type=jnp.float32)
    act_feat = jax.nn.silu(pre_in).astype(jnp.bfloat16)
    pre_out = jnp.dot(act_feat, outer_weight[layer_index], preferred_element_type=jnp.float32)
    saved_acts = [(pre_in, pre_out)]
    hidden_state = (hidden_state + jax.nn.silu(pre_out)) * ROOT_HALF
    output = hidden_state.astype(jnp.bfloat16)
    grad_state = cotangent.astype(jnp.float32)
    for layer_index in reversed(range(inner_weight.shape[0])):
        pre_in, pre_out = saved_acts[layer_index]
        grad_state = grad_state * ROOT_HALF
        grad_out = (grad_state * silu_grad(pre_out)).astype(jnp.bfloat16)
        grad_act = dot_trans(grad_out, outer_weight[layer_index])
        grad_in = (grad_act * silu_grad(pre_in)).astype(jnp.bfloat16)
        grad_state = grad_state + dot_trans(grad_in, inner_weight[layer_index])
    grad_msg = grad_state * ROOT_HALF
    grad_msg_round = grad_msg.astype(jnp.bfloat16)
    partner_grad = swapped(grad_msg_round, "cluster", top_bit)[rev_slot]
    grad_up = (grad_msg + partner_grad.astype(jnp.float32)) * ROOT_HALF
    grad_pre_up = (grad_up * silu_grad(pre_up)).astype(jnp.bfloat16)
    grad_trip = dot_trans(grad_pre_up, up_weight).astype(jnp.bfloat16)
    grad_blocks = grad_trip.reshape(local_blocks, block_edges, trip_width)
    pair_terms = jnp.einsum(
        "ksij,kif->ksjf", angle_mats, grad_blocks, preferred_element_type=jnp.float32
    )
    pair_terms = pair_terms.reshape(local_blocks, slot_count, block_edges * trip_width)
    high_terms, low_terms = split_parts(pair_terms)
    selector = one_hot(lax.axis_size("narrow") * local_blocks, jnp.bfloat16)
    upper = jnp.einsum("ksp,ksf->pf", selector, high_terms, preferred_element_type=jnp.float32)
    source_grad = lax.psum_scatter(
        (
            upper
            + jnp.einsum("ksp,ksf->pf", selector, low_terms, preferred_element_type=jnp.float32)
        ).astype(jnp.bfloat16),
        "narrow",
        scatter_dimension=0,
        tiled=True,
    ).astype(jnp.float32)
    source_grad = source_grad.reshape(local_edges, trip_width)
    grad_pre_down = (source_grad * silu_grad(pre_down)).astype(jnp.bfloat16)
    grad_x = grad_msg + dot_trans(grad_pre_down, down_weight)
    return (output, grad_x.astype(jnp.bfloat16))


def solution(mesh):
    in_specs = (
        P(("cluster", "narrow"), None),
        P(("cluster", "narrow"), None),
        P(),
        P(),
        P(),
        P(),
        P(("cluster", "narrow"), None, None),
        P(("cluster", "narrow")),
        P(("cluster", "narrow"), None),
        P(("cluster", "narrow")),
    )
    out_specs = (P(("cluster", "narrow"), None), P(("cluster", "narrow"), None))
    return jax.shard_map(
        on_device, mesh=mesh, in_specs=in_specs, out_specs=out_specs, check_vma=False
    )
```

profile of v0, /device:TPU:0, one launch (start us, length us, event | category | flops | bytes accessed | tf_op | source)
XLA Modules:
  0.0 273.8 jit_solution(3064374930113418047)
XLA Ops:
  7.2 0.0 copy-start
  7.2 0.0 copy-start.3
  7.2 0.0 all-gather.2.cloned.1.call-start
  7.2 3.3 %multiply_convert_fusion.13 = (bf16[2048,64]{0,1:T(8,128)(2,1)S(1)}, f32[2048,64]{0,1:T(8,128)}) fusion(bf16[2048,512]{1,0:T(8,128)(2,1)} %param.10, bf16[512,64]{0,1:T(8,128)(2,1)} %param.12), kind=kOutput, calls=%fused_computation.40 | convolution fusion | flops 134873088 | bytes 2949120 | tf_op jit(solution)/shard_map/dot_general | solution.py:59
  10.5 0.3 copy.15
  10.8 1.2 reshape.47
  12.0 0.0 all-gather.2.cloned.1.call-update
  12.0 0.0 reduce-scatter.2.cloned.1.call-start
  12.1 0.0 copy-done.3
  12.1 5.6 %reshape.49 = bf16[32,8,64,64]{3,2,1,0:T(8,128)(2,1)} reshape(bf16[32,8,4096]{2,1,0:T(8,128)(2,1)S(1)} %copy-done.3) | data formatting | bytes 4194304 | tf_op jit(solution)/shard_map/reshape | solution.py:53
  17.6 0.0 copy-done.10
  17.7 0.0 copy-done.9
  17.7 0.0 copy-done.8
  17.7 0.1 fusion.18
  17.9 13.8 %all-gather.2.cloned.1.call-done = bf16[128,4096]{1,0:T(8,128)(2,1)} async-done(((bf16[32,4096]{1,0:T(8,128)(2,1)}), bf16[128,4096]{1,0:T(8,128)(2,1)}) %all-gather.2.cloned.1.call-update) | async-done | bytes 1048592 | tf_op jit(solution)/shard_map/all_gather | solution.py:62
  31.6 1.9 convolution_convert_fusion
  33.5 5.5 %reshape.48 = bf16[32,8,64,64]{3,2,1,0:T(8,128)(2,1)} reshape(bf16[32,8,4096]{2,1,0:T(8,128)(2,1)S(1)} %convolution_convert_fusion) | data formatting | bytes 4194304 | tf_op jit(solution)/shard_map/reshape | solution.py:65
  39.1 4.8 %fusion.9 = bf16[32,64,64]{1,2,0:T(8,128)(2,1)S(1)} fusion(bf16[32,8,64,64]{3,2,1,0:T(8,128)(2,1)} %reshape.48, bf16[32,8,64,64]{3,2,1,0:T(8,128)(2,1)} %reshape.49), kind=kOutput, calls=%fused_computation.32 | convolution fusion | flops 134348800 | bytes 4456448 | tf_op jit(solution)/shard_map/ksij,ksjf->kif/dot_general | solution.py:66
  43.9 0.3 copy.18
  44.2 0.5 convert_element_type.86
  44.7 0.3 copy.19
  45.0 2.5 collective-permute-start
  47.4 0.0 copy-done.6
  47.4 2.7 fusion.36
  50.1 21.1 %collective-permute-done = bf16[2048,64]{1,0:T(8,128)(2,1)S(1)} collective-permute-done((bf16[2048,64]{1,0:T(8,128)(2,1)S(1)}, bf16[2048,64]{1,0:T(8,128)(2,1)S(1)}, u32[]{:S(2)}, u32[]{:S(2)}) %collective-permute-start) | collective-permute-done | bytes 262176 | tf_op jit(solution)/shard_map/ppermute | solution.py:10
  71.2 6.2 %gather_fusion = bf16[2048,64]{1,0:T(8,128)(2,1)S(1)} fusion(bf16[2048,64]{1,0:T(8,128)(2,1)S(1)} %collective-permute-done, s32[2048]{0:T(1024)S(1)} %fusion.21), kind=kCustom, calls=%fused_computation | custom fusion | bytes 532480 | tf_op jit(solution)/shard_map/gather | solution.py:71
  77.4 0.0 copy-start.5
  77.4 4.5 %add_multiply_fusion.1 = f32[2048,512]{1,0:T(8,128)S(1)} fusion(bf16[2048,512]{1,0:T(8,128)(2,1)} %param.10, bf16[2048,64]{1,0:T(8,128)(2,1)S(1)} %gather_fusion, bf16[64,512]{1,0:T(8,128)(2,1)S(1)} %copy-done.6, f32[2048,512]{1,0:T(8,128)} %fusion.36), kind=kOutput, calls=%fused_computation.18 | convolution fusion | flops 152043520 | bytes 10813440 | tf_op jit(solution)/shard_map/dot_general | solution.py:71
  82.0 1.2 fusion.4
  83.2 4.0 %multiply_convert_fusion.3 = (bf16[2048,512]{1,0:T(8,128)(2,1)}, f32[2048,512]{1,0:T(8,128)}) fusion(f32[2048,512]{1,0:T(8,128)S(1)} %add_multiply_fusion.1, bf16[1,512,512]{2,1,0:T(8,128)(2,1)S(1)} %copy-done, f32[2048,512]{1,0:T(8,128)S(1)} %fusion.4), kind=kOutput, calls=%fused_computation.14 | convolution fusion | flops 1086324736 | bytes 15204352 | tf_op jit(solution)/shard_map/dot_general | solution.py:79
  87.2 10.0 %fusion.33 = (bf16[2048,512]{1,0:T(8,128)(2,1)}, f32[2048,512]{1,0:T(8,128)}) fusion(bf16[1,512,512]{2,1,0:T(8,128)(2,1)S(1)} %copy-done.5, f32[2048,512]{1,0:T(8,128)} %copy-done.2, f32[2048,512]{1,0:T(8,128)} %get-tuple-element.7, bf16[2048,512]{1,0:T(8,128)(2,1)} %param.11, bf16[1,512,512]{2,1,0:T(8,128)(2,1)S(1)} %copy-done), kind=kOutput, calls=%fused_computation.63 | convolution fusion | flops 2173698048 | bytes 17825792 | tf_op jit(solution)/shard_map/dot_general | solution.py:19
  97.3 0.0 collective-permute-start.1
  97.3 93.0 %collective-permute-done.1 = bf16[2048,512]{1,0:T(8,128)(2,1)S(1)} collective-permute-done((bf16[2048,512]{1,0:T(8,128)(2,1)}, bf16[2048,512]{1,0:T(8,128)(2,1)S(1)}, u32[]{:S(2)}, u32[]{:S(2)}) %collective-permute-start.1) | collective-permute-done | bytes 2097184 | tf_op jit(solution)/shard_map/ppermute | solution.py:10
  190.3 9.2 %gather_fusion.1 = bf16[2048,512]{1,0:T(8,128)(2,1)} fusion(bf16[2048,512]{1,0:T(8,128)(2,1)S(1)} %collective-permute-done.1, s32[2048]{0:T(1024)S(1)} %fusion.21), kind=kCustom, calls=%fused_computation.1 | custom fusion | bytes 4202496 | tf_op jit(solution)/shard_map/gather | solution.py:93
  199.5 6.0 %convolution_convert_fusion.1 = bf16[2048,64]{0,1:T(8,128)(2,1)S(1)} fusion(bf16[64,512]{1,0:T(8,128)(2,1)S(1)} %copy-done.6, f32[2048,512]{1,0:T(8,128)} %fusion.36, f32[2048,512]{1,0:T(8,128)} %get-tuple-element.9, bf16[2048,512]{1,0:T(8,128)(2,1)} %gather_fusion.1), kind=kOutput, calls=%fused_computation.23 | convolution fusion | flops 146931712 | bytes 10813440 | tf_op jit(solution)/shard_map/dot_general | solution.py:19
  205.5 0.5 reshape.50
  206.0 6.7 %convolution_bitcast_fusion.2 = f32[32,8,64,64]{2,3,1,0:T(8,128)} fusion(bf16[32,8,64,64]{3,2,1,0:T(8,128)(2,1)} %reshape.49, bf16[32,64,64,1]{1,0,2,3:T(8,128)(2,1)S(1)} %bitcast.57), kind=kOutput, calls=%fused_computation.22 | convolution fusion | flops 134217728 | bytes 6553600 | tf_op jit(solution)/shard_map/ksij,kif->ksjf/dot_general | solution.py:98
  212.6 9.0 %copy.21 = f32[32,8,64,64]{3,2,1,0:T(8,128)} copy(f32[32,8,64,64]{2,3,1,0:T(8,128)} %convolution_bitcast_fusion.2) | data formatting | bytes 8388608 | tf_op jit(solution)/shard_map/ksij,kif->ksjf/dot_general | solution.py:98
  221.6 7.9 %reshape.51 = f32[32,8,4096]{2,1,0:T(8,128)} reshape(f32[32,8,64,64]{3,2,1,0:T(8,128)} %copy.21) | data formatting | bytes 8388608 | tf_op jit(solution)/shard_map/reshape | solution.py:101
  229.5 4.4 %subtract_convert_fusion = (bf16[32,8,4096]{2,1,0:T(8,128)(2,1)S(1)}, bf16[32,8,4096]{2,1,0:T(8,128)(2,1)S(1)}) fusion(f32[32,8,4096]{2,1,0:T(8,128)} %reshape.51), kind=kLoop, calls=%fused_computation.8 | loop fusion | flops 4194304 | bytes 8388608 | tf_op jit(solution)/shard_map/convert_element_type | solution.py:26
  234.0 1.5 convolution_bitcast_fusion
  235.5 0.0 copy-start.7
  235.5 2.5 fusion.1
  238.0 0.0 reduce-scatter.2.cloned.1.call-update
  238.0 22.9 %reduce-scatter.2.cloned.1.call-done = bf16[32,4096]{1,0:T(8,128)(2,1)} async-done(((bf16[128,4096]{1,0:T(8,128)(2,1)}), bf16[32,4096]{1,0:T(8,128)(2,1)}) %reduce-scatter.2.cloned.1.call-update) | async-done | bytes 262160 | tf_op jit(solution)/shard_map/reduce_scatter | solution.py:105
  260.9 1.4 reshape.55
  262.3 0.3 copy.24
  262.7 4.3 %add_convert_fusion = bf16[2048,512]{1,0:T(8,128)(2,1)} fusion(f32[2048,512]{1,0:T(8,128)} %get-tuple-element.9, bf16[512,64]{0,1:T(8,128)(2,1)S(1)} %copy-done.7, f32[2048,64]{0,1:T(8,128)S(1)} %copy.24, f32[2048,64]{0,1:T(8,128)S(1)} %copy-done.4), kind=kOutput, calls=%fused_computation.7 | convolution fusion | flops 137494528 | bytes 7405568 | tf_op jit(solution)/shard_map/dot_general | solution.py:19
  (16 shorter events, 0.1 us)
Async XLA Ops:
  7.2 76.1 %copy-start = (bf16[1,512,512]{2,1,0:T(8,128)(2,1)S(1)}, bf16[1,512,512]{2,1,0:T(8,128)(2,1)}, u32[]{:S(2)}) copy-start(bf16[1,512,512]{2,1,0:T(8,128)(2,1)} %param.15) | copy-start | bytes 1572868
  7.2 4.9 %copy-start.3 = (bf16[32,8,4096]{2,1,0:T(8,128)(2,1)S(1)}, bf16[32,8,4096]{2,1,0:T(8,128)(2,1)}, u32[]{:S(2)}) copy-start(bf16[32,8,4096]{2,1,0:T(8,128)(2,1)} %param.16) | copy-start | bytes 6291460
  7.2 24.4 %all-gather.2.cloned.1.call-start = ((), (), s32[]{:S(2)}) async-start(), calls=%async_computation.1 | async-start | bytes 1310720 | tf_op jit(solution)/shard_map/all_gather | solution.py:62
  10.5 7.1 %copy-start.10 = (s32[32]{0:T(128)S(1)}, s32[32]{0:T(128)}, u32[]{:S(2)}) copy-start(s32[32]{0:T(128)} %param.19) | copy-start | bytes 388
  10.5 7.1 %copy-start.9 = (s32[32,8]{0,1:T(8,128)S(1)}, s32[32,8]{0,1:T(8,128)}, u32[]{:S(2)}) copy-start(s32[32,8]{0,1:T(8,128)} %param.18) | copy-start | bytes 3076
  10.5 7.1 %copy-start.8 = (s32[2048]{0:T(1024)S(1)}, s32[2048]{0:T(1024)}, u32[]{:S(2)}) copy-start(s32[2048]{0:T(1024)} %param.17) | copy-start | bytes 24580
  12.0 248.9 %reduce-scatter.2.cloned.1.call-start = ((), (), s32[]{:S(2)}) async-start(), calls=%async_computation.2 | async-start | bytes 1310720 | tf_op jit(solution)/shard_map/reduce_scatter | solution.py:105
  39.1 8.4 %copy-start.6 = (bf16[64,512]{1,0:T(8,128)(2,1)S(1)}, bf16[64,512]{1,0:T(8,128)(2,1)}, u32[]{:S(2)}) copy-start(bf16[64,512]{1,0:T(8,128)(2,1)} %param.13) | copy-start | bytes 196612
  45.0 26.3 %collective-permute-start = (bf16[2048,64]{1,0:T(8,128)(2,1)S(1)}, bf16[2048,64]{1,0:T(8,128)(2,1)S(1)}, u32[]{:S(2)}, u32[]{:S(2)}) collective-permute-start(bf16[2048,64]{1,0:T(8,128)(2,1)S(1)} %copy.19), channel_id=1, source_target_pairs={{0,16},{4,20},{8,24},{12,28},{16,0},{20,4},{24,8},{28,12},{1,17},{... | collective-permute-start | bytes 786440 | tf_op jit(solution)/shard_map/ppermute | solution.py:10
  77.4 4.5 %copy-start.5 = (bf16[1,512,512]{2,1,0:T(8,128)(2,1)S(1)}, bf16[1,512,512]{2,1,0:T(8,128)(2,1)}, u32[]{:S(2)}) copy-start(bf16[1,512,512]{2,1,0:T(8,128)(2,1)} %param.14) | copy-start | bytes 1572868
  83.2 4.0 %copy-start.2 = (f32[2048,512]{1,0:T(8,128)}, f32[2048,512]{1,0:T(8,128)S(1)}, u32[]{:S(2)}) copy-start(f32[2048,512]{1,0:T(8,128)S(1)} %fusion.4) | copy-start | bytes 12582916
  97.3 93.0 %collective-permute-start.1 = (bf16[2048,512]{1,0:T(8,128)(2,1)}, bf16[2048,512]{1,0:T(8,128)(2,1)S(1)}, u32[]{:S(2)}, u32[]{:S(2)}) collective-permute-start(bf16[2048,512]{1,0:T(8,128)(2,1)} %get-tuple-element.8), channel_id=1, source_target_pairs={{0,16},{4,20},{8,24},{12,28},{16,0},{20,4},{24,8},{28,12},{1,17},{... | collective-permute-start | bytes 6291464 | tf_op jit(solution)/shard_map/ppermute | solution.py:10
  235.5 27.2 %copy-start.4 = (f32[2048,64]{0,1:T(8,128)S(1)}, f32[2048,64]{0,1:T(8,128)}, u32[]{:S(2)}) copy-start(f32[2048,64]{0,1:T(8,128)} %get-tuple-element.5) | copy-start | bytes 1572868
  235.5 27.2 %copy-start.7 = (bf16[512,64]{0,1:T(8,128)(2,1)S(1)}, bf16[512,64]{0,1:T(8,128)(2,1)}, u32[]{:S(2)}) copy-start(bf16[512,64]{0,1:T(8,128)(2,1)} %param.12) | copy-start | bytes 196612
  260.9 6.0 %copy-start.1 = (bf16[1,512,512]{2,1,0:T(8,128)(2,1)S(1)}, bf16[1,512,512]{2,1,0:T(8,128)(2,1)}, u32[]{:S(2)}) copy-start(bf16[1,512,512]{2,1,0:T(8,128)(2,1)} %param.15) | copy-start | bytes 1572868
Sparse Core Ops, SparseCore 0:
  12.1 19.4 all-gather.1
  238.1 22.7 reduce-scatter.1
where the time goes:
time: 274 us
  waiting for transfers between devices  151 us (55%)
  matrix products  53.4 us (19%)
  local copies, waits for them, and re-layouts  48.2 us (18%)
  between operations  14.3 us (5%)
  other arithmetic  4.6 us (2%)
    ppermute x2, waiting for transfers between devices, swapped(): lax.ppermute(array, axis, [(i, i ^ 1 << bit) for i in range(lax.axis_size...  114 us
    reduce_scatter x1, waiting for transfers between devices, on_device(): lax.psum_scatter((upper + jnp.einsum('ksp,ksf->pf', selector, low_terms,...  22.9 us
    dot_general x3, matrix products, dot_trans(): lax.dot_general(operand, matrix, (((1,), (1,)), ((), ())), preferred_elem...  20.3 us
    all_gather x1, waiting for transfers between devices, on_device(): shard_piece = lax.all_gather(trip_blocks, 'narrow', axis=0, tiled=True)  13.8 us
    gather x1, local copies, waits for them, and re-layouts, on_device(): partner_grad = swapped(grad_msg_round, 'cluster', top_bit)[rev_slot]  9.2 us
    dot_general x1, local copies, waits for them, and re-layouts, on_device(): jnp.einsum('ksij,kif->ksjf', angle_mats, grad_blocks, preferred_element_t...  8.98 us
    reshape x1, local copies, waits for them, and re-layouts, on_device(): pair_terms.reshape(local_blocks, slot_count, block_edges * trip_width)  7.91 us
    dot_general x1, matrix products, on_device(): jnp.einsum('ksij,kif->ksjf', angle_mats, grad_blocks, preferred_element_t...  6.66 us
  transfers between devices with their start and end apart: 4, of which 4 were waited for; matrix products, arithmetic and copies ran while one was open for 3% of the time, Pallas kernels for 0%

commit v1 on v0

v1 whole, which is shorter than its diff:
```python
import functools

import jax
import jax.numpy as jnp
from jax import lax
from jax.experimental import pallas as pl
from jax.experimental.pallas import tpu as pltpu
from jax.sharding import PartitionSpec as P

ROOT_HALF = 0.7071067811865476
MIB = 1 << 20
F32 = jnp.float32
BF16 = jnp.bfloat16


def dot(left, right):
    return jnp.dot(left, right, preferred_element_type=F32)


def dot_trans(left, right):
    return lax.dot_general(left, right, (((1,), (1,)), ((), ())), preferred_element_type=F32)


def sigmoid(value):
    return 0.5 * jnp.tanh(0.5 * value) + 0.5


def swapped(array, axis, bit):
    return lax.ppermute(array, axis, [(i, i ^ bit) for i in range(lax.axis_size(axis))])


def half_mask(shape, width):
    return lax.broadcasted_iota(jnp.int32, shape, 1) < width


def split_pairs(rows, block):
    parts = rows.reshape(-1, 2, block, rows.shape[-1])
    return parts[:, 0].reshape(-1, rows.shape[-1]), parts[:, 1].reshape(-1, rows.shape[-1])


def join_pairs(even, odd, block):
    width = even.shape[-1]
    both = jnp.concatenate([even.reshape(-1, 1, block, width), odd.reshape(-1, 1, block, width)], axis=1)
    return both.reshape(-1, width)


def params(limit, **more):
    return pltpu.CompilerParams(vmem_limit_bytes=limit, **more)


def down_kernel(block, x_ref, wl_ref, wr_ref, pre_ref, trip_ref):
    even, odd = split_pairs(x_ref[...], block)
    pre = dot(even, wl_ref[...]) + dot(odd, wr_ref[...])
    pre_ref[...] = pre
    trip_ref[...] = (pre * sigmoid(pre)).astype(BF16)


def down(x, wl, wr, block, steps):
    rows, width = x.shape
    lanes = wl.shape[1]
    return pl.pallas_call(
        functools.partial(down_kernel, block),
        grid=(steps,),
        in_specs=[
            pl.BlockSpec((rows // steps, width), lambda i: (i, 0)),
            pl.BlockSpec((width, lanes), lambda i: (0, 0)),
            pl.BlockSpec((width, lanes), lambda i: (0, 0)),
        ],
        out_specs=[pl.BlockSpec((rows // 2 // steps, lanes), lambda i: (i, 0))] * 2,
        out_shape=[
            jax.ShapeDtypeStruct((rows // 2, lanes), F32),
            jax.ShapeDtypeStruct((rows // 2, lanes), BF16),
        ],
        compiler_params=params(32 * MIB),
        name="down",
    )(x, wl, wr)


def triplet_kernel(block, slots, pieces, *refs):
    index_ref, code_ref, angle_ref = refs[:3]
    piece_refs = refs[3 : 3 + pieces]
    trip_ref, sent_ref, left_ref, right_ref, dup_ref = refs[3 + pieces :]
    packed_rows, lanes = trip_ref.shape
    half = lanes // 2
    groups = packed_rows // block
    zero = jnp.zeros((block, lanes), BF16)
    left_ref[pieces * groups * 2] = zero
    right_ref[pieces * groups * 2] = zero
    mask = half_mask((block, lanes), half)

    for piece in range(pieces):

        def spread(m, carry, piece=piece):
            rows = piece_refs[piece][pl.ds(pl.multiple_of(m * block, block), block), :].astype(F32)
            other = pltpu.roll(rows, half, 1)
            at = (piece * groups + m) * 2
            left_ref[at] = jnp.where(mask, rows, 0.0).astype(BF16)
            left_ref[at + 1] = jnp.where(mask, other, 0.0).astype(BF16)
            right_ref[at] = jnp.where(mask, 0.0, other).astype(BF16)
            right_ref[at + 1] = jnp.where(mask, 0.0, rows).astype(BF16)
            return carry

        lax.fori_loop(0, groups, spread, 0, unroll=4)

    def target(m, carry):
        base = m * (2 * slots)
        picked = [left_ref[index_ref[base + s]] for s in range(slots)]
        picked += [right_ref[index_ref[base + slots + s]] for s in range(slots)]
        total = dot(angle_ref[m], jnp.concatenate(picked, axis=0))
        at = pl.ds(pl.multiple_of(m * block, block), block)
        trip_ref[at, :] = total.astype(BF16)
        rounded = total.astype(BF16).astype(F32)
        other = pltpu.roll(rounded, half, 1)
        dup_ref[0, at, :] = jnp.where(mask, rounded, other).astype(BF16)
        dup_ref[1, at, :] = jnp.where(mask, other, rounded).astype(BF16)
        return carry

    lax.fori_loop(0, groups, target, 0, unroll=2)

    every = dup_ref[...].reshape(2 * packed_rows, lanes)
    code = code_ref[...]
    tile = 2 * block
    tile_mask = half_mask((tile, lanes), half)

    def send(t, carry):
        def part(base):
            spot = lax.broadcasted_iota(jnp.int32, (tile, 2 * packed_rows), 0) + (base + t * tile)
            return dot((spot == code).astype(F32).astype(BF16), every)

        both = jnp.where(tile_mask, part(0), part(packed_rows))
        sent_ref[pl.ds(pl.multiple_of(t * tile, tile), tile), :] = both.astype(BF16)
        return carry

    lax.fori_loop(0, packed_rows // tile, send, 0, unroll=2)


def triplet(index, code, angles, pieces, block, slots):
    packed_rows, lanes = pieces[0].shape
    blocks = packed_rows // block * 2 * len(pieces)
    vmem = pl.BlockSpec(memory_space=pltpu.VMEM)
    return pl.pallas_call(
        functools.partial(triplet_kernel, block, slots, len(pieces)),
        in_specs=[pl.BlockSpec(memory_space=pltpu.SMEM)] + [vmem] * (2 + len(pieces)),
        out_specs=[vmem] * 2,
        out_shape=[jax.ShapeDtypeStruct((packed_rows, lanes), BF16)] * 2,
        scratch_shapes=[
            pltpu.VMEM((blocks + 1, block, lanes), BF16),
            pltpu.VMEM((blocks + 1, block, lanes), BF16),
            pltpu.VMEM((2, packed_rows, lanes), BF16),
        ],
        compiler_params=params(48 * MIB),
        name="triplet",
    )(index, code, angles, *pieces)


def layer_kernel(
    block, x_ref, ct_ref, own_ref, far_ref, up2_ref, upl_ref, upr_ref, wi_ref, wo_ref, *refs
):
    out_ref, grad_ref, near_ref, send_ref = refs[-4:]
    lanes = own_ref.shape[1]
    up2 = up2_ref[...]
    mask = half_mask(own_ref.shape, lanes // 2)
    none = jnp.zeros(own_ref.shape, BF16)

    def pre_up(ref):
        rows = ref[...]
        return dot(join_pairs(jnp.where(mask, rows, none), jnp.where(mask, none, rows), block), up2)

    def gated(pre):
        squash = sigmoid(pre)
        value = pre * squash
        return value, squash + value * (1.0 - squash)

    own_value, own_slope = gated(pre_up(own_ref))
    far_value, far_slope = gated(pre_up(far_ref))
    message = (own_value.astype(BF16).astype(F32) + far_value.astype(BF16).astype(F32)) * ROOT_HALF
    hidden = (x_ref[...].astype(F32) + message) * ROOT_HALF
    wi, wo = wi_ref[...], wo_ref[...]
    in_value, in_slope = gated(dot(hidden.astype(BF16), wi))
    out_value, out_slope = gated(dot(in_value.astype(BF16), wo))
    out_ref[...] = ((hidden + out_value) * ROOT_HALF).astype(BF16)
    scaled = ct_ref[...].astype(F32) * ROOT_HALF
    grad_out = (scaled * out_slope).astype(BF16)
    grad_in = (dot_trans(grad_out, wo) * in_slope).astype(BF16)
    grad_msg = (scaled + dot_trans(grad_in, wi)) * ROOT_HALF
    grad_round = grad_msg.astype(BF16)
    grad_ref[...] = grad_round

    def project(rows):
        even, odd = split_pairs(rows.astype(BF16), block)
        return (dot_trans(even, upl_ref[...]) + dot_trans(odd, upr_ref[...])) * ROOT_HALF

    near_ref[...] = project(grad_msg * own_slope)
    send_ref[...] = project(grad_round.astype(F32) * far_slope).astype(BF16)


def layer(x, ct, own, far, up2, upl, upr, wi, wo, block, steps):
    rows, width = x.shape
    lanes = own.shape[1]
    whole = lambda array: pl.BlockSpec(array.shape, lambda i: (0, 0))
    wide = pl.BlockSpec((rows // steps, width), lambda i: (i, 0))
    thin = pl.BlockSpec((rows // 2 // steps, lanes), lambda i: (i, 0))
    return pl.pallas_call(
        functools.partial(layer_kernel, block),
        grid=(steps,),
        in_specs=[wide, wide, thin, thin] + [whole(w) for w in (up2, upl, upr, wi, wo)],
        out_specs=[wide, wide, thin, thin],
        out_shape=[
            jax.ShapeDtypeStruct((rows, width), BF16),
            jax.ShapeDtypeStruct((rows, width), BF16),
            jax.ShapeDtypeStruct((rows // 2, lanes), F32),
            jax.ShapeDtypeStruct((rows // 2, lanes), BF16),
        ],
        compiler_params=params(48 * MIB),
        name="layer",
    )(x, ct, own, far, up2, upl, upr, wi, wo)


def scatter_kernel(block, slots, pieces, index_ref, row_ref, angle_ref, near_ref, far_ref, *refs):
    out_refs = refs[:pieces]
    total_ref, grad_ref = refs[pieces:]
    packed_rows, lanes = near_ref.shape
    half = lanes // 2
    groups = packed_rows // block
    mask = half_mask((block, lanes), half)
    total_ref[...] = jnp.zeros(total_ref.shape, F32)
    far = far_ref[...]
    tile = 2 * block
    tile_mask = half_mask((tile, lanes), half)

    def collect(m, carry):
        rows = row_ref[pl.ds(pl.multiple_of(m * tile, tile), tile), :]
        spot = lax.broadcasted_iota(jnp.int32, (tile, packed_rows), 1)
        got = dot((spot == (rows & (packed_rows - 1))).astype(F32).astype(BF16), far)
        got = jnp.where(tile_mask == (rows < packed_rows), got, 0.0)
        got = got + pltpu.roll(got, half, 1)
        both = jnp.where(mask, got[:block], got[block:])
        at = pl.ds(pl.multiple_of(m * block, block), block)
        grad_ref[at, :] = (near_ref[at, :] + both).astype(BF16)
        return carry

    lax.fori_loop(0, groups, collect, 0, unroll=2)
    none = jnp.zeros((block, lanes), BF16)

    def target(m, carry):
        rows = grad_ref[pl.ds(pl.multiple_of(m * block, block), block), :]
        pair = jnp.concatenate([jnp.where(mask, rows, none), jnp.where(mask, none, rows)], axis=0)
        terms = dot(angle_ref[m], pair)
        base = m * (2 * slots)
        for s in range(slots):
            term = terms[s * block : (s + 1) * block]
            total_ref[index_ref[base + s]] += jnp.where(mask, term, 0.0)
            total_ref[index_ref[base + slots + s]] += jnp.where(mask, 0.0, term)
        return carry

    lax.fori_loop(0, groups, target, 0)

    for piece in range(pieces):

        def finish(m, carry, piece=piece):
            at = piece * groups + m
            total = total_ref[at] + pltpu.roll(total_ref[pieces * groups + at], half, 1)
            rows = pl.ds(pl.multiple_of(m * block, block), block)
            out_refs[piece][rows, :] = total.astype(out_refs[piece].dtype)
            return carry

        lax.fori_loop(0, groups, finish, 0, unroll=2)


def scatter(index, row, angles, near, far, types, block, slots):
    packed_rows, lanes = near.shape
    pieces = len(types)
    groups = packed_rows // block
    vmem = pl.BlockSpec(memory_space=pltpu.VMEM)
    return pl.pallas_call(
        functools.partial(scatter_kernel, block, slots, pieces),
        in_specs=[pl.BlockSpec(memory_space=pltpu.SMEM)] + [vmem] * 4,
        out_specs=[vmem] * pieces,
        out_shape=[jax.ShapeDtypeStruct((packed_rows, lanes), kind) for kind in types],
        scratch_shapes=[
            pltpu.VMEM((2 * pieces * groups + 1, block, lanes), F32),
            pltpu.VMEM((packed_rows, lanes), BF16),
        ],
        compiler_params=params(56 * MIB),
        name="scatter",
    )(index, row, angles, near, far)


def last_kernel(block, pre_ref, grad_ref, wl_ref, wr_ref, *refs):
    out_ref = refs[-1]
    total = refs[0][...].astype(F32)
    for ref in refs[1:-1]:
        total = total + ref[...].astype(F32)
    pre = pre_ref[...]
    squash = sigmoid(pre)
    grad = (total * (squash + pre * squash * (1.0 - squash))).astype(BF16)
    both = join_pairs(dot_trans(grad, wl_ref[...]), dot_trans(grad, wr_ref[...]), block)
    out_ref[...] = (grad_ref[...].astype(F32) + both).astype(BF16)


def last(pre, grad_msg, wl, wr, terms, block, steps):
    rows, width = grad_msg.shape
    lanes = wl.shape[1]
    wide = pl.BlockSpec((rows // steps, width), lambda i: (i, 0))
    thin = pl.BlockSpec((rows // 2 // steps, lanes), lambda i: (i, 0))
    weight = pl.BlockSpec((width, lanes), lambda i: (0, 0))
    return pl.pallas_call(
        functools.partial(last_kernel, block),
        grid=(steps,),
        in_specs=[thin, wide, weight, weight] + [thin] * len(terms),
        out_specs=wide,
        out_shape=jax.ShapeDtypeStruct((rows, width), BF16),
        compiler_params=params(32 * MIB),
        name="last",
    )(pre, grad_msg, wl, wr, *terms)


def on_device(
    edge_feats,
    cotangent,
    down_weight,
    up_weight,
    inner_weight,
    outer_weight,
    angular,
    reverse,
    sources,
    counts,
):
    lane_count = lax.axis_size("narrow")
    top_bit = lax.axis_size("cluster") // 2
    me = lax.axis_index("narrow")
    local_blocks, slots = sources.shape
    local_edges = edge_feats.shape[0]
    block = local_edges // local_blocks
    groups = local_blocks // 2
    packed_rows = local_edges // 2
    width = down_weight.shape[1]

    none = jnp.zeros_like(down_weight)
    wl = jnp.concatenate([down_weight, none], axis=1)
    wr = jnp.concatenate([none, down_weight], axis=1)
    up_none = jnp.zeros_like(up_weight)
    up2 = jnp.concatenate([up_weight, up_weight], axis=0)
    upl = jnp.concatenate([up_weight, up_none], axis=0).T
    upr = jnp.concatenate([up_none, up_weight], axis=0).T
    upl, upr = upl.T, upr.T

    live = lax.broadcasted_iota(jnp.int32, sources.shape, 1) < counts[:, None]
    local = sources % (local_blocks * lane_count)
    spot = (local // local_blocks ^ me) * local_blocks + local % local_blocks
    forward_index = jnp.where(live, spot, lane_count * local_blocks).reshape(-1)
    odd = lax.broadcasted_iota(jnp.int32, sources.shape, 0) % 2
    turned = jnp.where(spot % 2 == odd, 0, lane_count * groups)
    backward_index = jnp.where(live, turned + spot // 2, 2 * lane_count * groups).reshape(-1)

    slot = reverse % local_edges
    place = (slot // block % 2) * packed_rows + slot // (2 * block) * block + slot % block
    code = place.reshape(groups, 2, block).transpose(1, 0, 2).reshape(1, local_edges)

    angles = angular.reshape(groups, 2, slots, block, block)
    angle_in = angles.transpose(0, 3, 1, 2, 4).reshape(groups, block, 2 * slots * block)
    angle_out = angles.transpose(0, 2, 4, 1, 3).reshape(groups, slots * block, 2 * block)

    pre_down, trip = down(edge_feats, wl, wr, block, 4)
    pieces = {0: trip}
    bits = [1 << i for i in range(lane_count.bit_length() - 1)]
    for bit in reversed(bits):
        pieces.update({d ^ bit: swapped(piece, "narrow", bit) for d, piece in pieces.items()})
    trip_own, trip_sent = triplet(
        forward_index, code, angle_in, [pieces[d] for d in range(lane_count)], block, slots
    )
    trip_far = swapped(trip_sent, "cluster", top_bit)
    output, grad_msg, near, sent = layer(
        edge_feats,
        cotangent,
        trip_own,
        trip_far,
        up2,
        upl,
        upr,
        inner_weight[0],
        outer_weight[0],
        block,
        8,
    )
    far = swapped(sent, "cluster", top_bit)
    types = [BF16 if d % 2 else F32 for d in range(lane_count)]
    parts = scatter(backward_index, place.reshape(local_edges, 1), angle_out, near, far, types, block, slots)
    parts = dict(enumerate(parts))
    terms = [parts[0]]
    for bit in bits:
        for d in range(lane_count - bit, -1, -2 * bit):
            got = swapped(parts[d].astype(BF16), "narrow", bit)
            if d == bit:
                terms.append(got)
            else:
                parts[d ^ bit] = parts[d ^ bit] + got.astype(F32)
    grad_x = last(pre_down, grad_msg, wl, wr, terms, block, 4)
    return (output, grad_x)


def solution(mesh):
    in_specs = (
        P(("cluster", "narrow"), None),
        P(("cluster", "narrow"), None),
        P(),
        P(),
        P(),
        P(),
        P(("cluster", "narrow"), None, None),
        P(("cluster", "narrow")),
        P(("cluster", "narrow"), None),
        P(("cluster", "narrow")),
    )
    out_specs = (P(("cluster", "narrow"), None), P(("cluster", "narrow"), None))
    return jax.shard_map(
        on_device, mesh=mesh, in_specs=in_specs, out_specs=out_specs, check_vma=False
    )
```

time: 274 us -> 129 us (0.47)
  waiting for transfers between devices: 151 us -> 27.1 us
  matrix products: 53.4 us -> 0 us
  Pallas kernels: 0 us -> 43.2 us
  between operations: 14.3 us -> 0.79 us
  starting transfers between devices: 2.55 us -> 8.01 us
  other arithmetic: 4.6 us -> 1.19 us
    ppermute x2 -> x8, waiting for transfers between devices: 114 us -> 27.1 us  [swapped(): lax.ppermute(array, axis, [(i, i ^ bit) for i in range(lax.axis_size(axis...]
    dot_general x13 -> x0, matrix products: 53.4 us -> none  [the longest x3 20.3 us: dot_trans(): lax.dot_general(operand, matrix, (((1,), (1,)), ((), ())), preferred_elem...]
    pallas_call x0 -> x5, Pallas kernels: none -> 43.2 us  [the longest x1 16.3 us: layer(): pl.pallas_call(functools.partial(layer_kernel, block), grid=(steps,), in_...]
    reduce_scatter x1 -> x0, waiting for transfers between devices: 22.9 us -> none  [on_device(): lax.psum_scatter((upper + jnp.einsum('ksp,ksf->pf', selector, low_terms,...]
    reshape x7 -> x10, local copies, waits for them, and re-layouts: 22.4 us -> 40 us  [the longest x3 24.4 us: on_device(): angles = angular.reshape(groups, 2, slots, block, block)]
    gather x2 -> x0, local copies, waits for them, and re-layouts: 15.4 us -> none  [the longest x1 9.2 us: on_device(): partner_grad = swapped(grad_msg_round, 'cluster', top_bit)[rev_slot]]
    all_gather x1 -> x0, waiting for transfers between devices: 13.8 us -> none  [on_device(): shard_piece = lax.all_gather(trip_blocks, 'narrow', axis=0, tiled=True)]
    dot_general x1 -> x0, local copies, waits for them, and re-layouts: 8.98 us -> none  [on_device(): jnp.einsum('ksij,kif->ksjf', angle_mats, grad_blocks, preferred_element_t...]
  transfers between devices with their start and end apart: 4 -> 8, of which waited for: 4 -> 4; matrix products, arithmetic and copies ran while one was open for 3% -> 33% of each run, Pallas kernels for 0% -> 0%
where the time goes in v1:
time: 129 us; the launch traced here: 127 us
  local copies, waits for them, and re-layouts  46.2 us (36%)
  Pallas kernels  43.2 us (33%)
  waiting for transfers between devices  27.1 us (21%)
  starting transfers between devices  8.01 us (6%)
    ppermute x8, waiting for transfers between devices, swapped(): lax.ppermute(array, axis, [(i, i ^ bit) for i in range(lax.axis_size(axis...  27.1 us
    reshape x3, local copies, waits for them, and re-layouts, on_device(): angles = angular.reshape(groups, 2, slots, block, block)  24.4 us
    pallas_call x1, Pallas kernels, layer(): pl.pallas_call(functools.partial(layer_kernel, block), grid=(steps,), in_...  16.3 us
    pallas_call x1, Pallas kernels, scatter(): pl.pallas_call(functools.partial(scatter_kernel, block, slots, pieces), i...  14.2 us
    pallas_call x1, Pallas kernels, triplet(): pl.pallas_call(functools.partial(triplet_kernel, block, slots, len(pieces...  8.01 us
    ppermute x8, starting transfers between devices, swapped(): lax.ppermute(array, axis, [(i, i ^ bit) for i in range(lax.axis_size(axis...  8.01 us
    reshape x1, local copies, waits for them, and re-layouts, on_device(): angles.transpose(0, 2, 4, 1, 3).reshape(groups, slots * block, 2 * block)  7.78 us
    unnamed x27, local copies, waits for them, and re-layouts  5.99 us
  transfers between devices with their start and end apart: 8, of which 4 were waited for; matrix products, arithmetic and copies ran while one was open for 33% of the time, Pallas kernels for 0%

profile of v1, /device:TPU:0, one launch (start us, length us, event | category | flops | bytes accessed | tf_op | source)
XLA Modules:
  0.0 126.6 jit_solution(8226191032602184746)
XLA Ops:
  0.6 0.0 copy-start.11
  0.6 0.0 copy-start.12
  0.7 1.0 copy.19
  1.6 0.1 fusion.26
  1.7 0.0 copy-start
  1.7 1.6 %copy-done = bf16[2048,512]{1,0:T(8,128)(2,1)S(1)} copy-done((bf16[2048,512]{1,0:T(8,128)(2,1)S(1)}, bf16[2048,512]{1,0:T(8,128)(2,1)}, u32[]{:S(2)}) %copy-start) | copy-done | bytes 2097176
  3.3 2.2 %down.1 = (f32[1024,128]{1,0:T(8,128)S(1)}, bf16[1024,128]{1,0:T(8,128)(2,1)}) custom-call(bf16[2048,512]{1,0:T(8,128)(2,1)S(1)} %copy-done, bf16[512,128]{1,0:T(8,128)(2,1)S(1)} %get-tuple-element.29.wl_ref, bf16[512,128]{1,0:T(8,128)(2,1)S(1)} %get-tuple-element.28.wr_ref), custom_call_target="tpu_custom_call" | custom-call | tf_op jit(solution)/shard_map/down/pallas_call | solution.py:61
  5.5 0.9 copy-done.3
  6.4 3.0 %collective-permute-start.1 = (bf16[1024,128]{1,0:T(8,128)(2,1)}, bf16[1024,128]{1,0:T(8,128)(2,1)}, u32[]{:S(2)}, u32[]{:S(2)}) collective-permute-start(bf16[1024,128]{1,0:T(8,128)(2,1)} %get-tuple-element.14.refs_3_), channel_id=1, source_target_pairs={{0,2},{1,3},{2,0},{3,1},{4,6},{5,7},{6,4},{7,5},{8,10},{9,11},{10,... | collective-permute-start | bytes 786440 | tf_op jit(solution)/shard_map/ppermute | solution.py:29
  9.3 0.0 collective-permute-start
  9.3 0.0 copy-done.11
  9.4 6.6 %collective-permute-done.1.refs_5_ = bf16[1024,128]{1,0:T(8,128)(2,1)} collective-permute-done((bf16[1024,128]{1,0:T(8,128)(2,1)}, bf16[1024,128]{1,0:T(8,128)(2,1)}, u32[]{:S(2)}, u32[]{:S(2)}) %collective-permute-start.1) | collective-permute-done | bytes 262176 | tf_op jit(solution)/shard_map/ppermute | solution.py:29
  15.9 0.0 collective-permute-start.2
  16.0 0.1 copy.16
  16.0 0.1 reshape.29.refs_0_
  16.1 5.5 %reshape.32 = bf16[16,2,8,64,64]{4,3,2,1,0:T(8,128)(2,1)} reshape(bf16[32,8,4096]{2,1,0:T(8,128)(2,1)S(1)} %copy-done.7) | data formatting | bytes 4194304 | tf_op jit(solution)/shard_map/reshape | solution.py:361
  21.6 7.7 %copy.25 = bf16[16,2,8,64,64]{4,2,1,3,0:T(8,128)(2,1)} copy(bf16[16,2,8,64,64]{4,3,2,1,0:T(8,128)(2,1)} %reshape.32) | data formatting | bytes 4194304 | tf_op jit(solution)/shard_map/reshape | solution.py:361
  29.4 5.5 %reshape.33.refs_2_ = bf16[16,64,1024]{2,1,0:T(8,128)(2,1)S(1)} reshape(bf16[16,64,2,8,64]{4,3,2,1,0:T(8,128)(2,1)} %bitcast.13) | data formatting | bytes 4194304 | tf_op jit(solution)/shard_map/reshape | solution.py:362
  34.9 0.0 copy-start.9
  34.9 0.0 copy-start.1
  34.9 0.0 copy-start.2
  35.0 0.1 reshape.30
  35.0 0.1 reshape.31.refs_1_
  35.1 0.0 collective-permute-done.refs_4_
  35.1 0.0 collective-permute-done.2.refs_6_
  35.1 8.0 %triplet.1 = (bf16[1024,128]{1,0:T(8,128)(2,1)S(1)}, bf16[1024,128]{1,0:T(8,128)(2,1)S(1)}) custom-call(s32[256]{0:T(256)S(1)} %reshape.29.refs_0_, s32[1,2048]{1,0:T(1,128)S(1)} %reshape.31.refs_1_, bf16[16,64,1024]{2,1,0:T(8,128)(2,1)S(1)} %reshape.33.refs_2_, bf16[1024,128]{1,0:T(8,128)(2,1)} %get-tuple-element.14.refs_3_, ...), custom_call_target="tpu_custom_call" | custom-call | tf_op jit(solution)/shard_map/triplet/pallas_call | solution.py:141
  43.2 2.9 %collective-permute-start.3 = (bf16[1024,128]{1,0:T(8,128)(2,1)S(1)}, bf16[1024,128]{1,0:T(8,128)(2,1)S(1)}, u32[]{:S(2)}, u32[]{:S(2)}) collective-permute-start(bf16[1024,128]{1,0:T(8,128)(2,1)S(1)} %get-tuple-element.16), channel_id=1, source_target_pairs={{0,16},{4,20},{8,24},{12,28},{16,0},{20,4},{24,8},{28,12},{1,17},{... | collective-permute-start | bytes 786440 | tf_op jit(solution)/shard_map/ppermute | solution.py:29
  46.1 12.6 %collective-permute-done.3.far_ref = bf16[1024,128]{1,0:T(8,128)(2,1)S(1)} collective-permute-done((bf16[1024,128]{1,0:T(8,128)(2,1)S(1)}, bf16[1024,128]{1,0:T(8,128)(2,1)S(1)}, u32[]{:S(2)}, u32[]{:S(2)}) %collective-permute-start.3) | collective-permute-done | bytes 262176 | tf_op jit(solution)/shard_map/ppermute | solution.py:29
  58.6 16.3 %layer.1 = (bf16[2048,512]{1,0:T(8,128)(2,1)}, bf16[2048,512]{1,0:T(8,128)(2,1)S(1)}, f32[1024,128]{1,0:T(8,128)S(1)}, bf16[1024,128]{1,0:T(8,128)(2,1)}) custom-call(bf16[2048,512]{1,0:T(8,128)(2,1)} %x_ref.3, bf16[2048,512]{1,0:T(8,128)(2,1)} %ct_ref.1, bf16[1024,128]{1,0:T(8,128)(2,1)S(1)} %get-tuple-element.15.own_ref, ...), custom_call_target="tpu_custom_call" | custom-call | tf_op jit(solution)/shard_map/layer/pallas_call | solution.py:203
  75.0 0.8 copy-done.6
  75.8 0.0 collective-permute-start.4
  75.8 11.2 %copy.22 = bf16[16,2,8,64,64]{3,1,4,2,0:T(2,128)(2,1)} copy(bf16[16,2,8,64,64]{4,3,2,1,0:T(8,128)(2,1)} %reshape.32) | data formatting | bytes 4194304 | tf_op jit(solution)/shard_map/reshape | solution.py:361
  87.0 0.1 copy.21
  87.0 0.6 reshape.34.index_ref
  87.7 7.8 %reshape.36.angle_ref = bf16[16,512,128]{2,1,0:T(8,128)(2,1)} reshape(bf16[16,8,64,2,64]{4,3,2,1,0:T(2,128)(2,1)} %bitcast.12) | data formatting | bytes 4194304 | tf_op jit(solution)/shard_map/reshape | solution.py:363
  95.4 1.4 %copy.23.row_ref = s32[2048,1]{1,0:T(8,128)} copy(s32[2048,1]{0,1:T(1,128)S(1)} %bitcast.14) | data formatting | bytes 16384 | tf_op jit(solution)/shard_map/reshape | solution.py:389
  96.8 0.0 collective-permute-done.4.far_ref
  96.8 0.7 copy-done.8
  97.5 14.2 %scatter.1 = (f32[1024,128]{1,0:T(8,128)}, bf16[1024,128]{1,0:T(8,128)(2,1)}, f32[1024,128]{1,0:T(8,128)}, bf16[1024,128]{1,0:T(8,128)(2,1)}) custom-call(s32[256]{0:T(256)} %reshape.34.index_ref, s32[2048,1]{1,0:T(8,128)} %copy.23.row_ref, bf16[16,512,128]{2,1,0:T(8,128)(2,1)} %reshape.36.angle_ref, f32[1024,128]{1,0:T(8,128)} %copy-done.6, ...), custom_call_target="tpu_custom_call" | custom-call | tf_op jit(solution)/shard_map/scatter/pallas_call | solution.py:275
  111.7 0.0 collective-permute-start.6
  111.8 0.5 collective-permute-start.5
  112.3 1.2 collective-permute-done.6
  113.5 1.1 add_convert_fusion
  114.6 1.6 %collective-permute-start.7 = (bf16[1024,128]{1,0:T(8,128)(2,1)S(1)}, bf16[1024,128]{1,0:T(8,128)(2,1)S(1)}, u32[]{:S(2)}, u32[]{:S(2)}) collective-permute-start(bf16[1024,128]{1,0:T(8,128)(2,1)S(1)} %add_convert_fusion), channel_id=1, source_target_pairs={{0,2},{1,3},{2,0},{3,1},{4,6},{5,7},{6,4},{7,5},{8,10},{9,11},{10,... | collective-permute-start | bytes 786440 | tf_op jit(solution)/shard_map/ppermute | solution.py:29
  116.2 0.0 collective-permute-done.5.refs_1_
  116.2 6.8 %collective-permute-done.7.refs_2_ = bf16[1024,128]{1,0:T(8,128)(2,1)S(1)} collective-permute-done((bf16[1024,128]{1,0:T(8,128)(2,1)S(1)}, bf16[1024,128]{1,0:T(8,128)(2,1)S(1)}, u32[]{:S(2)}, u32[]{:S(2)}) %collective-permute-start.7) | collective-permute-done | bytes 262176 | tf_op jit(solution)/shard_map/ppermute | solution.py:29
  123.0 1.0 copy-done.5
  124.1 2.5 %last.1 = bf16[2048,512]{1,0:T(8,128)(2,1)} custom-call(f32[1024,128]{1,0:T(8,128)S(1)} %copy-done.4, bf16[2048,512]{1,0:T(8,128)(2,1)S(1)} %get-tuple-element.19.grad_ref, bf16[512,128]{1,0:T(8,128)(2,1)S(1)} %get-tuple-element.29.wl_ref, bf16[512,128]{1,0:T(8,128)(2,1)S(1)} %get-tuple-element.28.wr_ref, f32[1024,128]{1,0:T(8,128)S(1)} %copy-done.5, ...), custom_call_target="tpu_custom_call" | custom-call | tf_op jit(solution)/shard_map/last/pallas_call | solution.py:307
  (21 shorter events, 0.1 us)
Async XLA Ops:
  0.6 8.7 %copy-start.11 = (s32[32,8]{0,1:T(8,128)S(1)}, s32[32,8]{0,1:T(8,128)}, u32[]{:S(2)}) copy-start(s32[32,8]{0,1:T(8,128)} %param.18) | copy-start | bytes 3076
  0.6 8.7 %copy-start.12 = (s32[32]{0:T(128)S(1)}, s32[32]{0:T(128)}, u32[]{:S(2)}) copy-start(s32[32]{0:T(128)} %param.19) | copy-start | bytes 388
  1.7 1.6 %copy-start = (bf16[2048,512]{1,0:T(8,128)(2,1)S(1)}, bf16[2048,512]{1,0:T(8,128)(2,1)}, u32[]{:S(2)}) copy-start(bf16[2048,512]{1,0:T(8,128)(2,1)} %x_ref.3) | copy-start | bytes 6291460
  3.3 12.8 %copy-start.7 = (bf16[32,8,4096]{2,1,0:T(8,128)(2,1)S(1)}, bf16[32,8,4096]{2,1,0:T(8,128)(2,1)}, u32[]{:S(2)}) copy-start(bf16[32,8,4096]{2,1,0:T(8,128)(2,1)} %param.16) | copy-start | bytes 6291460
  5.5 0.9 copy-start.3
  6.4 9.6 %collective-permute-start.1 = (bf16[1024,128]{1,0:T(8,128)(2,1)}, bf16[1024,128]{1,0:T(8,128)(2,1)}, u32[]{:S(2)}, u32[]{:S(2)}) collective-permute-start(bf16[1024,128]{1,0:T(8,128)(2,1)} %get-tuple-element.14.refs_3_), channel_id=1, source_target_pairs={{0,2},{1,3},{2,0},{3,1},{4,6},{5,7},{6,4},{7,5},{8,10},{9,11},{10,... | collective-permute-start | bytes 786440 | tf_op jit(solution)/shard_map/ppermute | solution.py:29
  9.3 25.8 %collective-permute-start = (bf16[1024,128]{1,0:T(8,128)(2,1)}, bf16[1024,128]{1,0:T(8,128)(2,1)}, u32[]{:S(2)}, u32[]{:S(2)}) collective-permute-start(bf16[1024,128]{1,0:T(8,128)(2,1)} %get-tuple-element.14.refs_3_), channel_id=1, source_target_pairs={{0,1},{1,0},{2,3},{3,2},{4,5},{5,4},{6,7},{7,6},{8,9},{9,8},{10,11... | collective-permute-start | bytes 786440 | tf_op jit(solution)/shard_map/ppermute | solution.py:29
  15.9 19.2 %collective-permute-start.2 = (bf16[1024,128]{1,0:T(8,128)(2,1)}, bf16[1024,128]{1,0:T(8,128)(2,1)}, u32[]{:S(2)}, u32[]{:S(2)}) collective-permute-start(bf16[1024,128]{1,0:T(8,128)(2,1)} %collective-permute-done.1.refs_5_), channel_id=1, source_target_pairs={{0,1},{1,0},{2,3},{3,2},{4,5},{5,4},{6,7},{7,6},{8,9},{9,8},{10,11... | collective-permute-start | bytes 786440 | tf_op jit(solution)/shard_map/ppermute | solution.py:29
  29.4 5.5 %copy-start.10 = (s32[2048]{0:T(1024)S(1)}, s32[2048]{0:T(1024)}, u32[]{:S(2)}) copy-start(s32[2048]{0:T(1024)} %param.17) | copy-start | bytes 24580
  34.9 11.1 %copy-start.9 = (bf16[64,512]{1,0:T(8,128)(2,1)S(1)}, bf16[64,512]{1,0:T(8,128)(2,1)}, u32[]{:S(2)}) copy-start(bf16[64,512]{1,0:T(8,128)(2,1)} %param.13) | copy-start | bytes 196612
  34.9 23.7 %copy-start.1 = (bf16[1,512,512]{2,1,0:T(8,128)(2,1)S(1)}, bf16[1,512,512]{2,1,0:T(8,128)(2,1)}, u32[]{:S(2)}) copy-start(bf16[1,512,512]{2,1,0:T(8,128)(2,1)} %param.14) | copy-start | bytes 1572868
  34.9 23.7 %copy-start.2 = (bf16[1,512,512]{2,1,0:T(8,128)(2,1)S(1)}, bf16[1,512,512]{2,1,0:T(8,128)(2,1)}, u32[]{:S(2)}) copy-start(bf16[1,512,512]{2,1,0:T(8,128)(2,1)} %param.15) | copy-start | bytes 1572868
  43.2 15.5 %collective-permute-start.3 = (bf16[1024,128]{1,0:T(8,128)(2,1)S(1)}, bf16[1024,128]{1,0:T(8,128)(2,1)S(1)}, u32[]{:S(2)}, u32[]{:S(2)}) collective-permute-start(bf16[1024,128]{1,0:T(8,128)(2,1)S(1)} %get-tuple-element.16), channel_id=1, source_target_pairs={{0,16},{4,20},{8,24},{12,28},{16,0},{20,4},{24,8},{28,12},{1,17},{... | collective-permute-start | bytes 786440 | tf_op jit(solution)/shard_map/ppermute | solution.py:29
  75.0 0.8 copy-start.6
  75.8 21.1 %collective-permute-start.4 = (bf16[1024,128]{1,0:T(8,128)(2,1)}, bf16[1024,128]{1,0:T(8,128)(2,1)S(1)}, u32[]{:S(2)}, u32[]{:S(2)}) collective-permute-start(bf16[1024,128]{1,0:T(8,128)(2,1)} %get-tuple-element.21), channel_id=1, source_target_pairs={{0,16},{4,20},{8,24},{12,28},{16,0},{20,4},{24,8},{28,12},{1,17},{... | collective-permute-start | bytes 786440 | tf_op jit(solution)/shard_map/ppermute | solution.py:29
  96.8 0.7 copy-start.8
  97.5 25.5 %copy-start.4 = (f32[1024,128]{1,0:T(8,128)S(1)}, f32[1024,128]{1,0:T(8,128)}, u32[]{:S(2)}) copy-start(f32[1024,128]{1,0:T(8,128)} %copy-done.3) | copy-start | bytes 1572868
  111.7 1.7 %collective-permute-start.6 = (bf16[1024,128]{1,0:T(8,128)(2,1)}, bf16[1024,128]{1,0:T(8,128)(2,1)S(1)}, u32[]{:S(2)}, u32[]{:S(2)}) collective-permute-start(bf16[1024,128]{1,0:T(8,128)(2,1)} %get-tuple-element.25), channel_id=1, source_target_pairs={{0,1},{1,0},{2,3},{3,2},{4,5},{5,4},{6,7},{7,6},{8,9},{9,8},{10,11... | collective-permute-start | bytes 786440 | tf_op jit(solution)/shard_map/ppermute | solution.py:29
  111.8 4.5 %collective-permute-start.5 = (bf16[1024,128]{1,0:T(8,128)(2,1)}, bf16[1024,128]{1,0:T(8,128)(2,1)S(1)}, u32[]{:S(2)}, u32[]{:S(2)}) collective-permute-start(bf16[1024,128]{1,0:T(8,128)(2,1)} %get-tuple-element.23), channel_id=1, source_target_pairs={{0,1},{1,0},{2,3},{3,2},{4,5},{5,4},{6,7},{7,6},{8,9},{9,8},{10,11... | collective-permute-start | bytes 786440 | tf_op jit(solution)/shard_map/ppermute | solution.py:29
  114.6 8.4 %collective-permute-start.7 = (bf16[1024,128]{1,0:T(8,128)(2,1)S(1)}, bf16[1024,128]{1,0:T(8,128)(2,1)S(1)}, u32[]{:S(2)}, u32[]{:S(2)}) collective-permute-start(bf16[1024,128]{1,0:T(8,128)(2,1)S(1)} %add_convert_fusion), channel_id=1, source_target_pairs={{0,2},{1,3},{2,0},{3,1},{4,6},{5,7},{6,4},{7,5},{8,10},{9,11},{10,... | collective-permute-start | bytes 786440 | tf_op jit(solution)/shard_map/ppermute | solution.py:29
  123.0 1.0 copy-start.5

commit v2 on v0

v2 whole, which is shorter than its diff:
```python
import functools

import jax
import jax.numpy as jnp
from jax import lax
from jax.experimental import pallas as pl
from jax.experimental.pallas import tpu as pltpu
from jax.sharding import PartitionSpec as P

ROOT_HALF = 0.7071067811865476
MIB = 1 << 20
F32 = jnp.float32
BF16 = jnp.bfloat16
VMEM = pl.BlockSpec(memory_space=pltpu.VMEM)
SMEM = pl.BlockSpec(memory_space=pltpu.SMEM)
ANY = pl.BlockSpec(memory_space=pl.ANY)
CHUNKS = 2


def dot(left, right):
    return jnp.dot(left, right, preferred_element_type=F32)


def dot_trans(left, right):
    return lax.dot_general(left, right, (((1,), (1,)), ((), ())), preferred_element_type=F32)


def swapped(array, axis, bit):
    return lax.ppermute(array, axis, [(i, i ^ bit) for i in range(lax.axis_size(axis))])


def left_lanes(shape):
    return lax.broadcasted_iota(jnp.int32, shape, 1) < shape[1] // 2


def turn(values):
    return pltpu.roll(values, values.shape[1] // 2, 1)


def split_pairs(rows, block):
    parts = rows.reshape(-1, 2, block, rows.shape[-1])
    return parts[:, 0].reshape(-1, rows.shape[-1]), parts[:, 1].reshape(-1, rows.shape[-1])


def join_pairs(even, odd, block):
    width = even.shape[-1]
    both = jnp.concatenate([even.reshape(-1, 1, block, width), odd.reshape(-1, 1, block, width)], axis=1)
    return both.reshape(-1, width)


def padded(weight):
    none = jnp.zeros_like(weight)
    return jnp.concatenate([weight, none], axis=0), jnp.concatenate([none, weight], axis=0)


def call(kernel, name, limit, flops, moved, **more):
    return pl.pallas_call(
        kernel,
        compiler_params=pltpu.CompilerParams(vmem_limit_bytes=limit),
        cost_estimate=pl.CostEstimate(flops=flops, bytes_accessed=moved, transcendentals=0),
        name=name,
        **more,
    )


def down_kernel(block, x_ref, wt_ref, pre_ref, trip_ref):
    even, odd = split_pairs(x_ref[...], block)
    left, right = padded(wt_ref[...])
    pre = dot_trans(even, left) + dot_trans(odd, right)
    pre_ref[...] = pre
    trip_ref[...] = (pre * (0.5 * jnp.tanh(0.5 * pre) + 0.5)).astype(BF16)


def down(x, wt, block, steps):
    rows, width = x.shape
    lanes = 2 * wt.shape[0]
    thin = pl.BlockSpec((rows // 2 // steps, lanes), lambda i: (i, 0))
    return call(
        functools.partial(down_kernel, block),
        "down",
        8 * MIB,
        2 * rows * width * lanes,
        2 * rows * width,
        grid=(steps,),
        in_specs=[
            pl.BlockSpec((rows // steps, width), lambda i: (i, 0)),
            pl.BlockSpec(wt.shape, lambda i: (0, 0)),
        ],
        out_specs=[thin] * 2,
        out_shape=[
            jax.ShapeDtypeStruct((rows // 2, lanes), F32),
            jax.ShapeDtypeStruct((rows // 2, lanes), BF16),
        ],
    )(x, wt)


def angle_kernel(block, slots, angle_ref, after_ref, in_ref, out_ref, rows_ref, pair_ref):
    del after_ref
    lanes = 2 * block
    half = block // 2
    mask = left_lanes((half, lanes))
    for at in range(angle_ref.shape[0]):
        wide = angle_ref[at].astype(F32)
        for t in range(half):
            rows_ref[at, t * slots : (t + 1) * slots, :] = wide[:, t * lanes : (t + 1) * lanes]
        for s in range(0, slots, 2):
            first = rows_ref[at, pl.ds(s, half, stride=slots), :]
            second = rows_ref[at, pl.ds(s + 1, half, stride=slots), :]
            pair_ref[at, s // 2, pl.ds(0, half, stride=2), :] = jnp.where(mask, first, turn(second))
            pair_ref[at, s // 2, pl.ds(1, half, stride=2), :] = jnp.where(mask, turn(first), second)
    for at in range(0, angle_ref.shape[0], 2):
        for p in range(slots // 2):
            first, second = pair_ref[at, p], pair_ref[at + 1, p]
            in_ref[at, :, p * lanes : (p + 1) * lanes] = first.astype(BF16)
            in_ref[at + 1, :, p * lanes : (p + 1) * lanes] = second.astype(BF16)
            both = jnp.concatenate([first, second], axis=0)
            out_ref[at // 2, p * lanes : (p + 1) * lanes, :] = both.T.astype(BF16)


def turned_angles(angular, after, block, steps):
    blocks, slots, _ = angular.shape
    per = blocks // steps
    lanes = 2 * block
    return call(
        functools.partial(angle_kernel, block, slots),
        "angles",
        16 * MIB,
        0,
        8 * angular.size * 2,
        grid=(steps,),
        in_specs=[pl.BlockSpec((per, slots, block * block), lambda i: (i, 0, 0)), ANY],
        out_specs=[
            pl.BlockSpec((per, block, slots * block), lambda i: (i, 0, 0)),
            pl.BlockSpec((per // 2, slots * block, lanes), lambda i: (i, 0, 0)),
        ],
        out_shape=[
            jax.ShapeDtypeStruct((blocks, block, slots * block), BF16),
            jax.ShapeDtypeStruct((blocks // 2, slots * block, lanes), BF16),
        ],
        scratch_shapes=[
            pltpu.VMEM((per, slots * block // 2, lanes), F32),
            pltpu.VMEM((per, slots // 2, block, lanes), F32),
        ],
    )(angular, after)


def triplet_kernel(block, slots, pieces, chunks, *refs):
    index_ref, row_ref, place_ref, angle_ref = refs[:4]
    piece_refs = refs[4 : 4 + pieces]
    trip_ref = refs[4 + pieces]
    sent_refs = refs[5 + pieces : 5 + pieces + chunks]
    held_ref = refs[-1]
    packed_rows, lanes = trip_ref.shape
    groups = packed_rows // block
    mask = left_lanes((block, lanes))

    for piece in range(pieces):
        rows = piece_refs[piece][...]
        held_ref[piece * groups : (piece + 1) * groups] = rows.reshape(groups, block, lanes)
        rows = turn(rows.astype(F32)).astype(BF16)
        at = (pieces + piece) * groups
        held_ref[at : at + groups] = rows.reshape(groups, block, lanes)
    held_ref[2 * pieces * groups] = jnp.zeros((block, lanes), BF16)

    def target(q, carry):
        sides = []
        for pair in range(2):
            base = (4 * q + 2 * pair) * slots
            picked = [
                jnp.where(mask, held_ref[index_ref[base + s]], held_ref[index_ref[base + slots + s]])
                for s in range(slots)
            ]
            sides.append(jnp.concatenate(picked, axis=0))
        matrix = angle_ref[pl.ds(4 * q, 4)].reshape(4 * block, slots * block)
        every = dot(matrix, jnp.concatenate(sides, axis=1))
        for pair in range(2):
            part = every[pair * 2 * block : (pair + 1) * 2 * block, pair * lanes : (pair + 1) * lanes]
            total = jnp.where(mask, part[:block], part[block:]).astype(BF16)
            trip_ref[pl.ds(pl.multiple_of((2 * q + pair) * block, block), block), :] = total
        return carry

    lax.fori_loop(0, groups // 2, target, 0, unroll=2)

    place = place_ref[...].T
    turned_half = place >= packed_rows
    spread = []
    wide_mask = left_lanes((2 * block, lanes))
    for m in range(groups):
        rows = trip_ref[m * block : (m + 1) * block, :].astype(F32)
        other = turn(rows)
        both = jnp.concatenate([jnp.where(mask, rows, other), jnp.where(mask, other, rows)], axis=0)
        side = jnp.where(place[:, m : m + 1] < packed_rows, 1.0, 0.0)
        lane_side = jnp.where(wide_mask, 1.0, 0.0)
        spread.append(jnp.where(side == lane_side, both, 0.0).astype(BF16))
    spread = jnp.concatenate(spread, axis=0)
    row = row_ref[...]
    row = jnp.where(row < packed_rows, row, row - packed_rows)
    tile = 4 * block
    for t in range(packed_rows // tile):
        spot = lax.broadcasted_iota(jnp.int32, (tile, 2 * packed_rows), 0) + t * tile
        both = dot((spot == row).astype(F32).astype(BF16), spread).astype(BF16)
        at = t * tile
        per = packed_rows // chunks
        sent_refs[at // per][at % per : at % per + tile, :] = both


def triplet(index, row, place, angles, pieces, block, slots, chunks):
    packed_rows, lanes = pieces[0].shape
    held = packed_rows // block * 2 * len(pieces) + 1
    return call(
        functools.partial(triplet_kernel, block, slots, len(pieces), chunks),
        "triplet",
        12 * MIB + 2 * held * block * lanes,
        2 * packed_rows * slots * block * lanes,
        8 * MIB,
        in_specs=[SMEM] + [VMEM] * (3 + len(pieces)),
        out_specs=[VMEM] * (1 + chunks),
        out_shape=[jax.ShapeDtypeStruct((packed_rows, lanes), BF16)]
        + [jax.ShapeDtypeStruct((packed_rows // chunks, lanes), BF16)] * chunks,
        scratch_shapes=[pltpu.VMEM((held, block, lanes), BF16)],
    )(index, row, place, angles, *pieces)


def gated(half_pre):
    lifted = 1.0 + jnp.tanh(half_pre)
    value = half_pre * lifted
    return value, lifted + value * (2.0 - lifted)


def layer_kernel(block, x_ref, ct_ref, own_ref, far_ref, up_ref, wi_ref, wo_ref, *refs):
    out_ref, grad_ref, near_ref, send_ref = refs[-4:]
    up = up_ref[...] * 0.5
    up2 = jnp.concatenate([up, up], axis=0)
    up_left, up_right = padded(up)
    mask = left_lanes(own_ref.shape)
    none = jnp.zeros(own_ref.shape, BF16)

    def pre_up(ref):
        rows = ref[...]
        return dot(join_pairs(jnp.where(mask, rows, none), jnp.where(mask, none, rows), block), up2)

    own_value, own_slope = gated(pre_up(own_ref))
    far_value, far_slope = gated(pre_up(far_ref))
    hidden = x_ref[...].astype(F32) * ROOT_HALF + (own_value + far_value) * 0.5
    wi, wo = wi_ref[...] * 0.5, wo_ref[...] * 0.5
    in_value, in_slope = gated(dot(hidden.astype(BF16), wi))
    out_value, out_slope = gated(dot(in_value.astype(BF16), wo))
    out_ref[...] = ((hidden + out_value) * ROOT_HALF).astype(BF16)
    scaled = ct_ref[...].astype(F32) * (0.5 * ROOT_HALF)
    grad_out = (scaled * out_slope).astype(BF16)
    grad_in = (dot_trans(grad_out, wo) * in_slope).astype(BF16)
    half_grad = scaled + dot_trans(grad_in, wi)
    grad_ref[...] = (half_grad * (2.0 * ROOT_HALF)).astype(BF16)

    def project(rows):
        even, odd = split_pairs(rows.astype(BF16), block)
        return dot_trans(even, up_left) + dot_trans(odd, up_right)

    near_ref[...] = project(half_grad * own_slope)
    send_ref[...] = project(half_grad * far_slope).astype(BF16)


def layer(x, ct, own, far, up, wi, wo, before, block, steps, chunk, chunks):
    rows, width = x.shape
    lanes = own.shape[1]
    rows_in = rows // chunks // steps
    first = chunk * steps
    whole = lambda array: pl.BlockSpec(array.shape, lambda i: (0, 0))
    wide = pl.BlockSpec((rows_in, width), lambda i: (first + i, 0))
    thin = pl.BlockSpec((rows_in // 2, lanes), lambda i: (first + i, 0))
    part = pl.BlockSpec((rows_in // 2, lanes), lambda i: (i, 0))
    return call(
        functools.partial(layer_kernel, block),
        "layer",
        24 * MIB,
        rows // chunks * width * (8 * width + 8 * lanes),
        rows // chunks * width * 8,
        grid=(steps,),
        in_specs=[wide, wide, thin, part] + [whole(w) for w in (up, wi, wo)] + [ANY] * len(before),
        out_specs=[wide, wide, part, part],
        out_shape=[
            jax.ShapeDtypeStruct((rows, width), BF16),
            jax.ShapeDtypeStruct((rows, width), BF16),
            jax.ShapeDtypeStruct((rows // 2 // chunks, lanes), F32),
            jax.ShapeDtypeStruct((rows // 2 // chunks, lanes), BF16),
        ],
        input_output_aliases={7 + i: i for i in range(len(before))},
    )(x, ct, own, far, up, wi, wo, *before)


def scatter_kernel(block, slots, pieces, chunks, index_ref, place_ref, angle_ref, *refs):
    near_refs, far_refs = refs[:chunks], refs[chunks : 2 * chunks]
    out_refs = refs[2 * chunks : 2 * chunks + pieces]
    total_ref, grad_ref = refs[2 * chunks + pieces :]
    packed_rows, lanes = grad_ref.shape
    groups = packed_rows // block
    mask = left_lanes((block, lanes))
    total_ref[...] = jnp.zeros(total_ref.shape, F32)
    place = place_ref[...].T
    per = packed_rows // chunks
    tile = 2 * block
    wide_mask = left_lanes((tile, lanes))
    lane_side = jnp.where(wide_mask, 1.0, 0.0)
    several = 4
    for start in range(0, groups, several):
        spots, sides = [], []
        for m in range(start, start + several):
            column = place[:, m : m + 1]
            low = column < packed_rows
            spot = lax.broadcasted_iota(jnp.int32, (tile, packed_rows), 1)
            spots.append((spot == jnp.where(low, column, column - packed_rows)).astype(F32).astype(BF16))
            sides.append(jnp.where(low, 1.0, 0.0))
        spots = jnp.concatenate(spots, axis=0)
        got = dot(spots[:, :per], far_refs[0][...])
        for c in range(1, chunks):
            got = got + dot(spots[:, c * per : (c + 1) * per], far_refs[c][...])
        for i, m in enumerate(range(start, start + several)):
            mine = jnp.where(sides[i] == lane_side, got[i * tile : (i + 1) * tile], 0.0)
            mine = mine + turn(mine)
            at = m * block
            near = near_refs[at // per][at % per : at % per + block, :]
            grad_ref[at : at + block, :] = (near + jnp.where(mask, mine[:block], mine[block:])).astype(BF16)
    none = jnp.zeros((block, lanes), BF16)

    def target(m, carry):
        rows = grad_ref[pl.ds(pl.multiple_of(m * block, block), block), :]
        pair = jnp.concatenate([jnp.where(mask, rows, none), jnp.where(mask, none, rows)], axis=0)
        terms = dot(angle_ref[m], pair)
        base = m * (2 * slots)
        for s in range(slots):
            term = terms[s * block : (s + 1) * block]
            total_ref[index_ref[base + s]] += jnp.where(mask, term, 0.0)
            total_ref[index_ref[base + slots + s]] += jnp.where(mask, 0.0, term)
        return carry

    lax.fori_loop(0, groups, target, 0, unroll=4)

    for piece in range(pieces):
        at = piece * groups
        straight = total_ref[at : at + groups].reshape(packed_rows, lanes)
        at += pieces * groups
        crossed = total_ref[at : at + groups].reshape(packed_rows, lanes)
        out_refs[piece][...] = (straight + turn(crossed)).astype(out_refs[piece].dtype)


def scatter(index, place, angles, near, far, types, block, slots):
    chunks = len(near)
    packed_rows, lanes = near[0].shape[0] * chunks, near[0].shape[1]
    pieces = len(types)
    held = 2 * pieces * (packed_rows // block) + 1
    return call(
        functools.partial(scatter_kernel, block, slots, pieces, chunks),
        "scatter",
        16 * MIB + 4 * held * block * lanes,
        2 * packed_rows * slots * block * lanes,
        8 * MIB,
        in_specs=[SMEM] + [VMEM] * (2 + 2 * chunks),
        out_specs=[VMEM] * pieces,
        out_shape=[jax.ShapeDtypeStruct((packed_rows, lanes), kind) for kind in types],
        scratch_shapes=[
            pltpu.VMEM((held, block, lanes), F32),
            pltpu.VMEM((packed_rows, lanes), BF16),
        ],
    )(index, place, angles, *near, *far)


def last_kernel(block, pre_ref, grad_ref, wt_ref, *refs):
    out_ref = refs[-1]
    total = refs[0][...].astype(F32)
    for ref in refs[1:-1]:
        total = total + ref[...].astype(F32)
    _, slope = gated(pre_ref[...] * 0.5)
    grad = (total * (0.5 * slope)).astype(BF16)
    left, right = padded(wt_ref[...])
    both = join_pairs(dot(grad, left), dot(grad, right), block)
    out_ref[...] = (grad_ref[...].astype(F32) + both).astype(BF16)


def last(pre, grad_msg, wt, terms, block, steps):
    rows, width = grad_msg.shape
    lanes = 2 * wt.shape[0]
    wide = pl.BlockSpec((rows // steps, width), lambda i: (i, 0))
    thin = pl.BlockSpec((rows // 2 // steps, lanes), lambda i: (i, 0))
    return call(
        functools.partial(last_kernel, block),
        "last",
        16 * MIB,
        2 * rows * width * lanes,
        4 * rows * width,
        grid=(steps,),
        in_specs=[thin, wide, pl.BlockSpec(wt.shape, lambda i: (0, 0))] + [thin] * len(terms),
        out_specs=wide,
        out_shape=jax.ShapeDtypeStruct((rows, width), BF16),
    )(pre, grad_msg, wt, *terms)


def on_device(
    edge_feats,
    cotangent,
    down_weight,
    up_weight,
    inner_weight,
    outer_weight,
    angular,
    reverse,
    sources,
    counts,
):
    lane_count = lax.axis_size("narrow")
    top_bit = lax.axis_size("cluster") // 2
    me = lax.axis_index("narrow")
    local_blocks, slots = sources.shape
    local_edges = edge_feats.shape[0]
    block = local_edges // local_blocks
    groups = local_blocks // 2
    packed_rows = local_edges // 2
    down_trans = down_weight.T

    live = lax.broadcasted_iota(jnp.int32, sources.shape, 1) < counts[:, None]
    local = sources % (local_blocks * lane_count)
    spot = (local // local_blocks ^ me) * local_blocks + local % local_blocks
    odd = lax.broadcasted_iota(jnp.int32, sources.shape, 0) % 2
    turned = jnp.where(spot % 2 == odd, 0, lane_count * groups)
    index = jnp.where(live, turned + spot // 2, 2 * lane_count * groups).reshape(-1)

    slot = reverse % local_edges
    place = (slot // block % 2) * packed_rows + slot // (2 * block) * block + slot % block
    place_row = place.reshape(1, local_edges)
    place = place.reshape(groups, 2 * block)

    pre_down, trip = down(edge_feats, down_trans, block, 4)
    angle_in, angle_out = turned_angles(angular, trip, block, 4)
    pieces = {0: trip}
    bits = [1 << i for i in range(lane_count.bit_length() - 1)]
    for bit in reversed(bits):
        pieces.update({d ^ bit: swapped(piece, "narrow", bit) for d, piece in pieces.items()})
    pieces = [pieces[d] for d in range(lane_count)]
    trip_own, *trip_sent = triplet(index, place_row, place, angle_in, pieces, block, slots, CHUNKS)
    trip_far = [swapped(part, "cluster", top_bit) for part in trip_sent]
    done, near, far = [], [], []
    for chunk in range(CHUNKS):
        *done, own_part, sent = layer(
            edge_feats,
            cotangent,
            trip_own,
            trip_far[chunk],
            up_weight,
            inner_weight[0],
            outer_weight[0],
            done,
            block,
            2,
            chunk,
            CHUNKS,
        )
        near.append(own_part)
        far.append(swapped(sent, "cluster", top_bit))
    output, grad_msg = done
    types = [BF16 if d % 2 else F32 for d in range(lane_count)]
    parts = dict(enumerate(scatter(index, place, angle_out, near, far, types, block, slots)))
    terms = [parts[0]]
    for bit in bits:
        for d in range(lane_count - bit, -1, -2 * bit):
            got = swapped(parts[d].astype(BF16), "narrow", bit)
            if d == bit:
                terms.append(got)
            else:
                parts[d ^ bit] = parts[d ^ bit] + got.astype(F32)
    grad_x = last(pre_down, grad_msg, down_trans, terms, block, 4)
    return (output, grad_x)


def solution(mesh):
    in_specs = (
        P(("cluster", "narrow"), None),
        P(("cluster", "narrow"), None),
        P(),
        P(),
        P(),
        P(),
        P(("cluster", "narrow"), None, None),
        P(("cluster", "narrow")),
        P(("cluster", "narrow"), None),
        P(("cluster", "narrow")),
    )
    out_specs = (P(("cluster", "narrow"), None), P(("cluster", "narrow"), None))
    return jax.shard_map(
        on_device, mesh=mesh, in_specs=in_specs, out_specs=out_specs, check_vma=False
    )
```

time: 274 us -> 77.8 us (0.28)
  waiting for transfers between devices: 151 us -> 35.5 us
  matrix products: 53.4 us -> 0 us
  local copies, waits for them, and re-layouts: 48.2 us -> 2.79 us
  Pallas kernels: 0 us -> 27.4 us
  between operations: 14.3 us -> 0.81 us
  starting transfers between devices: 2.55 us -> 11 us
  other arithmetic: 4.6 us -> 0.16 us
    ppermute x2 -> x10, waiting for transfers between devices: 114 us -> 35.5 us  [swapped(): lax.ppermute(array, axis, [(i, i ^ bit) for i in range(lax.axis_size(axis...]
    dot_general x13 -> x0, matrix products: 53.4 us -> none  [the longest x3 20.3 us: dot_trans(): lax.dot_general(operand, matrix, (((1,), (1,)), ((), ())), preferred_elem...]
    pallas_call x0 -> x7, Pallas kernels: none -> 27.4 us  [the longest x2 11.5 us: layer(): call(functools.partial(layer_kernel, block), 'layer', 24 * MIB, rows // c...]
    reduce_scatter x1 -> x0, waiting for transfers between devices: 22.9 us -> none  [on_device(): lax.psum_scatter((upper + jnp.einsum('ksp,ksf->pf', selector, low_terms,...]
    reshape x7 -> x1, local copies, waits for them, and re-layouts: 22.4 us -> 0.09 us  [on_device(): jnp.where(live, turned + spot // 2, 2 * lane_count * groups).reshape(-1)]
    gather x2 -> x0, local copies, waits for them, and re-layouts: 15.4 us -> none  [the longest x1 9.2 us: on_device(): partner_grad = swapped(grad_msg_round, 'cluster', top_bit)[rev_slot]]
    all_gather x1 -> x0, waiting for transfers between devices: 13.8 us -> none  [on_device(): shard_piece = lax.all_gather(trip_blocks, 'narrow', axis=0, tiled=True)]
    dot_general x1 -> x0, local copies, waits for them, and re-layouts: 8.98 us -> none  [on_device(): jnp.einsum('ksij,kif->ksjf', angle_mats, grad_blocks, preferred_element_t...]
  transfers between devices with their start and end apart: 4 -> 10, of which waited for: 4 -> 6; matrix products, arithmetic and copies ran while one was open for 3% -> 0% of each run, Pallas kernels for 0% -> 11%
where the time goes in v2:
time: 77.8 us; the launch traced here: 77.7 us
  waiting for transfers between devices  35.5 us (46%)
  Pallas kernels  27.4 us (35%)
  starting transfers between devices  11 us (14%)
  local copies, waits for them, and re-layouts  2.79 us (4%)
  between operations  0.81 us (1%)
    ppermute x10, waiting for transfers between devices, swapped(): lax.ppermute(array, axis, [(i, i ^ bit) for i in range(lax.axis_size(axis...  35.5 us
    pallas_call x2, Pallas kernels, layer(): call(functools.partial(layer_kernel, block), 'layer', 24 * MIB, rows // c...  11.5 us
    ppermute x10, starting transfers between devices, swapped(): lax.ppermute(array, axis, [(i, i ^ bit) for i in range(lax.axis_size(axis...  11 us
    pallas_call x1, Pallas kernels, scatter(): call(functools.partial(scatter_kernel, block, slots, pieces, chunks), 'sc...  5.28 us
    pallas_call x1, Pallas kernels, triplet(): call(functools.partial(triplet_kernel, block, slots, len(pieces), chunks)...  4.42 us
    unnamed x24, local copies, waits for them, and re-layouts  2.62 us
    pallas_call x1, Pallas kernels, turned_angles(): call(functools.partial(angle_kernel, block, slots), 'angles', 16 * MIB, 0...  2.54 us
    pallas_call x1, Pallas kernels, last(): call(functools.partial(last_kernel, block), 'last', 16 * MIB, 2 * rows *...  2.48 us
  transfers between devices with their start and end apart: 10, of which 6 were waited for; matrix products, arithmetic and copies ran while one was open for 0% of the time, Pallas kernels for 11%

profile of v2, /device:TPU:0, one launch (start us, length us, event | category | flops | bytes accessed | tf_op | source)
XLA Modules:
  0.0 77.7 jit_solution(12363866743035486225)
XLA Ops:
  0.6 0.0 copy-start
  0.6 0.0 copy-start.1
  0.7 1.7 %copy-done.1 = bf16[2048,512]{1,0:T(8,128)(2,1)S(1)} copy-done((bf16[2048,512]{1,0:T(8,128)(2,1)S(1)}, bf16[2048,512]{1,0:T(8,128)(2,1)}, u32[]{:S(2)}) %copy-start.1) | copy-done | bytes 2097176
  2.4 0.8 %copy-done.3 = bf16[512,64]{0,1:T(8,128)(2,1)S(1)} copy-done((bf16[512,64]{0,1:T(8,128)(2,1)S(1)}, bf16[512,64]{0,1:T(8,128)(2,1)}, u32[]{:S(2)}) %copy-start.3) | copy-done | bytes 65560
  3.2 1.2 %down.1 = (f32[1024,128]{1,0:T(8,128)S(1)}, bf16[1024,128]{1,0:T(8,128)(2,1)S(1)}) custom-call(bf16[2048,512]{1,0:T(8,128)(2,1)S(1)} %copy-done.1, bf16[64,512]{1,0:T(8,128)(2,1)S(1)} %bitcast.6), custom_call_target="tpu_custom_call" | custom-call | flops 268435456 | bytes 2097152 | tf_op jit(solution)/shard_map/down/pallas_call | solution.py:78
  4.4 3.0 %collective-permute-start.1 = (bf16[1024,128]{1,0:T(8,128)(2,1)S(1)}, bf16[1024,128]{1,0:T(8,128)(2,1)S(1)}, u32[]{:S(2)}, u32[]{:S(2)}) collective-permute-start(bf16[1024,128]{1,0:T(8,128)(2,1)S(1)} %get-tuple-element.21.after_ref.refs_4_), channel_id=1, source_target_pairs={{0,2},{1,3},{2,0},{3,1},{4,6},{5,7},{6,4},{7,5},{8,10},{9,11},{10,... | collective-permute-start | bytes 786440 | tf_op jit(solution)/shard_map/ppermute | solution.py:29
  7.5 0.0 collective-permute-start
  7.5 0.0 copy-done.9
  7.5 6.2 %collective-permute-done.1.refs_6_ = bf16[1024,128]{1,0:T(8,128)(2,1)S(1)} collective-permute-done((bf16[1024,128]{1,0:T(8,128)(2,1)S(1)}, bf16[1024,128]{1,0:T(8,128)(2,1)S(1)}, u32[]{:S(2)}, u32[]{:S(2)}) %collective-permute-start.1) | collective-permute-done | bytes 262176 | tf_op jit(solution)/shard_map/ppermute | solution.py:29
  13.8 0.0 collective-permute-start.2
  13.8 0.0 copy-done.10
  13.8 0.0 copy-done.11
  13.8 0.1 copy.14
  13.9 0.1 reshape.14.refs_0_.index_ref
  14.0 0.0 copy-done
  14.0 0.0 copy-start.5
  14.0 0.0 copy-start.8
  14.0 2.5 %angles.1 = (bf16[32,64,512]{2,1,0:T(8,128)(2,1)S(1)}, bf16[16,512,128]{2,1,0:T(8,128)(2,1)S(1)}) custom-call(bf16[32,8,4096]{2,1,0:T(8,128)(2,1)S(1)} %copy-done, bf16[1024,128]{1,0:T(8,128)(2,1)S(1)} %get-tuple-element.21.after_ref.refs_4_), custom_call_target="tpu_custom_call" | custom-call | bytes 16777216 | tf_op jit(solution)/shard_map/angles/pallas_call | solution.py:124
  16.6 0.0 copy-start.2
  16.6 0.0 copy-start.6
  16.6 0.0 copy-start.7
  16.6 0.0 collective-permute-done.refs_5_
  16.7 0.0 collective-permute-done.2.refs_7_
  16.7 4.4 %triplet.1 = (bf16[1024,128]{1,0:T(8,128)(2,1)S(1)}, bf16[512,128]{1,0:T(8,128)(2,1)S(1)}, bf16[512,128]{1,0:T(8,128)(2,1)S(1)}) custom-call(s32[256]{0:T(256)S(1)} %reshape.14.refs_0_.index_ref, s32[1,2048]{1,0:T(1,128)S(1)} %bitcast.8, s32[16,128]{1,0:T(8,128)S(1)} %fusion.24.refs_2_.place_ref, bf16[32,64,512]{2,1,0:T(8,128)(2,1)S(1)} %get-tuple-element.22.refs_3_, ...), custom_call_target="tpu_custom_call" | custom-call | flops 134217728 | bytes 8388608 | tf_op jit(solution)/shard_map/triplet/pallas_call | solution.py:210
  21.1 2.9 %collective-permute-start.4 = (bf16[512,128]{1,0:T(8,128)(2,1)S(1)}, bf16[512,128]{1,0:T(8,128)(2,1)S(1)}, u32[]{:S(2)}, u32[]{:S(2)}) collective-permute-start(bf16[512,128]{1,0:T(8,128)(2,1)S(1)} %get-tuple-element.25), channel_id=1, source_target_pairs={{0,16},{4,20},{8,24},{12,28},{16,0},{20,4},{24,8},{28,12},{1,17},{... | collective-permute-start | bytes 393224 | tf_op jit(solution)/shard_map/ppermute | solution.py:29
  24.0 0.1 collective-permute-start.3
  24.1 9.9 %collective-permute-done.4.far_ref = bf16[512,128]{1,0:T(8,128)(2,1)S(1)} collective-permute-done((bf16[512,128]{1,0:T(8,128)(2,1)S(1)}, bf16[512,128]{1,0:T(8,128)(2,1)S(1)}, u32[]{:S(2)}, u32[]{:S(2)}) %collective-permute-start.4) | collective-permute-done | bytes 131104 | tf_op jit(solution)/shard_map/ppermute | solution.py:29
  34.0 0.0 copy-done.5
  34.0 0.0 copy-done.8
  34.0 0.0 copy-done.2
  34.1 0.0 copy-done.6
  34.1 0.0 copy-done.7
  34.1 5.7 %layer.2 = (bf16[2048,512]{1,0:T(8,128)(2,1)}, bf16[2048,512]{1,0:T(8,128)(2,1)S(1)}, f32[512,128]{1,0:T(8,128)S(1)}, bf16[512,128]{1,0:T(8,128)(2,1)S(1)}) custom-call(bf16[2048,512]{1,0:T(8,128)(2,1)S(1)} %copy-done.2, bf16[2048,512]{1,0:T(8,128)(2,1)S(1)} %copy-done.5, bf16[1024,128]{1,0:T(8,128)(2,1)S(1)} %get-tuple-element.23.own_ref, ...), custom_call_target="tpu_custom_call" | custom-call | flops 2684354560 | bytes 4194304 | tf_op jit(solution)/shard_map/layer/pallas_call | solution.py:272
  39.8 0.0 collective-permute-done.3.far_ref
  39.8 5.7 %layer.3 = (bf16[2048,512]{1,0:T(8,128)(2,1)}, bf16[2048,512]{1,0:T(8,128)(2,1)S(1)}, f32[512,128]{1,0:T(8,128)S(1)}, bf16[512,128]{1,0:T(8,128)(2,1)S(1)}) custom-call(bf16[2048,512]{1,0:T(8,128)(2,1)S(1)} %copy-done.2, bf16[2048,512]{1,0:T(8,128)(2,1)S(1)} %copy-done.5, ...), custom_call_target="tpu_custom_call", output_to_operand_aliasing={{0}: (7, {}), {1}: (8, {})} | custom-call | flops 2684354560 | bytes 4194304 | tf_op jit(solution)/shard_map/layer/pallas_call | solution.py:272
  45.5 0.0 collective-permute-start.6
  45.5 2.9 %collective-permute-start.5 = (bf16[512,128]{1,0:T(8,128)(2,1)S(1)}, bf16[512,128]{1,0:T(8,128)(2,1)S(1)}, u32[]{:S(2)}, u32[]{:S(2)}) collective-permute-start(bf16[512,128]{1,0:T(8,128)(2,1)S(1)} %get-tuple-element.34), channel_id=1, source_target_pairs={{0,16},{4,20},{8,24},{12,28},{16,0},{20,4},{24,8},{28,12},{1,17},{... | collective-permute-start | bytes 393224 | tf_op jit(solution)/shard_map/ppermute | solution.py:29
  48.5 9.8 %collective-permute-done.6.refs_3_ = bf16[512,128]{1,0:T(8,128)(2,1)S(1)} collective-permute-done((bf16[512,128]{1,0:T(8,128)(2,1)S(1)}, bf16[512,128]{1,0:T(8,128)(2,1)S(1)}, u32[]{:S(2)}, u32[]{:S(2)}) %collective-permute-start.6) | collective-permute-done | bytes 131104 | tf_op jit(solution)/shard_map/ppermute | solution.py:29
  58.3 1.5 %collective-permute-done.5.refs_2_ = bf16[512,128]{1,0:T(8,128)(2,1)S(1)} collective-permute-done((bf16[512,128]{1,0:T(8,128)(2,1)S(1)}, bf16[512,128]{1,0:T(8,128)(2,1)S(1)}, u32[]{:S(2)}, u32[]{:S(2)}) %collective-permute-start.5) | collective-permute-done | bytes 131104 | tf_op jit(solution)/shard_map/ppermute | solution.py:29
  59.8 5.3 %scatter.1 = (f32[1024,128]{1,0:T(8,128)S(1)}, bf16[1024,128]{1,0:T(8,128)(2,1)S(1)}, f32[1024,128]{1,0:T(8,128)S(1)}, bf16[1024,128]{1,0:T(8,128)(2,1)S(1)}) custom-call(s32[256]{0:T(256)S(1)} %reshape.14.refs_0_.index_ref, s32[16,128]{1,0:T(8,128)S(1)} %fusion.24.refs_2_.place_ref, bf16[16,512,128]{2,1,0:T(8,128)(2,1)S(1)} %get-tuple-element.31.angle_ref, ...), custom_call_target="tpu_custom_call" | custom-call | flops 134217728 | bytes 8388608 | tf_op jit(solution)/shard_map/scatter/pallas_call | solution.py:351
  65.1 0.1 collective-permute-start.8
  65.2 0.5 collective-permute-start.7
  65.7 1.0 %collective-permute-done.8 = bf16[1024,128]{1,0:T(8,128)(2,1)S(1)} collective-permute-done((bf16[1024,128]{1,0:T(8,128)(2,1)S(1)}, bf16[1024,128]{1,0:T(8,128)(2,1)S(1)}, u32[]{:S(2)}, u32[]{:S(2)}) %collective-permute-start.8) | collective-permute-done | bytes 262176 | tf_op jit(solution)/shard_map/ppermute | solution.py:29
  66.7 0.1 add_convert_fusion
  66.8 1.4 %collective-permute-start.9 = (bf16[1024,128]{1,0:T(8,128)(2,1)S(1)}, bf16[1024,128]{1,0:T(8,128)(2,1)S(1)}, u32[]{:S(2)}, u32[]{:S(2)}) collective-permute-start(bf16[1024,128]{1,0:T(8,128)(2,1)S(1)} %add_convert_fusion), channel_id=1, source_target_pairs={{0,2},{1,3},{2,0},{3,1},{4,6},{5,7},{6,4},{7,5},{8,10},{9,11},{10,... | collective-permute-start | bytes 786440 | tf_op jit(solution)/shard_map/ppermute | solution.py:29
  68.2 0.0 collective-permute-done.7.refs_1_
  68.2 7.0 %collective-permute-done.9.refs_2_ = bf16[1024,128]{1,0:T(8,128)(2,1)S(1)} collective-permute-done((bf16[1024,128]{1,0:T(8,128)(2,1)S(1)}, bf16[1024,128]{1,0:T(8,128)(2,1)S(1)}, u32[]{:S(2)}, u32[]{:S(2)}) %collective-permute-start.9) | collective-permute-done | bytes 262176 | tf_op jit(solution)/shard_map/ppermute | solution.py:29
  75.2 2.5 %last.1 = bf16[2048,512]{1,0:T(8,128)(2,1)} custom-call(f32[1024,128]{1,0:T(8,128)S(1)} %get-tuple-element.29.pre_ref, bf16[2048,512]{1,0:T(8,128)(2,1)S(1)} %get-tuple-element.30.grad_ref, bf16[64,512]{1,0:T(8,128)(2,1)S(1)} %bitcast.7, f32[1024,128]{1,0:T(8,128)S(1)} %get-tuple-element.36.refs_0_, bf16[1024,128]{1,0:T(8,128)(2,1)S(1)} %collective-permute-done.7.refs_1_, ...), custom_call_target="tpu_custom_call" | custom-call | flops 268435456 | bytes 4194304 | tf_op jit(solution)/shard_map/last/pallas_call | solution.py:384
  (11 shorter events, 0.1 us)
Async XLA Ops:
  0.6 13.4 %copy-start = (bf16[32,8,4096]{2,1,0:T(8,128)(2,1)S(1)}, bf16[32,8,4096]{2,1,0:T(8,128)(2,1)}, u32[]{:S(2)}) copy-start(bf16[32,8,4096]{2,1,0:T(8,128)(2,1)} %angle_ref.1) | copy-start | bytes 6291460
  0.6 1.7 %copy-start.1 = (bf16[2048,512]{1,0:T(8,128)(2,1)S(1)}, bf16[2048,512]{1,0:T(8,128)(2,1)}, u32[]{:S(2)}) copy-start(bf16[2048,512]{1,0:T(8,128)(2,1)} %x_ref.5) | copy-start | bytes 6291460
  2.4 0.8 %copy-start.3 = (bf16[512,64]{0,1:T(8,128)(2,1)S(1)}, bf16[512,64]{0,1:T(8,128)(2,1)}, u32[]{:S(2)}) copy-start(bf16[512,64]{0,1:T(8,128)(2,1)} %param.12) | copy-start | bytes 196612
  3.2 4.3 %copy-start.9 = (s32[2048]{0:T(1024)S(1)}, s32[2048]{0:T(1024)}, u32[]{:S(2)}) copy-start(s32[2048]{0:T(1024)} %param.17) | copy-start | bytes 24580
  3.2 10.6 %copy-start.10 = (s32[32,8]{0,1:T(8,128)S(1)}, s32[32,8]{0,1:T(8,128)}, u32[]{:S(2)}) copy-start(s32[32,8]{0,1:T(8,128)} %param.18) | copy-start | bytes 3076
  3.2 10.6 %copy-start.11 = (s32[32]{0:T(128)S(1)}, s32[32]{0:T(128)}, u32[]{:S(2)}) copy-start(s32[32]{0:T(128)} %param.19) | copy-start | bytes 388
  4.4 9.3 %collective-permute-start.1 = (bf16[1024,128]{1,0:T(8,128)(2,1)S(1)}, bf16[1024,128]{1,0:T(8,128)(2,1)S(1)}, u32[]{:S(2)}, u32[]{:S(2)}) collective-permute-start(bf16[1024,128]{1,0:T(8,128)(2,1)S(1)} %get-tuple-element.21.after_ref.refs_4_), channel_id=1, source_target_pairs={{0,2},{1,3},{2,0},{3,1},{4,6},{5,7},{6,4},{7,5},{8,10},{9,11},{10,... | collective-permute-start | bytes 786440 | tf_op jit(solution)/shard_map/ppermute | solution.py:29
  7.5 9.2 %collective-permute-start = (bf16[1024,128]{1,0:T(8,128)(2,1)S(1)}, bf16[1024,128]{1,0:T(8,128)(2,1)S(1)}, u32[]{:S(2)}, u32[]{:S(2)}) collective-permute-start(bf16[1024,128]{1,0:T(8,128)(2,1)S(1)} %get-tuple-element.21.after_ref.refs_4_), channel_id=1, source_target_pairs={{0,1},{1,0},{2,3},{3,2},{4,5},{5,4},{6,7},{7,6},{8,9},{9,8},{10,11... | collective-permute-start | bytes 786440 | tf_op jit(solution)/shard_map/ppermute | solution.py:29
  13.8 2.9 %collective-permute-start.2 = (bf16[1024,128]{1,0:T(8,128)(2,1)S(1)}, bf16[1024,128]{1,0:T(8,128)(2,1)}, u32[]{:S(2)}, u32[]{:S(2)}) collective-permute-start(bf16[1024,128]{1,0:T(8,128)(2,1)S(1)} %collective-permute-done.1.refs_6_), channel_id=1, source_target_pairs={{0,1},{1,0},{2,3},{3,2},{4,5},{5,4},{6,7},{7,6},{8,9},{9,8},{10,11... | collective-permute-start | bytes 786440 | tf_op jit(solution)/shard_map/ppermute | solution.py:29
  14.0 20.0 %copy-start.5 = (bf16[2048,512]{1,0:T(8,128)(2,1)S(1)}, bf16[2048,512]{1,0:T(8,128)(2,1)}, u32[]{:S(2)}) copy-start(bf16[2048,512]{1,0:T(8,128)(2,1)} %ct_ref.3) | copy-start | bytes 6291460
  14.0 20.0 %copy-start.8 = (bf16[64,512]{1,0:T(8,128)(2,1)S(1)}, bf16[64,512]{1,0:T(8,128)(2,1)}, u32[]{:S(2)}) copy-start(bf16[64,512]{1,0:T(8,128)(2,1)} %up_ref.3) | copy-start | bytes 196612
  16.6 17.5 %copy-start.2 = (bf16[2048,512]{1,0:T(8,128)(2,1)S(1)}, bf16[2048,512]{1,0:T(8,128)(2,1)}, u32[]{:S(2)}) copy-start(bf16[2048,512]{1,0:T(8,128)(2,1)} %x_ref.5) | copy-start | bytes 6291460
  16.6 17.5 %copy-start.6 = (bf16[1,512,512]{2,1,0:T(8,128)(2,1)S(1)}, bf16[1,512,512]{2,1,0:T(8,128)(2,1)}, u32[]{:S(2)}) copy-start(bf16[1,512,512]{2,1,0:T(8,128)(2,1)} %param.14) | copy-start | bytes 1572868
  16.6 17.5 %copy-start.7 = (bf16[1,512,512]{2,1,0:T(8,128)(2,1)S(1)}, bf16[1,512,512]{2,1,0:T(8,128)(2,1)}, u32[]{:S(2)}) copy-start(bf16[1,512,512]{2,1,0:T(8,128)(2,1)} %param.15) | copy-start | bytes 1572868
  21.1 13.0 %collective-permute-start.4 = (bf16[512,128]{1,0:T(8,128)(2,1)S(1)}, bf16[512,128]{1,0:T(8,128)(2,1)S(1)}, u32[]{:S(2)}, u32[]{:S(2)}) collective-permute-start(bf16[512,128]{1,0:T(8,128)(2,1)S(1)} %get-tuple-element.25), channel_id=1, source_target_pairs={{0,16},{4,20},{8,24},{12,28},{16,0},{20,4},{24,8},{28,12},{1,17},{... | collective-permute-start | bytes 393224 | tf_op jit(solution)/shard_map/ppermute | solution.py:29
  24.0 15.8 %collective-permute-start.3 = (bf16[512,128]{1,0:T(8,128)(2,1)S(1)}, bf16[512,128]{1,0:T(8,128)(2,1)S(1)}, u32[]{:S(2)}, u32[]{:S(2)}) collective-permute-start(bf16[512,128]{1,0:T(8,128)(2,1)S(1)} %get-tuple-element.24), channel_id=1, source_target_pairs={{0,16},{4,20},{8,24},{12,28},{16,0},{20,4},{24,8},{28,12},{1,17},{... | collective-permute-start | bytes 393224 | tf_op jit(solution)/shard_map/ppermute | solution.py:29
  45.5 29.6 %copy-start.4 = (bf16[512,64]{0,1:T(8,128)(2,1)S(1)}, bf16[512,64]{0,1:T(8,128)(2,1)}, u32[]{:S(2)}) copy-start(bf16[512,64]{0,1:T(8,128)(2,1)} %param.12) | copy-start | bytes 196612
  45.5 12.8 %collective-permute-start.6 = (bf16[512,128]{1,0:T(8,128)(2,1)S(1)}, bf16[512,128]{1,0:T(8,128)(2,1)S(1)}, u32[]{:S(2)}, u32[]{:S(2)}) collective-permute-start(bf16[512,128]{1,0:T(8,128)(2,1)S(1)} %get-tuple-element.35), channel_id=1, source_target_pairs={{0,16},{4,20},{8,24},{12,28},{16,0},{20,4},{24,8},{28,12},{1,17},{... | collective-permute-start | bytes 393224 | tf_op jit(solution)/shard_map/ppermute | solution.py:29
  45.5 14.3 %collective-permute-start.5 = (bf16[512,128]{1,0:T(8,128)(2,1)S(1)}, bf16[512,128]{1,0:T(8,128)(2,1)S(1)}, u32[]{:S(2)}, u32[]{:S(2)}) collective-permute-start(bf16[512,128]{1,0:T(8,128)(2,1)S(1)} %get-tuple-element.34), channel_id=1, source_target_pairs={{0,16},{4,20},{8,24},{12,28},{16,0},{20,4},{24,8},{28,12},{1,17},{... | collective-permute-start | bytes 393224 | tf_op jit(solution)/shard_map/ppermute | solution.py:29
  65.1 1.6 %collective-permute-start.8 = (bf16[1024,128]{1,0:T(8,128)(2,1)S(1)}, bf16[1024,128]{1,0:T(8,128)(2,1)S(1)}, u32[]{:S(2)}, u32[]{:S(2)}) collective-permute-start(bf16[1024,128]{1,0:T(8,128)(2,1)S(1)} %get-tuple-element.39), channel_id=1, source_target_pairs={{0,1},{1,0},{2,3},{3,2},{4,5},{5,4},{6,7},{7,6},{8,9},{9,8},{10,11... | collective-permute-start | bytes 786440 | tf_op jit(solution)/shard_map/ppermute | solution.py:29
  65.2 3.0 %collective-permute-start.7 = (bf16[1024,128]{1,0:T(8,128)(2,1)S(1)}, bf16[1024,128]{1,0:T(8,128)(2,1)S(1)}, u32[]{:S(2)}, u32[]{:S(2)}) collective-permute-start(bf16[1024,128]{1,0:T(8,128)(2,1)S(1)} %get-tuple-element.37), channel_id=1, source_target_pairs={{0,1},{1,0},{2,3},{3,2},{4,5},{5,4},{6,7},{7,6},{8,9},{9,8},{10,11... | collective-permute-start | bytes 786440 | tf_op jit(solution)/shard_map/ppermute | solution.py:29
  66.8 8.4 %collective-permute-start.9 = (bf16[1024,128]{1,0:T(8,128)(2,1)S(1)}, bf16[1024,128]{1,0:T(8,128)(2,1)S(1)}, u32[]{:S(2)}, u32[]{:S(2)}) collective-permute-start(bf16[1024,128]{1,0:T(8,128)(2,1)S(1)} %add_convert_fusion), channel_id=1, source_target_pairs={{0,2},{1,3},{2,0},{3,1},{4,6},{5,7},{6,4},{7,5},{8,10},{9,11},{10,... | collective-permute-start | bytes 786440 | tf_op jit(solution)/shard_map/ppermute | solution.py:29

commit v3 on v2

v3 whole, which is shorter than its diff:
```python
import functools

import jax
import jax.numpy as jnp
from jax import lax
from jax.experimental import pallas as pl
from jax.experimental.pallas import tpu as pltpu
from jax.sharding import PartitionSpec as P

ROOT_HALF = 0.7071067811865476
MIB = 1 << 20
F32 = jnp.float32
BF16 = jnp.bfloat16
VMEM = pl.BlockSpec(memory_space=pltpu.VMEM)
SMEM = pl.BlockSpec(memory_space=pltpu.SMEM)
ANY = pl.BlockSpec(memory_space=pl.ANY)
HBM = pl.BlockSpec(memory_space=pltpu.HBM)


def dot(left, right):
    return jnp.dot(left, right, preferred_element_type=F32)


def dot_trans(left, right):
    return lax.dot_general(left, right, (((1,), (1,)), ((), ())), preferred_element_type=F32)


def swapped(array, axis, bit):
    return lax.ppermute(array, axis, [(i, i ^ bit) for i in range(lax.axis_size(axis))])


def left_lanes(shape):
    return lax.broadcasted_iota(jnp.int32, shape, 1) < shape[1] // 2


def turn(values):
    return pltpu.roll(values, values.shape[1] // 2, 1)


def split_pairs(rows, block):
    parts = rows.reshape(-1, 2, block, rows.shape[-1])
    return parts[:, 0].reshape(-1, rows.shape[-1]), parts[:, 1].reshape(-1, rows.shape[-1])


def join_pairs(even, odd, block):
    width = even.shape[-1]
    both = jnp.concatenate([even.reshape(-1, 1, block, width), odd.reshape(-1, 1, block, width)], axis=1)
    return both.reshape(-1, width)


def padded(weight):
    none = jnp.zeros_like(weight)
    return jnp.concatenate([weight, none], axis=0), jnp.concatenate([none, weight], axis=0)


def call(kernel, name, limit, flops, moved, **more):
    return pl.pallas_call(
        kernel,
        compiler_params=pltpu.CompilerParams(vmem_limit_bytes=limit),
        cost_estimate=pl.CostEstimate(flops=flops, bytes_accessed=moved, transcendentals=0),
        name=name,
        **more,
    )


def down_kernel(block, x_ref, wt_ref, pre_ref, trip_ref):
    left, right = padded(wt_ref[...])
    even, odd = split_pairs(x_ref[...], block)
    pre = dot_trans(even, left) + dot_trans(odd, right)
    pre_ref[...] = pre
    trip_ref[...] = (pre * (0.5 * jnp.tanh(0.5 * pre) + 0.5)).astype(BF16)


def down(x, wt, block):
    rows, width = x.shape
    lanes = 2 * wt.shape[0]
    return call(
        functools.partial(down_kernel, block),
        "down",
        8 * MIB,
        2 * rows * width * lanes,
        2 * rows * width,
        in_specs=[VMEM] * 2,
        out_specs=[VMEM] * 2,
        out_shape=[
            jax.ShapeDtypeStruct((rows // 2, lanes), F32),
            jax.ShapeDtypeStruct((rows // 2, lanes), BF16),
        ],
    )(x, wt)


def ahead_kernel(block, slots, angle_ref, row_ref, *refs):
    in_ref, out_ref, spot_ref, token_ref, rows_ref, pair_ref = refs[-6:]
    lanes = 2 * block
    half = block // 2
    mask = left_lanes((half, lanes))
    token_ref[...] = jnp.zeros(token_ref.shape, BF16)

    def pair(m, carry):
        for k in range(2):
            wide = angle_ref[2 * m + k].astype(F32)
            for t in range(half):
                rows_ref[k, t * slots : (t + 1) * slots, :] = wide[:, t * lanes : (t + 1) * lanes]
            for s in range(0, slots, 2):
                first = rows_ref[k, pl.ds(s, half, stride=slots), :]
                second = rows_ref[k, pl.ds(s + 1, half, stride=slots), :]
                pair_ref[k, s // 2, pl.ds(0, half, stride=2), :] = jnp.where(mask, first, turn(second))
                pair_ref[k, s // 2, pl.ds(1, half, stride=2), :] = jnp.where(mask, turn(first), second)
        for p in range(slots // 2):
            first, second = pair_ref[0, p], pair_ref[1, p]
            in_ref[2 * m, :, p * lanes : (p + 1) * lanes] = first.astype(BF16)
            in_ref[2 * m + 1, :, p * lanes : (p + 1) * lanes] = second.astype(BF16)
            both = jnp.concatenate([first, second], axis=0)
            out_ref[m, p * lanes : (p + 1) * lanes, :] = both.T.astype(BF16)
        return carry

    lax.fori_loop(0, angle_ref.shape[0] // 2, pair, 0, unroll=2)
    row = row_ref[...]
    packed_rows = spot_ref.shape[0]
    row = jnp.where(row < packed_rows, row, row - packed_rows)
    tile = packed_rows // 8
    for start in range(0, packed_rows, tile):
        spot = lax.broadcasted_iota(jnp.int32, (tile, row.shape[1]), 0) + start
        spot_ref[start : start + tile, :] = (spot == row).astype(F32).astype(BF16)


def ahead(angular, row, after, block):
    blocks, slots, _ = angular.shape
    edges = row.shape[1]
    lanes = 2 * block
    return call(
        functools.partial(ahead_kernel, block, slots),
        "ahead",
        4 * MIB,
        0,
        8 * angular.size * 2,
        in_specs=[VMEM, VMEM] + [ANY] * len(after),
        out_specs=[VMEM] * 4,
        out_shape=[
            jax.ShapeDtypeStruct((blocks, block, slots * block), BF16),
            jax.ShapeDtypeStruct((blocks // 2, slots * block, lanes), BF16),
            jax.ShapeDtypeStruct((edges // 2, edges), BF16),
            jax.ShapeDtypeStruct((16, lanes), BF16),
        ],
        scratch_shapes=[
            pltpu.VMEM((2, slots * block // 2, lanes), F32),
            pltpu.VMEM((2, slots // 2, block, lanes), F32),
        ],
    )(angular, row, *after)


def triplet_kernel(block, slots, pieces, parts, *refs):
    index_ref, spot_ref, place_ref, angle_ref = refs[:4]
    piece_refs = refs[4 : 4 + pieces]
    trip_ref = refs[5 + pieces]
    sent_refs = refs[6 + pieces : 6 + pieces + len(parts)]
    held_ref = refs[-1]
    packed_rows, lanes = trip_ref.shape
    groups = packed_rows // block
    mask = left_lanes((block, lanes))

    for piece in range(pieces):
        rows = piece_refs[piece][...]
        held_ref[piece * groups : (piece + 1) * groups] = rows.reshape(groups, block, lanes)
        rows = turn(rows.astype(F32)).astype(BF16)
        at = (pieces + piece) * groups
        held_ref[at : at + groups] = rows.reshape(groups, block, lanes)
    held_ref[2 * pieces * groups] = jnp.zeros((block, lanes), BF16)

    def target(q, carry):
        sides = []
        for pair in range(2):
            base = (4 * q + 2 * pair) * slots
            picked = [
                jnp.where(mask, held_ref[index_ref[base + s]], held_ref[index_ref[base + slots + s]])
                for s in range(slots)
            ]
            sides.append(jnp.concatenate(picked, axis=0))
        matrix = angle_ref[pl.ds(4 * q, 4)].reshape(4 * block, slots * block)
        every = dot(matrix, jnp.concatenate(sides, axis=1))
        for pair in range(2):
            part = every[pair * 2 * block : (pair + 1) * 2 * block, pair * lanes : (pair + 1) * lanes]
            total = jnp.where(mask, part[:block], part[block:]).astype(BF16)
            trip_ref[pl.ds(pl.multiple_of((2 * q + pair) * block, block), block), :] = total
        return carry

    lax.fori_loop(0, groups // 2, target, 0, unroll=2)

    place = place_ref[...].T
    turned_half = place >= packed_rows
    spread = []
    wide_mask = left_lanes((2 * block, lanes))
    for m in range(groups):
        rows = trip_ref[m * block : (m + 1) * block, :].astype(F32)
        other = turn(rows)
        both = jnp.concatenate([jnp.where(mask, rows, other), jnp.where(mask, other, rows)], axis=0)
        side = jnp.where(place[:, m : m + 1] < packed_rows, 1.0, 0.0)
        lane_side = jnp.where(wide_mask, 1.0, 0.0)
        spread.append(jnp.where(side == lane_side, both, 0.0).astype(BF16))
    spread = jnp.concatenate(spread, axis=0)
    first = 0
    for part, sent_ref in zip(parts, sent_refs):
        rows = slice(first * block, (first + part) * block)
        sent_ref[...] = dot(spot_ref[rows, :], spread).astype(BF16)
        first += part


def triplet(index, spot, place, angles, pieces, after, block, slots, parts):
    packed_rows, lanes = pieces[0].shape
    held = packed_rows // block * 2 * len(pieces) + 1
    return call(
        functools.partial(triplet_kernel, block, slots, len(pieces), parts),
        "triplet",
        6 * MIB + 2 * held * block * lanes,
        2 * packed_rows * slots * block * lanes,
        8 * MIB,
        in_specs=[SMEM] + [VMEM] * (3 + len(pieces)) + [ANY],
        out_specs=[VMEM] * (1 + len(parts)),
        out_shape=[jax.ShapeDtypeStruct((packed_rows, lanes), BF16)]
        + [jax.ShapeDtypeStruct((part * block, lanes), BF16) for part in parts],
        scratch_shapes=[pltpu.VMEM((held, block, lanes), BF16)],
    )(index, spot, place, angles, *pieces, after)


def gated(half_pre):
    lifted = 1.0 + jnp.tanh(half_pre)
    value = half_pre * lifted
    return value, lifted + value * (2.0 - lifted)


def pre_up(rows, up, block):
    up2 = jnp.concatenate([up, up], axis=0)
    mask = left_lanes(rows.shape)
    none = jnp.zeros(rows.shape, BF16)
    return dot(join_pairs(jnp.where(mask, rows, none), jnp.where(mask, none, rows), block), up2)


def project(rows, up, block):
    both = dot_trans(rows.astype(BF16), jnp.concatenate([up, up], axis=0))
    even, odd = split_pairs(both, block)
    return jnp.where(left_lanes(even.shape), even, odd)


def gate_kernel(block, tile, x_ref, own_ref, up_ref, base_ref, slope_ref):
    up = up_ref[...] * 0.5
    for start in range(0, x_ref.shape[0], tile):
        rows = own_ref[start // 2 : (start + tile) // 2, :]
        value, slope = gated(pre_up(rows, up, block))
        wide = slice(start, start + tile)
        base_ref[wide, :] = x_ref[wide, :].astype(F32) * ROOT_HALF + value * 0.5
        slope_ref[wide, :] = slope.astype(BF16)


def gate(x, own, up, block):
    rows, width = x.shape
    return call(
        functools.partial(gate_kernel, block, 8 * block),
        "gate",
        8 * MIB,
        2 * rows * width * own.shape[1],
        8 * rows * width,
        in_specs=[VMEM] * 3,
        out_specs=[VMEM] * 2,
        out_shape=[
            jax.ShapeDtypeStruct((rows, width), F32),
            jax.ShapeDtypeStruct((rows, width), BF16),
        ],
    )(x, own, up)


def layer_kernel(block, first, far_first, base_ref, ct_ref, far_ref, up_ref, wi_ref, wo_ref, *refs):
    out_ref, grad_ref, send_ref, held_ref, sem = refs[-5:]
    rows = grad_ref.shape[0]
    wide = slice(first * 2 * block, first * 2 * block + rows)
    up = up_ref[...] * 0.5
    far = far_ref[far_first * block : far_first * block + rows // 2, :]
    far_value, far_slope = gated(pre_up(far, up, block))
    hidden = base_ref[wide, :] + far_value * 0.5
    wi, wo = wi_ref[...] * 0.5, wo_ref[...] * 0.5
    in_value, in_slope = gated(dot(hidden.astype(BF16), wi))
    out_value, out_slope = gated(dot(in_value.astype(BF16), wo))
    held_ref[...] = ((hidden + out_value) * ROOT_HALF).astype(BF16)
    copy = pltpu.make_async_copy(held_ref, out_ref.at[wide, :], sem)
    copy.start()
    scaled = ct_ref[wide, :].astype(F32) * (0.5 * ROOT_HALF)
    grad_out = (scaled * out_slope).astype(BF16)
    grad_in = (dot_trans(grad_out, wo) * in_slope).astype(BF16)
    half_grad = scaled + dot_trans(grad_in, wi)
    grad_ref[...] = (half_grad * (2.0 * ROOT_HALF)).astype(BF16)
    send_ref[...] = project(half_grad * far_slope, up, block).astype(BF16)
    copy.wait()


def layer(base, ct, far, up, wi, wo, before, block, first, part, far_first):
    rows, width = base.shape
    lanes = far.shape[1]
    return call(
        functools.partial(layer_kernel, block, first, far_first),
        "layer",
        32 * MIB,
        0,
        0,
        in_specs=[VMEM] * 6 + [HBM] * len(before),
        out_specs=[HBM, VMEM, VMEM],
        out_shape=[
            jax.ShapeDtypeStruct((rows, width), BF16),
            jax.ShapeDtypeStruct((part * 2 * block, width), BF16),
            jax.ShapeDtypeStruct((part * block, lanes), BF16),
        ],
        scratch_shapes=[pltpu.VMEM((part * 2 * block, width), BF16), pltpu.SemaphoreType.DMA(())],
        input_output_aliases={6 + i: i for i in range(len(before))},
    )(base, ct, far, up, wi, wo, *before)


def near_kernel(block, slope_ref, up_ref, place_ref, *refs):
    near_ref, spot_ref = refs[-2:]
    packed_rows = near_ref.shape[0]
    place = place_ref[...].T
    tile = 2 * block
    for m in range(packed_rows // block):
        column = place[:, m : m + 1]
        column = jnp.where(column < packed_rows, column, column - packed_rows)
        spot = lax.broadcasted_iota(jnp.int32, (tile, packed_rows), 1)
        spot_ref[m * tile : (m + 1) * tile, :] = (spot == column).astype(F32).astype(BF16)
    up = up_ref[...] * 0.5
    first = 0
    for grad_ref in refs[:-2]:
        rows = grad_ref.shape[0]
        both = grad_ref[...].astype(F32) * slope_ref[first : first + rows, :].astype(F32)
        near_ref[first // 2 : (first + rows) // 2, :] = project(both, up, block) * ROOT_HALF
        first += rows


def near_part(slope, up, place, grads, block):
    rows, width = slope.shape
    lanes = 2 * up.shape[0]
    return call(
        functools.partial(near_kernel, block),
        "near",
        8 * MIB,
        2 * rows * width * lanes,
        4 * rows * width,
        in_specs=[VMEM] * (3 + len(grads)),
        out_specs=[VMEM] * 2,
        out_shape=[
            jax.ShapeDtypeStruct((rows // 2, lanes), F32),
            jax.ShapeDtypeStruct((rows, rows // 2), BF16),
        ],
    )(slope, up, place, *grads)


def scatter_kernel(block, slots, pieces, chunks, index_ref, place_ref, spot_ref, angle_ref, near_ref, *refs):
    far_refs = refs[:chunks]
    out_refs = refs[chunks : chunks + pieces]
    total_ref, grad_ref = refs[chunks + pieces :]
    packed_rows, lanes = grad_ref.shape
    groups = packed_rows // block
    mask = left_lanes((block, lanes))
    total_ref[...] = jnp.zeros(total_ref.shape, F32)
    place = place_ref[...].T
    tile = 2 * block
    wide_mask = left_lanes((tile, lanes))
    lane_side = jnp.where(wide_mask, 1.0, 0.0)
    far = jnp.concatenate([far_ref[...] for far_ref in far_refs], axis=0)
    several = 4
    for start in range(0, groups, several):
        got = dot(spot_ref[start * tile : (start + several) * tile, :], far)
        for i, m in enumerate(range(start, start + several)):
            side = jnp.where(place[:, m : m + 1] < packed_rows, 1.0, 0.0)
            mine = jnp.where(side == lane_side, got[i * tile : (i + 1) * tile], 0.0)
            mine = mine + turn(mine)
            at = m * block
            both = near_ref[at : at + block, :] + jnp.where(mask, mine[:block], mine[block:])
            grad_ref[at : at + block, :] = both.astype(BF16)
    none = jnp.zeros((block, lanes), BF16)

    def target(m, carry):
        rows = grad_ref[pl.ds(pl.multiple_of(m * block, block), block), :]
        pair = jnp.concatenate([jnp.where(mask, rows, none), jnp.where(mask, none, rows)], axis=0)
        terms = dot(angle_ref[m], pair)
        base = m * (2 * slots)
        for s in range(slots):
            term = terms[s * block : (s + 1) * block]
            total_ref[index_ref[base + s]] += jnp.where(mask, term, 0.0)
            total_ref[index_ref[base + slots + s]] += jnp.where(mask, 0.0, term)
        return carry

    lax.fori_loop(0, groups, target, 0, unroll=4)

    for piece in range(pieces):
        at = piece * groups
        straight = total_ref[at : at + groups].reshape(packed_rows, lanes)
        at += pieces * groups
        crossed = total_ref[at : at + groups].reshape(packed_rows, lanes)
        out_refs[piece][...] = (straight + turn(crossed)).astype(out_refs[piece].dtype)


def scatter(index, place, spot, angles, near, far, types, block, slots):
    chunks = len(far)
    packed_rows, lanes = near.shape
    pieces = len(types)
    held = 2 * pieces * (packed_rows // block) + 1
    return call(
        functools.partial(scatter_kernel, block, slots, pieces, chunks),
        "scatter",
        16 * MIB + 4 * held * block * lanes,
        2 * packed_rows * slots * block * lanes,
        8 * MIB,
        in_specs=[SMEM] + [VMEM] * (4 + chunks),
        out_specs=[VMEM] * pieces,
        out_shape=[jax.ShapeDtypeStruct((packed_rows, lanes), kind) for kind in types],
        scratch_shapes=[
            pltpu.VMEM((held, block, lanes), F32),
            pltpu.VMEM((packed_rows, lanes), BF16),
        ],
    )(index, place, spot, angles, near, *far)


def last_kernel(block, grads, pre_ref, wt_ref, *refs):
    grad_refs, term_refs = refs[:grads], refs[grads:-3]
    out_ref, held_ref, sems = refs[-3:]
    left, right = padded(wt_ref[...])
    first = 0
    copies = []
    for i, grad_ref in enumerate(grad_refs):
        rows = grad_ref.shape[0]
        thin = slice(first // 2, (first + rows) // 2)
        wide = slice(first, first + rows)
        total = term_refs[0][thin, :].astype(F32)
        for ref in term_refs[1:]:
            total = total + ref[thin, :].astype(F32)
        _, slope = gated(pre_ref[thin, :] * 0.5)
        grad = (total * (0.5 * slope)).astype(BF16)
        both = join_pairs(dot(grad, left), dot(grad, right), block)
        held_ref[wide, :] = (grad_ref[...].astype(F32) + both).astype(BF16)
        copies.append(pltpu.make_async_copy(held_ref.at[wide, :], out_ref.at[wide, :], sems.at[i]))
        copies[-1].start()
        first += rows
    for copy in copies:
        copy.wait()


def last(pre, grads, wt, terms, block):
    rows, width = 2 * pre.shape[0], wt.shape[1]
    return call(
        functools.partial(last_kernel, block, len(grads)),
        "last",
        8 * MIB,
        2 * rows * width * pre.shape[1],
        4 * rows * width,
        in_specs=[VMEM] * (2 + len(grads) + len(terms)),
        out_specs=HBM,
        out_shape=jax.ShapeDtypeStruct((rows, width), BF16),
        scratch_shapes=[pltpu.VMEM((rows, width), BF16), pltpu.SemaphoreType.DMA((len(grads),))],
    )(pre, wt, *grads, *terms)


def on_device(
    edge_feats,
    cotangent,
    down_weight,
    up_weight,
    inner_weight,
    outer_weight,
    angular,
    reverse,
    sources,
    counts,
):
    lane_count = lax.axis_size("narrow")
    top_bit = lax.axis_size("cluster") // 2
    me = lax.axis_index("narrow")
    local_blocks, slots = sources.shape
    local_edges = edge_feats.shape[0]
    block = local_edges // local_blocks
    groups = local_blocks // 2
    packed_rows = local_edges // 2
    down_trans = down_weight.T

    live = lax.broadcasted_iota(jnp.int32, sources.shape, 1) < counts[:, None]
    local = sources % (local_blocks * lane_count)
    spot = (local // local_blocks ^ me) * local_blocks + local % local_blocks
    odd = lax.broadcasted_iota(jnp.int32, sources.shape, 0) % 2
    turned = jnp.where(spot % 2 == odd, 0, lane_count * groups)
    index = jnp.where(live, turned + spot // 2, 2 * lane_count * groups).reshape(-1)

    slot = reverse % local_edges
    place = (slot // block % 2) * packed_rows + slot // (2 * block) * block + slot % block
    place_row = place.reshape(1, local_edges)
    place = place.reshape(groups, 2 * block)

    pre_down, trip = down(edge_feats, down_trans, block)
    angle_in, angle_out, spot, token = ahead(angular, place_row, [trip, index, place], block)
    pieces = {0: trip}
    bits = [1 << i for i in range(lane_count.bit_length() - 1)]
    for bit in reversed(bits):
        if bit == 1:
            last_piece = lane_count - 2
            pieces[last_piece], token = lax.optimization_barrier((pieces[last_piece], token))
        pieces.update({d ^ bit: swapped(piece, "narrow", bit) for d, piece in pieces.items()})
    pieces = [pieces[d] for d in range(lane_count)]
    cuts = [0, groups * 7 // 16, groups * 12 // 16, groups]
    parts = [end - start for start, end in zip(cuts, cuts[1:])]
    sizes = [parts[0], groups - parts[0]]
    trip_own, early, late = triplet(index, spot, place, angle_in, pieces, token, block, slots, sizes)
    early = swapped(early, "cluster", top_bit)
    base, slope = gate(edge_feats, trip_own, up_weight, block)
    early, late = lax.optimization_barrier((early, late))
    late = swapped(late, "cluster", top_bit)
    done, grads, far = [], [], []
    for first, part in zip(cuts, parts):
        output, grad, sent = layer(
            base,
            cotangent,
            late if first else early,
            up_weight,
            inner_weight[0],
            outer_weight[0],
            done,
            block,
            first,
            part,
            first - parts[0] if first else 0,
        )
        done = [output]
        grads.append(grad)
        far.append(swapped(sent, "cluster", top_bit))
    near, spot = near_part(slope, up_weight, place, grads, block)
    types = [BF16 if d % 2 else F32 for d in range(lane_count)]
    sums = dict(enumerate(scatter(index, place, spot, angle_out, near, far, types, block, slots)))
    terms = [sums[0]]
    for bit in bits:
        for d in range(lane_count - bit, -1, -2 * bit):
            got = swapped(sums[d].astype(BF16), "narrow", bit)
            if d == bit:
                terms.append(got)
            else:
                sums[d ^ bit] = sums[d ^ bit] + got.astype(F32)
    grad_x = last(pre_down, grads, down_trans, terms, block)
    return (output, grad_x)


def solution(mesh):
    in_specs = (
        P(("cluster", "narrow"), None),
        P(("cluster", "narrow"), None),
        P(),
        P(),
        P(),
        P(),
        P(("cluster", "narrow"), None, None),
        P(("cluster", "narrow")),
        P(("cluster", "narrow"), None),
        P(("cluster", "narrow")),
    )
    out_specs = (P(("cluster", "narrow"), None), P(("cluster", "narrow"), None))
    return jax.shard_map(
        on_device, mesh=mesh, in_specs=in_specs, out_specs=out_specs, check_vma=False
    )
```

time: 77.8 us -> 65.4 us (0.84)
  waiting for transfers between devices: 35.5 us -> 20.5 us
  starting transfers between devices: 11 us -> 14.2 us
    ppermute x10 -> x11, waiting for transfers between devices: 35.5 us -> 20.5 us  [swapped(): lax.ppermute(array, axis, [(i, i ^ bit) for i in range(lax.axis_size(axis...]
    ppermute x10 -> x11, starting transfers between devices: 11 us -> 14.2 us  [swapped(): lax.ppermute(array, axis, [(i, i ^ bit) for i in range(lax.axis_size(axis...]
    pallas_call x5 -> x8, Pallas kernels: 20.9 us -> 21.1 us  [the longest x3 8.2 us: layer(): call(functools.partial(layer_kernel, block, first, far_first), 'layer', 3...]
  transfers between devices with their start and end apart: 10 -> 11, of which waited for: 6 -> 7; matrix products, arithmetic and copies ran while one was open for 0% -> 0% of each run, Pallas kernels for 11% -> 24%
where the time goes in v3:
time: 65.4 us; the launch traced here: 65.2 us
  Pallas kernels  26.8 us (41%)
  waiting for transfers between devices  20.5 us (31%)
  starting transfers between devices  14.2 us (22%)
  local copies, waits for them, and re-layouts  2.64 us (4%)
  between operations  1.01 us (2%)
    ppermute x11, waiting for transfers between devices, swapped(): lax.ppermute(array, axis, [(i, i ^ bit) for i in range(lax.axis_size(axis...  20.5 us
    ppermute x11, starting transfers between devices, swapped(): lax.ppermute(array, axis, [(i, i ^ bit) for i in range(lax.axis_size(axis...  14.2 us
    pallas_call x3, Pallas kernels, layer(): call(functools.partial(layer_kernel, block, first, far_first), 'layer', 3...  8.2 us
    pallas_call x1, Pallas kernels, scatter(): call(functools.partial(scatter_kernel, block, slots, pieces, chunks), 'sc...  5.03 us
    pallas_call x1, Pallas kernels, triplet(): call(functools.partial(triplet_kernel, block, slots, len(pieces), parts),...  3.88 us
    pallas_call x1, Pallas kernels, ahead(): call(functools.partial(ahead_kernel, block, slots), 'ahead', 4 * MIB, 0,...  3.6 us
    unnamed x24, local copies, waits for them, and re-layouts  2.47 us
    pallas_call x1, Pallas kernels, near_part(): call(functools.partial(near_kernel, block), 'near', 8 * MIB, 2 * rows * w...  1.82 us
  transfers between devices with their start and end apart: 11, of which 7 were waited for; matrix products, arithmetic and copies ran while one was open for 0% of the time, Pallas kernels for 24%

profile of v3, /device:TPU:0, one launch (start us, length us, event | category | flops | bytes accessed | tf_op | source)
XLA Modules:
  0.0 65.2 jit_solution(15822066224261211281)
XLA Ops:
  0.6 0.0 copy-start.11
  0.6 0.0 copy-start.1
  0.7 1.6 %copy-done.1 = bf16[2048,512]{1,0:T(8,128)(2,1)S(1)} copy-done((bf16[2048,512]{1,0:T(8,128)(2,1)S(1)}, bf16[2048,512]{1,0:T(8,128)(2,1)}, u32[]{:S(2)}) %copy-start.1) | copy-done | bytes 2097176
  2.2 0.8 %copy-done.7 = bf16[512,64]{0,1:T(8,128)(2,1)S(1)} copy-done((bf16[512,64]{0,1:T(8,128)(2,1)S(1)}, bf16[512,64]{0,1:T(8,128)(2,1)}, u32[]{:S(2)}) %copy-start.7) | copy-done | bytes 65560
  3.1 0.7 %down.1 = (f32[1024,128]{1,0:T(8,128)S(1)}, bf16[1024,128]{1,0:T(8,128)(2,1)S(1)}) custom-call(bf16[2048,512]{1,0:T(8,128)(2,1)S(1)} %copy-done.1, bf16[64,512]{1,0:T(8,128)(2,1)S(1)} %bitcast.12), custom_call_target="tpu_custom_call" | custom-call | flops 268435456 | bytes 2097152 | tf_op jit(solution)/shard_map/down/pallas_call | solution.py:77
  3.8 3.0 %collective-permute-start.1 = (bf16[1024,128]{1,0:T(8,128)(2,1)S(1)}, bf16[1024,128]{1,0:T(8,128)(2,1)S(1)}, u32[]{:S(2)}, u32[]{:S(2)}) collective-permute-start(bf16[1024,128]{1,0:T(8,128)(2,1)S(1)} %get-tuple-element.32.refs_0_.refs_4_), channel_id=1, source_target_pairs={{0,2},{1,3},{2,0},{3,1},{4,6},{5,7},{6,4},{7,5},{8,10},{9,11},{10,... | collective-permute-start | bytes 786440 | tf_op jit(solution)/shard_map/ppermute | solution.py:29
  6.8 0.0 collective-permute-start
  6.8 0.0 copy-done.9
  6.9 0.0 copy-done.11
  6.9 0.0 copy-done.10
  6.9 0.1 copy.14
  7.0 0.1 reshape.14.refs_1_.refs_0_.index_ref
  7.1 0.0 copy-done.5
  7.1 3.6 %ahead.1 = (bf16[32,64,512]{2,1,0:T(8,128)(2,1)S(1)}, bf16[16,512,128]{2,1,0:T(8,128)(2,1)S(1)}, bf16[1024,2048]{1,0:T(8,128)(2,1)S(1)}, bf16[16,128]{1,0:T(8,128)(2,1)S(1)}) custom-call(bf16[32,8,4096]{2,1,0:T(8,128)(2,1)S(1)} %copy-done.5, s32[1,2048]{1,0:T(1,128)S(1)} %bitcast.14, bf16[1024,128]{1,0:T(8,128)(2,1)S(1)} %get-tuple-element.32.refs_0_.refs_4_, ...), custom_call_target="tpu_custom_call" | custom-call | bytes 16777216 | tf_op jit(solution)/shard_map/ahead/pallas_call | solution.py:131
  10.8 2.4 %collective-permute-done.1.refs_6_ = bf16[1024,128]{1,0:T(8,128)(2,1)S(1)} collective-permute-done((bf16[1024,128]{1,0:T(8,128)(2,1)S(1)}, bf16[1024,128]{1,0:T(8,128)(2,1)S(1)}, u32[]{:S(2)}, u32[]{:S(2)}) %collective-permute-start.1) | collective-permute-done | bytes 262176 | tf_op jit(solution)/shard_map/ppermute | solution.py:29
  13.1 0.0 collective-permute-start.2
  13.1 0.0 collective-permute-done.refs_5_
  13.1 1.5 %collective-permute-done.2.refs_7_ = bf16[1024,128]{1,0:T(8,128)(2,1)S(1)} collective-permute-done((bf16[1024,128]{1,0:T(8,128)(2,1)S(1)}, bf16[1024,128]{1,0:T(8,128)(2,1)S(1)}, u32[]{:S(2)}, u32[]{:S(2)}) %collective-permute-start.2) | collective-permute-done | bytes 262176 | tf_op jit(solution)/shard_map/ppermute | solution.py:29
  14.7 3.9 %triplet.1 = (bf16[1024,128]{1,0:T(8,128)(2,1)S(1)}, bf16[448,128]{1,0:T(8,128)(2,1)S(1)}, bf16[576,128]{1,0:T(8,128)(2,1)S(1)}) custom-call(s32[256]{0:T(256)S(1)} %reshape.14.refs_1_.refs_0_.index_ref, bf16[1024,2048]{1,0:T(8,128)(2,1)S(1)} %get-tuple-element.33.refs_1_, s32[16,128]{1,0:T(8,128)S(1)} %fusion.24.refs_2_.place_ref, ...), custom_call_target="tpu_custom_call" | custom-call | flops 134217728 | bytes 8388608 | tf_op jit(solution)/shard_map/triplet/pallas_call | solution.py:211
  18.6 0.0 copy-start
  18.6 2.9 %collective-permute-start.3 = (bf16[448,128]{1,0:T(8,128)(2,1)S(1)}, bf16[448,128]{1,0:T(8,128)(2,1)S(1)}, u32[]{:S(2)}, u32[]{:S(2)}) collective-permute-start(bf16[448,128]{1,0:T(8,128)(2,1)S(1)} %get-tuple-element.40), channel_id=1, source_target_pairs={{0,16},{4,20},{8,24},{12,28},{16,0},{20,4},{24,8},{28,12},{1,17},{... | collective-permute-start | bytes 344072 | tf_op jit(solution)/shard_map/ppermute | solution.py:29
  21.4 5.9 %collective-permute-done.3.far_ref = bf16[448,128]{1,0:T(8,128)(2,1)S(1)} collective-permute-done((bf16[448,128]{1,0:T(8,128)(2,1)S(1)}, bf16[448,128]{1,0:T(8,128)(2,1)S(1)}, u32[]{:S(2)}, u32[]{:S(2)}) %collective-permute-start.3) | collective-permute-done | bytes 114720 | tf_op jit(solution)/shard_map/ppermute | solution.py:29
  27.3 0.3 collective-permute-start.4
  27.6 0.0 copy-done.2
  27.6 0.0 copy-done.6
  27.6 1.8 %gate.1 = (f32[2048,512]{1,0:T(8,128)S(1)}, bf16[2048,512]{1,0:T(8,128)(2,1)S(1)}) custom-call(bf16[2048,512]{1,0:T(8,128)(2,1)S(1)} %copy-done.2, bf16[1024,128]{1,0:T(8,128)(2,1)S(1)} %get-tuple-element.38.own_ref, bf16[64,512]{1,0:T(8,128)(2,1)S(1)} %copy-done.6), custom_call_target="tpu_custom_call" | custom-call | flops 268435456 | bytes 8388608 | tf_op jit(solution)/shard_map/gate/pallas_call | solution.py:256
  29.4 0.0 copy-done.3
  29.4 0.0 copy-done.4
  29.5 3.5 %layer.3 = (bf16[2048,512]{1,0:T(8,128)(2,1)}, bf16[896,512]{1,0:T(8,128)(2,1)S(1)}, bf16[448,128]{1,0:T(8,128)(2,1)S(1)}) custom-call(f32[2048,512]{1,0:T(8,128)S(1)} %get-tuple-element.39.base_ref, bf16[2048,512]{1,0:T(8,128)(2,1)S(1)} %copy-done, bf16[448,128]{1,0:T(8,128)(2,1)S(1)} %collective-permute-done.3.far_ref, bf16[64,512]{1,0:T(8,128)(2,1)S(1)} %copy-done.6, ...), custom_call_target="tpu_custom_call" | custom-call | tf_op jit(solution)/shard_map/layer/pallas_call | solution.py:297
  33.0 2.7 %collective-permute-start.5 = (bf16[448,128]{1,0:T(8,128)(2,1)S(1)}, bf16[448,128]{1,0:T(8,128)(2,1)S(1)}, u32[]{:S(2)}, u32[]{:S(2)}) collective-permute-start(bf16[448,128]{1,0:T(8,128)(2,1)S(1)} %get-tuple-element.55), channel_id=1, source_target_pairs={{0,16},{4,20},{8,24},{12,28},{16,0},{20,4},{24,8},{28,12},{1,17},{... | collective-permute-start | bytes 344072 | tf_op jit(solution)/shard_map/ppermute | solution.py:29
  35.7 1.8 %collective-permute-done.4.far_ref = bf16[576,128]{1,0:T(8,128)(2,1)S(1)} collective-permute-done((bf16[576,128]{1,0:T(8,128)(2,1)S(1)}, bf16[576,128]{1,0:T(8,128)(2,1)S(1)}, u32[]{:S(2)}, u32[]{:S(2)}) %collective-permute-start.4) | collective-permute-done | bytes 147488 | tf_op jit(solution)/shard_map/ppermute | solution.py:29
  37.5 2.6 %layer.4 = (bf16[2048,512]{1,0:T(8,128)(2,1)}, bf16[640,512]{1,0:T(8,128)(2,1)S(1)}, bf16[320,128]{1,0:T(8,128)(2,1)S(1)}) custom-call(f32[2048,512]{1,0:T(8,128)S(1)} %get-tuple-element.39.base_ref, bf16[2048,512]{1,0:T(8,128)(2,1)S(1)} %copy-done, bf16[576,128]{1,0:T(8,128)(2,1)S(1)} %collective-permute-done.4.far_ref, ...), custom_call_target="tpu_custom_call", output_to_operand_aliasing={{0}: (6, {})} | custom-call | tf_op jit(solution)/shard_map/layer/pallas_call | solution.py:297
  40.1 0.1 collective-permute-start.6
  40.2 2.1 %layer.5 = (bf16[2048,512]{1,0:T(8,128)(2,1)}, bf16[512,512]{1,0:T(8,128)(2,1)S(1)}, bf16[256,128]{1,0:T(8,128)(2,1)S(1)}) custom-call(f32[2048,512]{1,0:T(8,128)S(1)} %get-tuple-element.39.base_ref, bf16[2048,512]{1,0:T(8,128)(2,1)S(1)} %copy-done, bf16[576,128]{1,0:T(8,128)(2,1)S(1)} %collective-permute-done.4.far_ref, ...), custom_call_target="tpu_custom_call", output_to_operand_aliasing={{0}: (6, {})} | custom-call | tf_op jit(solution)/shard_map/layer/pallas_call | solution.py:297
  42.3 3.0 %collective-permute-start.7 = (bf16[256,128]{1,0:T(8,128)(2,1)S(1)}, bf16[256,128]{1,0:T(8,128)(2,1)S(1)}, u32[]{:S(2)}, u32[]{:S(2)}) collective-permute-start(bf16[256,128]{1,0:T(8,128)(2,1)S(1)} %get-tuple-element.57), channel_id=1, source_target_pairs={{0,16},{4,20},{8,24},{12,28},{16,0},{20,4},{24,8},{28,12},{1,17},{... | collective-permute-start | bytes 196616 | tf_op jit(solution)/shard_map/ppermute | solution.py:29
  45.3 1.8 %near.1 = (f32[1024,128]{1,0:T(8,128)S(1)}, bf16[2048,1024]{1,0:T(8,128)(2,1)S(1)}) custom-call(bf16[2048,512]{1,0:T(8,128)(2,1)S(1)} %get-tuple-element.51.slope_ref, bf16[64,512]{1,0:T(8,128)(2,1)S(1)} %copy-done.6, s32[16,128]{1,0:T(8,128)S(1)} %fusion.24.refs_2_.place_ref, bf16[896,512]{1,0:T(8,128)(2,1)S(1)} %get-tuple-element.48.refs_0_, ...), custom_call_target="tpu_custom_call" | custom-call | flops 268435456 | bytes 4194304 | tf_op jit(solution)/shard_map/near/pallas_call | solution.py:337
  47.1 0.0 collective-permute-done.5.refs_0_
  47.1 1.0 %collective-permute-done.7.refs_2_ = bf16[256,128]{1,0:T(8,128)(2,1)S(1)} collective-permute-done((bf16[256,128]{1,0:T(8,128)(2,1)S(1)}, bf16[256,128]{1,0:T(8,128)(2,1)S(1)}, u32[]{:S(2)}, u32[]{:S(2)}) %collective-permute-start.7) | collective-permute-done | bytes 65568 | tf_op jit(solution)/shard_map/ppermute | solution.py:29
  48.2 0.0 collective-permute-done.6.refs_1_
  48.2 5.0 %scatter.1 = (f32[1024,128]{1,0:T(8,128)S(1)}, bf16[1024,128]{1,0:T(8,128)(2,1)S(1)}, f32[1024,128]{1,0:T(8,128)S(1)}, bf16[1024,128]{1,0:T(8,128)(2,1)S(1)}) custom-call(s32[256]{0:T(256)S(1)} %reshape.14.refs_1_.refs_0_.index_ref, s32[16,128]{1,0:T(8,128)S(1)} %fusion.24.refs_2_.place_ref, bf16[2048,1024]{1,0:T(8,128)(2,1)S(1)} %get-tuple-element.52.spot_ref, ...), custom_call_target="tpu_custom_call" | custom-call | flops 134217728 | bytes 8388608 | tf_op jit(solution)/shard_map/scatter/pallas_call | solution.py:403
  53.2 0.1 collective-permute-start.9
  53.3 0.5 collective-permute-start.8
  53.8 1.0 %collective-permute-done.9 = bf16[1024,128]{1,0:T(8,128)(2,1)S(1)} collective-permute-done((bf16[1024,128]{1,0:T(8,128)(2,1)S(1)}, bf16[1024,128]{1,0:T(8,128)(2,1)S(1)}, u32[]{:S(2)}, u32[]{:S(2)}) %collective-permute-start.9) | collective-permute-done | bytes 262176 | tf_op jit(solution)/shard_map/ppermute | solution.py:29
  54.8 0.1 add_convert_fusion
  54.9 1.6 %collective-permute-start.10 = (bf16[1024,128]{1,0:T(8,128)(2,1)S(1)}, bf16[1024,128]{1,0:T(8,128)(2,1)S(1)}, u32[]{:S(2)}, u32[]{:S(2)}) collective-permute-start(bf16[1024,128]{1,0:T(8,128)(2,1)S(1)} %add_convert_fusion), channel_id=1, source_target_pairs={{0,2},{1,3},{2,0},{3,1},{4,6},{5,7},{6,4},{7,5},{8,10},{9,11},{10,... | collective-permute-start | bytes 786440 | tf_op jit(solution)/shard_map/ppermute | solution.py:29
  56.5 0.0 collective-permute-done.8.refs_4_
  56.5 6.8 %collective-permute-done.10.refs_5_ = bf16[1024,128]{1,0:T(8,128)(2,1)S(1)} collective-permute-done((bf16[1024,128]{1,0:T(8,128)(2,1)S(1)}, bf16[1024,128]{1,0:T(8,128)(2,1)S(1)}, u32[]{:S(2)}, u32[]{:S(2)}) %collective-permute-start.10) | collective-permute-done | bytes 262176 | tf_op jit(solution)/shard_map/ppermute | solution.py:29
  63.3 1.8 %last.1 = bf16[2048,512]{1,0:T(8,128)(2,1)} custom-call(f32[1024,128]{1,0:T(8,128)S(1)} %get-tuple-element.47.pre_ref, bf16[64,512]{1,0:T(8,128)(2,1)S(1)} %bitcast.13, bf16[896,512]{1,0:T(8,128)(2,1)S(1)} %get-tuple-element.48.refs_0_, bf16[640,512]{1,0:T(8,128)(2,1)S(1)} %get-tuple-element.49.refs_1_, bf16[512,512]{1,0:T(8,128)(2,1)S(1)} %get-tuple-element.50.refs_2_, ...), custom_call_target="tpu_custom_call" | custom-call | flops 268435456 | bytes 4194304 | tf_op jit(solution)/shard_map/last/pallas_call | solution.py:445
  (16 shorter events, 0.1 us)
Async XLA Ops:
  0.6 6.3 %copy-start.11 = (s32[32]{0:T(128)S(1)}, s32[32]{0:T(128)}, u32[]{:S(2)}) copy-start(s32[32]{0:T(128)} %param.19) | copy-start | bytes 388
  0.6 1.6 %copy-start.1 = (bf16[2048,512]{1,0:T(8,128)(2,1)S(1)}, bf16[2048,512]{1,0:T(8,128)(2,1)}, u32[]{:S(2)}) copy-start(bf16[2048,512]{1,0:T(8,128)(2,1)} %x_ref.3) | copy-start | bytes 6291460
  2.2 0.8 %copy-start.7 = (bf16[512,64]{0,1:T(8,128)(2,1)S(1)}, bf16[512,64]{0,1:T(8,128)(2,1)}, u32[]{:S(2)}) copy-start(bf16[512,64]{0,1:T(8,128)(2,1)} %param.12) | copy-start | bytes 196612
  3.1 3.8 %copy-start.9 = (s32[2048]{0:T(1024)S(1)}, s32[2048]{0:T(1024)}, u32[]{:S(2)}) copy-start(s32[2048]{0:T(1024)} %param.17) | copy-start | bytes 24580
  3.1 3.8 %copy-start.10 = (s32[32,8]{0,1:T(8,128)S(1)}, s32[32,8]{0,1:T(8,128)}, u32[]{:S(2)}) copy-start(s32[32,8]{0,1:T(8,128)} %param.18) | copy-start | bytes 3076
  3.1 4.1 %copy-start.5 = (bf16[32,8,4096]{2,1,0:T(8,128)(2,1)S(1)}, bf16[32,8,4096]{2,1,0:T(8,128)(2,1)}, u32[]{:S(2)}) copy-start(bf16[32,8,4096]{2,1,0:T(8,128)(2,1)} %angle_ref.1) | copy-start | bytes 6291460
  3.8 9.3 %collective-permute-start.1 = (bf16[1024,128]{1,0:T(8,128)(2,1)S(1)}, bf16[1024,128]{1,0:T(8,128)(2,1)S(1)}, u32[]{:S(2)}, u32[]{:S(2)}) collective-permute-start(bf16[1024,128]{1,0:T(8,128)(2,1)S(1)} %get-tuple-element.32.refs_0_.refs_4_), channel_id=1, source_target_pairs={{0,2},{1,3},{2,0},{3,1},{4,6},{5,7},{6,4},{7,5},{8,10},{9,11},{10,... | collective-permute-start | bytes 786440 | tf_op jit(solution)/shard_map/ppermute | solution.py:29
  6.8 6.3 %collective-permute-start = (bf16[1024,128]{1,0:T(8,128)(2,1)S(1)}, bf16[1024,128]{1,0:T(8,128)(2,1)S(1)}, u32[]{:S(2)}, u32[]{:S(2)}) collective-permute-start(bf16[1024,128]{1,0:T(8,128)(2,1)S(1)} %get-tuple-element.32.refs_0_.refs_4_), channel_id=1, source_target_pairs={{0,1},{1,0},{2,3},{3,2},{4,5},{5,4},{6,7},{7,6},{8,9},{9,8},{10,11... | collective-permute-start | bytes 786440 | tf_op jit(solution)/shard_map/ppermute | solution.py:29
  13.1 1.5 %collective-permute-start.2 = (bf16[1024,128]{1,0:T(8,128)(2,1)S(1)}, bf16[1024,128]{1,0:T(8,128)(2,1)S(1)}, u32[]{:S(2)}, u32[]{:S(2)}) collective-permute-start(bf16[1024,128]{1,0:T(8,128)(2,1)S(1)} %collective-permute-done.1.refs_6_), channel_id=1, source_target_pairs={{0,1},{1,0},{2,3},{3,2},{4,5},{5,4},{6,7},{7,6},{8,9},{9,8},{10,11... | collective-permute-start | bytes 786440 | tf_op jit(solution)/shard_map/ppermute | solution.py:29
  14.7 13.0 %copy-start.2 = (bf16[2048,512]{1,0:T(8,128)(2,1)S(1)}, bf16[2048,512]{1,0:T(8,128)(2,1)}, u32[]{:S(2)}) copy-start(bf16[2048,512]{1,0:T(8,128)(2,1)} %x_ref.3) | copy-start | bytes 6291460
  14.7 13.0 %copy-start.6 = (bf16[64,512]{1,0:T(8,128)(2,1)S(1)}, bf16[64,512]{1,0:T(8,128)(2,1)}, u32[]{:S(2)}) copy-start(bf16[64,512]{1,0:T(8,128)(2,1)} %up_ref.9) | copy-start | bytes 196612
  14.7 14.8 %copy-start.3 = (bf16[1,512,512]{2,1,0:T(8,128)(2,1)S(1)}, bf16[1,512,512]{2,1,0:T(8,128)(2,1)}, u32[]{:S(2)}) copy-start(bf16[1,512,512]{2,1,0:T(8,128)(2,1)} %param.14) | copy-start | bytes 1572868
  14.7 14.8 %copy-start.4 = (bf16[1,512,512]{2,1,0:T(8,128)(2,1)S(1)}, bf16[1,512,512]{2,1,0:T(8,128)(2,1)}, u32[]{:S(2)}) copy-start(bf16[1,512,512]{2,1,0:T(8,128)(2,1)} %param.15) | copy-start | bytes 1572868
  18.6 10.9 %copy-start = (bf16[2048,512]{1,0:T(8,128)(2,1)S(1)}, bf16[2048,512]{1,0:T(8,128)(2,1)}, u32[]{:S(2)}) copy-start(bf16[2048,512]{1,0:T(8,128)(2,1)} %ct_ref.5) | copy-start | bytes 6291460
  18.6 8.8 %collective-permute-start.3 = (bf16[448,128]{1,0:T(8,128)(2,1)S(1)}, bf16[448,128]{1,0:T(8,128)(2,1)S(1)}, u32[]{:S(2)}, u32[]{:S(2)}) collective-permute-start(bf16[448,128]{1,0:T(8,128)(2,1)S(1)} %get-tuple-element.40), channel_id=1, source_target_pairs={{0,16},{4,20},{8,24},{12,28},{16,0},{20,4},{24,8},{28,12},{1,17},{... | collective-permute-start | bytes 344072 | tf_op jit(solution)/shard_map/ppermute | solution.py:29
  27.3 10.1 %collective-permute-start.4 = (bf16[576,128]{1,0:T(8,128)(2,1)S(1)}, bf16[576,128]{1,0:T(8,128)(2,1)S(1)}, u32[]{:S(2)}, u32[]{:S(2)}) collective-permute-start(bf16[576,128]{1,0:T(8,128)(2,1)S(1)} %get-tuple-element.42), channel_id=1, source_target_pairs={{0,16},{4,20},{8,24},{12,28},{16,0},{20,4},{24,8},{28,12},{1,17},{... | collective-permute-start | bytes 442376 | tf_op jit(solution)/shard_map/ppermute | solution.py:29
  33.0 14.1 %collective-permute-start.5 = (bf16[448,128]{1,0:T(8,128)(2,1)S(1)}, bf16[448,128]{1,0:T(8,128)(2,1)S(1)}, u32[]{:S(2)}, u32[]{:S(2)}) collective-permute-start(bf16[448,128]{1,0:T(8,128)(2,1)S(1)} %get-tuple-element.55), channel_id=1, source_target_pairs={{0,16},{4,20},{8,24},{12,28},{16,0},{20,4},{24,8},{28,12},{1,17},{... | collective-permute-start | bytes 344072 | tf_op jit(solution)/shard_map/ppermute | solution.py:29
  40.1 8.1 %collective-permute-start.6 = (bf16[320,128]{1,0:T(8,128)(2,1)S(1)}, bf16[320,128]{1,0:T(8,128)(2,1)S(1)}, u32[]{:S(2)}, u32[]{:S(2)}) collective-permute-start(bf16[320,128]{1,0:T(8,128)(2,1)S(1)} %get-tuple-element.56), channel_id=1, source_target_pairs={{0,16},{4,20},{8,24},{12,28},{16,0},{20,4},{24,8},{28,12},{1,17},{... | collective-permute-start | bytes 245768 | tf_op jit(solution)/shard_map/ppermute | solution.py:29
  42.3 5.9 %collective-permute-start.7 = (bf16[256,128]{1,0:T(8,128)(2,1)S(1)}, bf16[256,128]{1,0:T(8,128)(2,1)S(1)}, u32[]{:S(2)}, u32[]{:S(2)}) collective-permute-start(bf16[256,128]{1,0:T(8,128)(2,1)S(1)} %get-tuple-element.57), channel_id=1, source_target_pairs={{0,16},{4,20},{8,24},{12,28},{16,0},{20,4},{24,8},{28,12},{1,17},{... | collective-permute-start | bytes 196616 | tf_op jit(solution)/shard_map/ppermute | solution.py:29
  48.2 15.1 %copy-start.8 = (bf16[512,64]{0,1:T(8,128)(2,1)S(1)}, bf16[512,64]{0,1:T(8,128)(2,1)}, u32[]{:S(2)}) copy-start(bf16[512,64]{0,1:T(8,128)(2,1)} %param.12) | copy-start | bytes 196612
  53.2 1.6 %collective-permute-start.9 = (bf16[1024,128]{1,0:T(8,128)(2,1)S(1)}, bf16[1024,128]{1,0:T(8,128)(2,1)S(1)}, u32[]{:S(2)}, u32[]{:S(2)}) collective-permute-start(bf16[1024,128]{1,0:T(8,128)(2,1)S(1)} %get-tuple-element.61), channel_id=1, source_target_pairs={{0,1},{1,0},{2,3},{3,2},{4,5},{5,4},{6,7},{7,6},{8,9},{9,8},{10,11... | collective-permute-start | bytes 786440 | tf_op jit(solution)/shard_map/ppermute | solution.py:29
  53.3 3.2 %collective-permute-start.8 = (bf16[1024,128]{1,0:T(8,128)(2,1)S(1)}, bf16[1024,128]{1,0:T(8,128)(2,1)S(1)}, u32[]{:S(2)}, u32[]{:S(2)}) collective-permute-start(bf16[1024,128]{1,0:T(8,128)(2,1)S(1)} %get-tuple-element.59), channel_id=1, source_target_pairs={{0,1},{1,0},{2,3},{3,2},{4,5},{5,4},{6,7},{7,6},{8,9},{9,8},{10,11... | collective-permute-start | bytes 786440 | tf_op jit(solution)/shard_map/ppermute | solution.py:29
  54.9 8.4 %collective-permute-start.10 = (bf16[1024,128]{1,0:T(8,128)(2,1)S(1)}, bf16[1024,128]{1,0:T(8,128)(2,1)S(1)}, u32[]{:S(2)}, u32[]{:S(2)}) collective-permute-start(bf16[1024,128]{1,0:T(8,128)(2,1)S(1)} %add_convert_fusion), channel_id=1, source_target_pairs={{0,2},{1,3},{2,0},{3,1},{4,6},{5,7},{6,4},{7,5},{8,10},{9,11},{10,... | collective-permute-start | bytes 786440 | tf_op jit(solution)/shard_map/ppermute | solution.py:29

commit v4 on v3

--- a/solution.py
+++ b/solution.py
@@ -63,30 +63,44 @@
     )
 
 
-def down_kernel(block, x_ref, wt_ref, pre_ref, trip_ref):
-    left, right = padded(wt_ref[...])
-    even, odd = split_pairs(x_ref[...], block)
-    pre = dot_trans(even, left) + dot_trans(odd, right)
+def down_kernel(block, x_ref, wt_ref, pre_ref, *refs):
+    trip_refs, (x_held, wt_held, sems) = refs[:-3], refs[-3:]
+    copies = [
+        pltpu.make_async_copy(x_ref, x_held, sems.at[0]),
+        pltpu.make_async_copy(wt_ref, wt_held, sems.at[1]),
+    ]
+    for copy in copies:
+        copy.start()
+    for copy in copies:
+        copy.wait()
+    pre = project(x_held[...], wt_held[...], block)
     pre_ref[...] = pre
-    trip_ref[...] = (pre * (0.5 * jnp.tanh(0.5 * pre) + 0.5)).astype(BF16)
-
-
-def down(x, wt, block):
+    trip = (pre * (0.5 * jnp.tanh(0.5 * pre) + 0.5)).astype(BF16)
+    first = 0
+    for trip_ref in trip_refs:
+        trip_ref[...] = trip[first : first + trip_ref.shape[0]]
+        first += trip_ref.shape[0]
+
+
+def down(x, wt, block, halves):
     rows, width = x.shape
     lanes = 2 * wt.shape[0]
     return call(
         functools.partial(down_kernel, block),
         "down",
-        8 * MIB,
+        12 * MIB,
         2 * rows * width * lanes,
         2 * rows * width,
-        in_specs=[VMEM] * 2,
-        out_specs=[VMEM] * 2,
-        out_shape=[
-            jax.ShapeDtypeStruct((rows // 2, lanes), F32),
-            jax.ShapeDtypeStruct((rows // 2, lanes), BF16),
-        ],
-    )(x, wt)
+        in_specs=[HBM] * 2,
+        out_specs=[VMEM] * (1 + len(halves)),
+        out_shape=[jax.ShapeDtypeStruct((rows // 2, lanes), F32)]
+        + [jax.ShapeDtypeStruct((half * block, lanes), BF16) for half in halves],
+        scratch_shapes=[
+            pltpu.VMEM(x.shape, BF16),
+            pltpu.VMEM(wt.shape, BF16),
+            pltpu.SemaphoreType.DMA((2,)),
+        ],
+    )(*[pltpu.with_memory_space_constraint(array, pltpu.HBM) for array in (x, wt)])
 
 
 def ahead_kernel(block, slots, angle_ref, row_ref, *refs):
@@ -131,7 +145,7 @@
     return call(
         functools.partial(ahead_kernel, block, slots),
         "ahead",
-        4 * MIB,
+        20 * MIB,
         0,
         8 * angular.size * 2,
         in_specs=[VMEM, VMEM] + [ANY] * len(after),
@@ -149,22 +163,24 @@
     )(angular, row, *after)
 
 
-def triplet_kernel(block, slots, pieces, parts, *refs):
+def triplet_kernel(block, slots, pieces, halves, parts, *refs):
     index_ref, spot_ref, place_ref, angle_ref = refs[:4]
-    piece_refs = refs[4 : 4 + pieces]
-    trip_ref = refs[5 + pieces]
-    sent_refs = refs[6 + pieces : 6 + pieces + len(parts)]
+    piece_refs = refs[4 : 4 + halves * pieces]
+    trip_ref = refs[5 + halves * pieces]
+    sent_refs = refs[-1 - len(parts) : -1]
     held_ref = refs[-1]
     packed_rows, lanes = trip_ref.shape
     groups = packed_rows // block
     mask = left_lanes((block, lanes))
 
-    for piece in range(pieces):
-        rows = piece_refs[piece][...]
-        held_ref[piece * groups : (piece + 1) * groups] = rows.reshape(groups, block, lanes)
+    at = 0
+    for piece_ref in piece_refs:
+        rows = piece_ref[...]
+        here = rows.shape[0] // block
+        held_ref[at : at + here] = rows.reshape(here, block, lanes)
         rows = turn(rows.astype(F32)).astype(BF16)
-        at = (pieces + piece) * groups
-        held_ref[at : at + groups] = rows.reshape(groups, block, lanes)
+        held_ref[pieces * groups + at : pieces * groups + at + here] = rows.reshape(here, block, lanes)
+        at += here
     held_ref[2 * pieces * groups] = jnp.zeros((block, lanes), BF16)
 
     def target(q, carry):
@@ -184,7 +200,7 @@
             trip_ref[pl.ds(pl.multiple_of((2 * q + pair) * block, block), block), :] = total
         return carry
 
-    lax.fori_loop(0, groups // 2, target, 0, unroll=2)
+    lax.fori_loop(0, groups // 2, target, 0, unroll=True)
 
     place = place_ref[...].T
     turned_half = place >= packed_rows
@@ -206,10 +222,13 @@
 
 
 def triplet(index, spot, place, angles, pieces, after, block, slots, parts):
-    packed_rows, lanes = pieces[0].shape
-    held = packed_rows // block * 2 * len(pieces) + 1
-    return call(
-        functools.partial(triplet_kernel, block, slots, len(pieces), parts),
+    count, halves = len(pieces), len(pieces[0])
+    pieces = [half for piece in pieces for half in piece]
+    lanes = pieces[0].shape[1]
+    packed_rows = sum(half.shape[0] for half in pieces) // count
+    held = packed_rows // block * 2 * count + 1
+    return call(
+        functools.partial(triplet_kernel, block, slots, count, halves, parts),
         "triplet",
         6 * MIB + 2 * held * block * lanes,
         2 * packed_rows * slots * block * lanes,
@@ -319,8 +338,9 @@
     tile = 2 * block
     for m in range(packed_rows // block):
         column = place[:, m : m + 1]
-        column = jnp.where(column < packed_rows, column, column - packed_rows)
-        spot = lax.broadcasted_iota(jnp.int32, (tile, packed_rows), 1)
+        folded = spot_ref.shape[1]
+        spot = lax.broadcasted_iota(jnp.int32, (tile, folded), 1)
+        column = lax.rem(column, folded)
         spot_ref[m * tile : (m + 1) * tile, :] = (spot == column).astype(F32).astype(BF16)
     up = up_ref[...] * 0.5
     first = 0
@@ -344,15 +364,14 @@
         out_specs=[VMEM] * 2,
         out_shape=[
             jax.ShapeDtypeStruct((rows // 2, lanes), F32),
-            jax.ShapeDtypeStruct((rows, rows // 2), BF16),
+            jax.ShapeDtypeStruct((rows, rows // 4), BF16),
         ],
     )(slope, up, place, *grads)
 
 
 def scatter_kernel(block, slots, pieces, chunks, index_ref, place_ref, spot_ref, angle_ref, near_ref, *refs):
-    far_refs = refs[:chunks]
-    out_refs = refs[chunks : chunks + pieces]
-    total_ref, grad_ref = refs[chunks + pieces :]
+    far_refs, out_refs = refs[:chunks], refs[chunks:-2]
+    total_ref, grad_ref = refs[-2:]
     packed_rows, lanes = grad_ref.shape
     groups = packed_rows // block
     mask = left_lanes((block, lanes))
@@ -362,12 +381,18 @@
     wide_mask = left_lanes((tile, lanes))
     lane_side = jnp.where(wide_mask, 1.0, 0.0)
     far = jnp.concatenate([far_ref[...] for far_ref in far_refs], axis=0)
+    folded = packed_rows // 2
+    far = jnp.concatenate([far[:folded], far[folded:]], axis=1)
     several = 4
     for start in range(0, groups, several):
         got = dot(spot_ref[start * tile : (start + several) * tile, :], far)
         for i, m in enumerate(range(start, start + several)):
-            side = jnp.where(place[:, m : m + 1] < packed_rows, 1.0, 0.0)
-            mine = jnp.where(side == lane_side, got[i * tile : (i + 1) * tile], 0.0)
+            column = place[:, m : m + 1]
+            side = jnp.where(column < packed_rows, 1.0, 0.0)
+            column = jnp.where(column < packed_rows, column, column - packed_rows)
+            mine = got[i * tile : (i + 1) * tile]
+            mine = jnp.where(column < folded, mine[:, :lanes], mine[:, lanes:])
+            mine = jnp.where(side == lane_side, mine, 0.0)
             mine = mine + turn(mine)
             at = m * block
             both = near_ref[at : at + block, :] + jnp.where(mask, mine[:block], mine[block:])
@@ -385,21 +410,25 @@
             total_ref[index_ref[base + slots + s]] += jnp.where(mask, 0.0, term)
         return carry
 
-    lax.fori_loop(0, groups, target, 0, unroll=4)
+    lax.fori_loop(0, groups, target, 0, unroll=True)
 
     for piece in range(pieces):
         at = piece * groups
-        straight = total_ref[at : at + groups].reshape(packed_rows, lanes)
-        at += pieces * groups
-        crossed = total_ref[at : at + groups].reshape(packed_rows, lanes)
-        out_refs[piece][...] = (straight + turn(crossed)).astype(out_refs[piece].dtype)
-
-
-def scatter(index, place, spot, angles, near, far, types, block, slots):
+        for half in range(len(out_refs) // pieces):
+            out_ref = out_refs[piece * (len(out_refs) // pieces) + half]
+            rows = out_ref.shape[0]
+            straight = total_ref[at : at + rows // block].reshape(rows, lanes)
+            crossed = total_ref[pieces * groups + at : pieces * groups + at + rows // block].reshape(rows, lanes)
+            out_ref[...] = (straight + turn(crossed)).astype(out_ref.dtype)
+            at += rows // block
+
+
+def scatter(index, place, spot, angles, near, far, types, halves, block, slots):
     chunks = len(far)
     packed_rows, lanes = near.shape
     pieces = len(types)
     held = 2 * pieces * (packed_rows // block) + 1
+    outs = [jax.ShapeDtypeStruct((half * block, lanes), kind) for kind in types for half in halves]
     return call(
         functools.partial(scatter_kernel, block, slots, pieces, chunks),
         "scatter",
@@ -407,8 +436,8 @@
         2 * packed_rows * slots * block * lanes,
         8 * MIB,
         in_specs=[SMEM] + [VMEM] * (4 + chunks),
-        out_specs=[VMEM] * pieces,
-        out_shape=[jax.ShapeDtypeStruct((packed_rows, lanes), kind) for kind in types],
+        out_specs=[VMEM] * len(outs),
+        out_shape=outs,
         scratch_shapes=[
             pltpu.VMEM((held, block, lanes), F32),
             pltpu.VMEM((packed_rows, lanes), BF16),
@@ -416,43 +445,44 @@
     )(index, place, spot, angles, near, *far)
 
 
-def last_kernel(block, grads, pre_ref, wt_ref, *refs):
-    grad_refs, term_refs = refs[:grads], refs[grads:-3]
-    out_ref, held_ref, sems = refs[-3:]
+def last_kernel(block, grads, terms, start, pre_ref, wt_ref, *refs):
+    grad_refs, term_refs = refs[:grads], refs[grads : grads + terms]
+    out_ref, held_ref, sem = refs[-3:]
+    rows = held_ref.shape[0]
+    thin = slice(start // 2, (start + rows) // 2)
     left, right = padded(wt_ref[...])
+    total = term_refs[0][...].astype(F32)
+    for ref in term_refs[1:]:
+        total = total + ref[...].astype(F32)
+    _, slope = gated(pre_ref[thin, :] * 0.5)
+    grad = (total * (0.5 * slope)).astype(BF16)
+    both = join_pairs(dot(grad, left), dot(grad, right), block)
     first = 0
-    copies = []
-    for i, grad_ref in enumerate(grad_refs):
-        rows = grad_ref.shape[0]
-        thin = slice(first // 2, (first + rows) // 2)
-        wide = slice(first, first + rows)
-        total = term_refs[0][thin, :].astype(F32)
-        for ref in term_refs[1:]:
-            total = total + ref[thin, :].astype(F32)
-        _, slope = gated(pre_ref[thin, :] * 0.5)
-        grad = (total * (0.5 * slope)).astype(BF16)
-        both = join_pairs(dot(grad, left), dot(grad, right), block)
-        held_ref[wide, :] = (grad_ref[...].astype(F32) + both).astype(BF16)
-        copies.append(pltpu.make_async_copy(held_ref.at[wide, :], out_ref.at[wide, :], sems.at[i]))
-        copies[-1].start()
-        first += rows
-    for copy in copies:
-        copy.wait()
-
-
-def last(pre, grads, wt, terms, block):
+    for grad_ref in grad_refs:
+        here = slice(first, first + grad_ref.shape[0])
+        held_ref[here, :] = (grad_ref[...].astype(F32) + both[here]).astype(BF16)
+        first += grad_ref.shape[0]
+    copy = pltpu.make_async_copy(held_ref, out_ref.at[start : start + rows, :], sem)
+    copy.start()
+    copy.wait()
+
+
+def last(pre, grads, wt, terms, before, block, start):
     rows, width = 2 * pre.shape[0], wt.shape[1]
-    return call(
-        functools.partial(last_kernel, block, len(grads)),
+    here = 2 * terms[0].shape[0]
+    inputs = [pre, wt, *grads, *terms]
+    return call(
+        functools.partial(last_kernel, block, len(grads), len(terms), start),
         "last",
-        8 * MIB,
-        2 * rows * width * pre.shape[1],
-        4 * rows * width,
-        in_specs=[VMEM] * (2 + len(grads) + len(terms)),
+        12 * MIB,
+        0,
+        0,
+        in_specs=[VMEM] * len(inputs) + [HBM] * len(before),
         out_specs=HBM,
         out_shape=jax.ShapeDtypeStruct((rows, width), BF16),
-        scratch_shapes=[pltpu.VMEM((rows, width), BF16), pltpu.SemaphoreType.DMA((len(grads),))],
-    )(pre, wt, *grads, *terms)
+        scratch_shapes=[pltpu.VMEM((here, width), BF16), pltpu.SemaphoreType.DMA(())],
+        input_output_aliases={len(inputs): 0} if before else {},
+    )(*inputs, *before)
 
 
 def on_device(
@@ -489,23 +519,29 @@
     place_row = place.reshape(1, local_edges)
     place = place.reshape(groups, 2 * block)
 
-    pre_down, trip = down(edge_feats, down_trans, block)
-    angle_in, angle_out, spot, token = ahead(angular, place_row, [trip, index, place], block)
+    cuts = [0, groups * 8 // 16, groups * 13 // 16, groups]
+    parts = [end - start for start, end in zip(cuts, cuts[1:])]
+    sizes = [parts[0], groups - parts[0]]
+
+    pre_down, *trip = down(edge_feats, down_trans, block, [groups])
+    angle_in, angle_out, spot, token = ahead(angular, place_row, [trip[0], index, place], block)
     pieces = {0: trip}
     bits = [1 << i for i in range(lane_count.bit_length() - 1)]
     for bit in reversed(bits):
-        if bit == 1:
-            last_piece = lane_count - 2
-            pieces[last_piece], token = lax.optimization_barrier((pieces[last_piece], token))
-        pieces.update({d ^ bit: swapped(piece, "narrow", bit) for d, piece in pieces.items()})
+        if bit > 1:
+            pieces.update({d ^ bit: [swapped(half, "narrow", bit) for half in piece] for d, piece in pieces.items()})
+    more = {d ^ 1: [swapped(half, "narrow", 1) for half in piece] for d, piece in pieces.items() if d + 2 < lane_count}
+    here, gone = pieces[lane_count - 2], []
+    for i in range(len(here)):
+        here[i], token, *gone = lax.optimization_barrier((here[i], token, *gone))
+        gone.append(swapped(here[i], "narrow", 1))
+    pieces.update(more)
+    pieces[lane_count - 1] = gone
     pieces = [pieces[d] for d in range(lane_count)]
-    cuts = [0, groups * 7 // 16, groups * 12 // 16, groups]
-    parts = [end - start for start, end in zip(cuts, cuts[1:])]
-    sizes = [parts[0], groups - parts[0]]
     trip_own, early, late = triplet(index, spot, place, angle_in, pieces, token, block, slots, sizes)
     early = swapped(early, "cluster", top_bit)
     base, slope = gate(edge_feats, trip_own, up_weight, block)
-    early, late = lax.optimization_barrier((early, late))
+    early, late, base, slope = lax.optimization_barrier((early, late, base, slope))
     late = swapped(late, "cluster", top_bit)
     done, grads, far = [], [], []
     for first, part in zip(cuts, parts):
@@ -527,16 +563,18 @@
         far.append(swapped(sent, "cluster", top_bit))
     near, spot = near_part(slope, up_weight, place, grads, block)
     types = [BF16 if d % 2 else F32 for d in range(lane_count)]
-    sums = dict(enumerate(scatter(index, place, spot, angle_out, near, far, types, block, slots)))
-    terms = [sums[0]]
+    sums = scatter(index, place, spot, angle_out, near, far, types, sizes, block, slots)
+    sums = {d: sums[len(sizes) * d : len(sizes) * (d + 1)] for d in range(lane_count)}
+    terms = [[half] for half in sums[0]]
     for bit in bits:
         for d in range(lane_count - bit, -1, -2 * bit):
-            got = swapped(sums[d].astype(BF16), "narrow", bit)
+            got = [swapped(half.astype(BF16), "narrow", bit) for half in sums[d]]
             if d == bit:
-                terms.append(got)
+                terms = [term + [half] for term, half in zip(terms, got)]
             else:
-                sums[d ^ bit] = sums[d ^ bit] + got.astype(F32)
-    grad_x = last(pre_down, grads, down_trans, terms, block)
+                sums[d ^ bit] = [held + half.astype(F32) for held, half in zip(sums[d ^ bit], got)]
+    grad_x = last(pre_down, grads[:1], down_trans, terms[0], [], block, 0)
+    grad_x = last(pre_down, grads[1:], down_trans, terms[1], [grad_x], block, 2 * sizes[0] * block)
     return (output, grad_x)
 
 

time: 65.4 us -> 61.8 us (0.945)
  waiting for transfers between devices: 20.5 us -> 17.7 us
  local copies, waits for them, and re-layouts: 2.64 us -> 0.21 us
  starting transfers between devices: 14.2 us -> 15.2 us
    ppermute x11 -> x14, waiting for transfers between devices: 20.5 us -> 17.7 us  [swapped(): lax.ppermute(array, axis, [(i, i ^ bit) for i in range(lax.axis_size(axis...]
    unnamed x24 -> x20, local copies, waits for them, and re-layouts: 2.47 us -> 0.04 us
    pallas_call x4 -> x5, Pallas kernels: 9.95 us -> 11.8 us  [the longest x1 3.6 us: ahead(): call(functools.partial(ahead_kernel, block, slots), 'ahead', 20 * MIB, 0,...]
    ppermute x11 -> x14, starting transfers between devices: 14.2 us -> 15.2 us  [swapped(): lax.ppermute(array, axis, [(i, i ^ bit) for i in range(lax.axis_size(axis...]
    pallas_call x1, Pallas kernels: 5.03 us -> 4.19 us  [scatter(): call(functools.partial(scatter_kernel, block, slots, pieces, chunks), 'sc...]
    pallas_call x1, Pallas kernels: 1.82 us -> 1.13 us  [near_part(): call(functools.partial(near_kernel, block), 'near', 8 * MIB, 2 * rows * w...]
  transfers between devices with their start and end apart: 11 -> 14, of which waited for: 7 -> 8; matrix products, arithmetic and copies ran while one was open for 0% -> 1% of each run, Pallas kernels for 24% -> 27%
where the time goes in v4:
time: 61.8 us; the launch traced here: 61.7 us
  Pallas kernels  27.4 us (44%)
  waiting for transfers between devices  17.7 us (29%)
  starting transfers between devices  15.2 us (25%)
  between operations  1.02 us (2%)
    ppermute x14, waiting for transfers between devices, swapped(): lax.ppermute(array, axis, [(i, i ^ bit) for i in range(lax.axis_size(axis...  17.7 us
    ppermute x14, starting transfers between devices, swapped(): lax.ppermute(array, axis, [(i, i ^ bit) for i in range(lax.axis_size(axis...  15.2 us
    pallas_call x3, Pallas kernels, layer(): call(functools.partial(layer_kernel, block, first, far_first), 'layer', 3...  8.52 us
    pallas_call x1, Pallas kernels, scatter(): call(functools.partial(scatter_kernel, block, slots, pieces, chunks), 'sc...  4.19 us
    pallas_call x1, Pallas kernels, ahead(): call(functools.partial(ahead_kernel, block, slots), 'ahead', 20 * MIB, 0,...  3.6 us
    pallas_call x1, Pallas kernels, triplet(): call(functools.partial(triplet_kernel, block, slots, count, halves, parts...  2.87 us
    pallas_call x2, Pallas kernels, last(): call(functools.partial(last_kernel, block, len(grads), len(terms), start)...  2.83 us
    pallas_call x1, Pallas kernels, down(): call(functools.partial(down_kernel, block), 'down', 12 * MIB, 2 * rows *...  2.48 us
  transfers between devices with their start and end apart: 14, of which 8 were waited for; matrix products, arithmetic and copies ran while one was open for 1% of the time, Pallas kernels for 27%

profile of v4, /device:TPU:0, one launch (start us, length us, event | category | flops | bytes accessed | tf_op | source)
XLA Modules:
  0.0 61.7 jit_solution(5697297650900147905)
XLA Ops:
  0.6 0.0 copy-start.7
  0.6 0.0 copy-start.9
  0.7 0.0 copy-start.8
  0.7 0.0 copy-start.4
  0.7 2.5 %down.1 = (f32[1024,128]{1,0:T(8,128)S(1)}, bf16[1024,128]{1,0:T(8,128)(2,1)S(1)}) custom-call(bf16[2048,512]{1,0:T(8,128)(2,1)} %x_ref.3, bf16[64,512]{1,0:T(8,128)(2,1)} %bitcast.12), custom_call_target="tpu_custom_call" | custom-call | flops 268435456 | bytes 2097152 | tf_op jit(solution)/shard_map/down/pallas_call | solution.py:88
  3.2 3.0 %collective-permute-start.1 = (bf16[1024,128]{1,0:T(8,128)(2,1)S(1)}, bf16[1024,128]{1,0:T(8,128)(2,1)S(1)}, u32[]{:S(2)}, u32[]{:S(2)}) collective-permute-start(bf16[1024,128]{1,0:T(8,128)(2,1)S(1)} %get-tuple-element.38.refs_0_.refs_4_), channel_id=1, source_target_pairs={{0,2},{1,3},{2,0},{3,1},{4,6},{5,7},{6,4},{7,5},{8,10},{9,11},{10,... | collective-permute-start | bytes 786440 | tf_op jit(solution)/shard_map/ppermute | solution.py:29
  6.2 0.0 collective-permute-start
  6.2 0.0 copy-done.7
  6.2 0.0 copy-done.9
  6.3 0.1 copy.15
  6.4 0.1 reshape.14.refs_1_.refs_0_.index_ref
  6.5 3.6 %ahead.1 = (bf16[32,64,512]{2,1,0:T(8,128)(2,1)S(1)}, bf16[16,512,128]{2,1,0:T(8,128)(2,1)S(1)}, bf16[1024,2048]{1,0:T(8,128)(2,1)S(1)}, bf16[16,128]{1,0:T(8,128)(2,1)S(1)}) custom-call(bf16[32,8,4096]{2,1,0:T(8,128)(2,1)S(1)} %copy-done.4, s32[1,2048]{1,0:T(1,128)S(1)} %bitcast.15, bf16[1024,128]{1,0:T(8,128)(2,1)S(1)} %get-tuple-element.38.refs_0_.refs_4_, ...), custom_call_target="tpu_custom_call" | custom-call | bytes 16777216 | tf_op jit(solution)/shard_map/ahead/pallas_call | solution.py:145
  10.1 2.4 %collective-permute-done.1.refs_6_ = bf16[1024,128]{1,0:T(8,128)(2,1)S(1)} collective-permute-done((bf16[1024,128]{1,0:T(8,128)(2,1)S(1)}, bf16[1024,128]{1,0:T(8,128)(2,1)S(1)}, u32[]{:S(2)}, u32[]{:S(2)}) %collective-permute-start.1) | collective-permute-done | bytes 262176 | tf_op jit(solution)/shard_map/ppermute | solution.py:29
  12.5 0.0 collective-permute-start.2
  12.5 0.0 collective-permute-done.refs_5_
  12.5 1.5 %collective-permute-done.2.refs_7_ = bf16[1024,128]{1,0:T(8,128)(2,1)S(1)} collective-permute-done((bf16[1024,128]{1,0:T(8,128)(2,1)S(1)}, bf16[1024,128]{1,0:T(8,128)(2,1)S(1)}, u32[]{:S(2)}, u32[]{:S(2)}) %collective-permute-start.2) | collective-permute-done | bytes 262176 | tf_op jit(solution)/shard_map/ppermute | solution.py:29
  14.0 2.9 %triplet.1 = (bf16[1024,128]{1,0:T(8,128)(2,1)S(1)}, bf16[512,128]{1,0:T(8,128)(2,1)S(1)}, bf16[512,128]{1,0:T(8,128)(2,1)S(1)}) custom-call(s32[256]{0:T(256)S(1)} %reshape.14.refs_1_.refs_0_.index_ref, bf16[1024,2048]{1,0:T(8,128)(2,1)S(1)} %get-tuple-element.39.refs_1_, s32[16,128]{1,0:T(8,128)S(1)} %fusion.24.refs_2_.place_ref, ...), custom_call_target="tpu_custom_call" | custom-call | flops 134217728 | bytes 8388608 | tf_op jit(solution)/shard_map/triplet/pallas_call | solution.py:230
  16.9 0.0 copy-start
  16.9 2.9 %collective-permute-start.3 = (bf16[512,128]{1,0:T(8,128)(2,1)S(1)}, bf16[512,128]{1,0:T(8,128)(2,1)S(1)}, u32[]{:S(2)}, u32[]{:S(2)}) collective-permute-start(bf16[512,128]{1,0:T(8,128)(2,1)S(1)} %get-tuple-element.44), channel_id=1, source_target_pairs={{0,16},{4,20},{8,24},{12,28},{16,0},{20,4},{24,8},{28,12},{1,17},{... | collective-permute-start | bytes 393224 | tf_op jit(solution)/shard_map/ppermute | solution.py:29
  19.8 1.8 %gate.1 = (f32[2048,512]{1,0:T(8,128)S(1)}, bf16[2048,512]{1,0:T(8,128)(2,1)S(1)}) custom-call(bf16[2048,512]{1,0:T(8,128)(2,1)S(1)} %copy-done.1, bf16[1024,128]{1,0:T(8,128)(2,1)S(1)} %get-tuple-element.46.own_ref, bf16[64,512]{1,0:T(8,128)(2,1)S(1)} %copy-done.5), custom_call_target="tpu_custom_call" | custom-call | flops 268435456 | bytes 8388608 | tf_op jit(solution)/shard_map/gate/pallas_call | solution.py:275
  21.6 4.8 %collective-permute-done.3.far_ref = bf16[512,128]{1,0:T(8,128)(2,1)S(1)} collective-permute-done((bf16[512,128]{1,0:T(8,128)(2,1)S(1)}, bf16[512,128]{1,0:T(8,128)(2,1)S(1)}, u32[]{:S(2)}, u32[]{:S(2)}) %collective-permute-start.3) | collective-permute-done | bytes 131104 | tf_op jit(solution)/shard_map/ppermute | solution.py:29
  26.4 0.0 collective-permute-start.4
  26.4 4.0 %layer.3 = (bf16[2048,512]{1,0:T(8,128)(2,1)}, bf16[1024,512]{1,0:T(8,128)(2,1)S(1)}, bf16[512,128]{1,0:T(8,128)(2,1)S(1)}) custom-call(f32[2048,512]{1,0:T(8,128)S(1)} %get-tuple-element.49.base_ref, bf16[2048,512]{1,0:T(8,128)(2,1)S(1)} %copy-done, bf16[512,128]{1,0:T(8,128)(2,1)S(1)} %collective-permute-done.3.far_ref, bf16[64,512]{1,0:T(8,128)(2,1)S(1)} %copy-done.5, ...), custom_call_target="tpu_custom_call" | custom-call | tf_op jit(solution)/shard_map/layer/pallas_call | solution.py:316
  30.4 3.0 %collective-permute-start.5 = (bf16[512,128]{1,0:T(8,128)(2,1)S(1)}, bf16[512,128]{1,0:T(8,128)(2,1)S(1)}, u32[]{:S(2)}, u32[]{:S(2)}) collective-permute-start(bf16[512,128]{1,0:T(8,128)(2,1)S(1)} %get-tuple-element.63), channel_id=1, source_target_pairs={{0,16},{4,20},{8,24},{12,28},{16,0},{20,4},{24,8},{28,12},{1,17},{... | collective-permute-start | bytes 393224 | tf_op jit(solution)/shard_map/ppermute | solution.py:29
  33.4 3.0 %collective-permute-done.4.far_ref = bf16[512,128]{1,0:T(8,128)(2,1)S(1)} collective-permute-done((bf16[512,128]{1,0:T(8,128)(2,1)S(1)}, bf16[512,128]{1,0:T(8,128)(2,1)S(1)}, u32[]{:S(2)}, u32[]{:S(2)}) %collective-permute-start.4) | collective-permute-done | bytes 131104 | tf_op jit(solution)/shard_map/ppermute | solution.py:29
  36.4 2.6 %layer.4 = (bf16[2048,512]{1,0:T(8,128)(2,1)}, bf16[640,512]{1,0:T(8,128)(2,1)S(1)}, bf16[320,128]{1,0:T(8,128)(2,1)S(1)}) custom-call(f32[2048,512]{1,0:T(8,128)S(1)} %get-tuple-element.49.base_ref, bf16[2048,512]{1,0:T(8,128)(2,1)S(1)} %copy-done, bf16[512,128]{1,0:T(8,128)(2,1)S(1)} %collective-permute-done.4.far_ref, ...), custom_call_target="tpu_custom_call", output_to_operand_aliasing={{0}: (6, {})} | custom-call | tf_op jit(solution)/shard_map/layer/pallas_call | solution.py:316
  38.9 0.1 collective-permute-start.6
  39.0 2.0 %layer.5 = (bf16[2048,512]{1,0:T(8,128)(2,1)}, bf16[384,512]{1,0:T(8,128)(2,1)S(1)}, bf16[192,128]{1,0:T(8,128)(2,1)S(1)}) custom-call(f32[2048,512]{1,0:T(8,128)S(1)} %get-tuple-element.49.base_ref, bf16[2048,512]{1,0:T(8,128)(2,1)S(1)} %copy-done, bf16[512,128]{1,0:T(8,128)(2,1)S(1)} %collective-permute-done.4.far_ref, ...), custom_call_target="tpu_custom_call", output_to_operand_aliasing={{0}: (6, {})} | custom-call | tf_op jit(solution)/shard_map/layer/pallas_call | solution.py:316
  41.0 3.0 %collective-permute-start.7 = (bf16[192,128]{1,0:T(8,128)(2,1)S(1)}, bf16[192,128]{1,0:T(8,128)(2,1)S(1)}, u32[]{:S(2)}, u32[]{:S(2)}) collective-permute-start(bf16[192,128]{1,0:T(8,128)(2,1)S(1)} %get-tuple-element.65), channel_id=1, source_target_pairs={{0,16},{4,20},{8,24},{12,28},{16,0},{20,4},{24,8},{28,12},{1,17},{... | collective-permute-start | bytes 147464 | tf_op jit(solution)/shard_map/ppermute | solution.py:29
  44.0 1.1 %near.1 = (f32[1024,128]{1,0:T(8,128)S(1)}, bf16[2048,512]{1,0:T(8,128)(2,1)S(1)}) custom-call(bf16[2048,512]{1,0:T(8,128)(2,1)S(1)} %get-tuple-element.58.slope_ref, bf16[64,512]{1,0:T(8,128)(2,1)S(1)} %copy-done.5, s32[16,128]{1,0:T(8,128)S(1)} %fusion.24.refs_2_.place_ref, bf16[1024,512]{1,0:T(8,128)(2,1)S(1)} %get-tuple-element.59.refs_0_, ...), custom_call_target="tpu_custom_call" | custom-call | flops 268435456 | bytes 4194304 | tf_op jit(solution)/shard_map/near/pallas_call | solution.py:357
  45.1 0.0 collective-permute-done.5.refs_0_
  45.1 0.9 %collective-permute-done.7.refs_2_ = bf16[192,128]{1,0:T(8,128)(2,1)S(1)} collective-permute-done((bf16[192,128]{1,0:T(8,128)(2,1)S(1)}, bf16[192,128]{1,0:T(8,128)(2,1)S(1)}, u32[]{:S(2)}, u32[]{:S(2)}) %collective-permute-start.7) | collective-permute-done | bytes 49184 | tf_op jit(solution)/shard_map/ppermute | solution.py:29
  46.0 0.0 collective-permute-done.6.refs_1_
  46.1 4.2 %scatter.1 = (f32[512,128]{1,0:T(8,128)S(1)}, f32[512,128]{1,0:T(8,128)S(1)}, bf16[512,128]{1,0:T(8,128)(2,1)S(1)}, bf16[512,128]{1,0:T(8,128)(2,1)S(1)}, f32[51...) custom-call(s32[256]{0:T(256)S(1)} %reshape.14.refs_1_.refs_0_.index_ref, ...), custom_call_target="tpu_custom_call" | custom-call | flops 134217728 | bytes 8388608 | tf_op jit(solution)/shard_map/scatter/pallas_call | solution.py:432
  50.3 0.1 collective-permute-start.12
  50.3 0.5 collective-permute-start.8
  50.8 0.1 collective-permute-start.9
  50.9 0.4 collective-permute-start.11
  51.3 0.3 collective-permute-done.12
  51.7 1.6 %collective-permute-start.13 = (bf16[512,128]{1,0:T(8,128)(2,1)S(1)}, bf16[512,128]{1,0:T(8,128)(2,1)S(1)}, u32[]{:S(2)}, u32[]{:S(2)}) collective-permute-start(bf16[512,128]{1,0:T(8,128)(2,1)S(1)} %add_convert_fusion), channel_id=1, source_target_pairs={{0,2},{1,3},{2,0},{3,1},{4,6},{5,7},{6,4},{7,5},{8,10},{9,11},{10,... | collective-permute-start | bytes 393224 | tf_op jit(solution)/shard_map/ppermute | solution.py:29
  53.3 0.0 collective-permute-done.9
  53.3 0.6 collective-permute-start.10
  53.9 0.0 collective-permute-done.11.refs_2_
  53.9 4.2 %collective-permute-done.13.refs_3_ = bf16[512,128]{1,0:T(8,128)(2,1)S(1)} collective-permute-done((bf16[512,128]{1,0:T(8,128)(2,1)S(1)}, bf16[512,128]{1,0:T(8,128)(2,1)S(1)}, u32[]{:S(2)}, u32[]{:S(2)}) %collective-permute-start.13) | collective-permute-done | bytes 131104 | tf_op jit(solution)/shard_map/ppermute | solution.py:29
  58.1 1.4 %last.2.refs_5_ = bf16[2048,512]{1,0:T(8,128)(2,1)} custom-call(f32[1024,128]{1,0:T(8,128)S(1)} %get-tuple-element.55.pre_ref, bf16[64,512]{1,0:T(8,128)(2,1)S(1)} %bitcast.13, bf16[1024,512]{1,0:T(8,128)(2,1)S(1)} %get-tuple-element.59.refs_0_, f32[512,128]{1,0:T(8,128)S(1)} %get-tuple-element.70.refs_1_, ...), custom_call_target="tpu_custom_call" | custom-call | tf_op jit(solution)/shard_map/last/pallas_call | solution.py:474
  59.5 0.0 collective-permute-done.8.refs_3_
  59.5 0.6 collective-permute-done.10.refs_4_
  60.1 1.4 %last.3 = bf16[2048,512]{1,0:T(8,128)(2,1)} custom-call(f32[1024,128]{1,0:T(8,128)S(1)} %get-tuple-element.55.pre_ref, bf16[64,512]{1,0:T(8,128)(2,1)S(1)} %bitcast.14, bf16[640,512]{1,0:T(8,128)(2,1)S(1)} %get-tuple-element.56.refs_1_.refs_0_, bf16[384,512]{1,0:T(8,128)(2,1)S(1)} %get-tuple-element.57.refs_2_.refs_1_, ...), custom_call_target="tpu_custom_call", output_to_operand_aliasing={{}: (7, {})} | custom-call | tf_op jit(solution)/shard_map/last/pallas_call | solution.py:474
  (20 shorter events, 0.2 us)
Async XLA Ops:
  0.6 5.6 %copy-start.7 = (s32[2048]{0:T(1024)S(1)}, s32[2048]{0:T(1024)}, u32[]{:S(2)}) copy-start(s32[2048]{0:T(1024)} %param.17) | copy-start | bytes 24580
  0.6 5.6 %copy-start.9 = (s32[32]{0:T(128)S(1)}, s32[32]{0:T(128)}, u32[]{:S(2)}) copy-start(s32[32]{0:T(128)} %param.19) | copy-start | bytes 388
  0.7 5.6 %copy-start.8 = (s32[32,8]{0,1:T(8,128)S(1)}, s32[32,8]{0,1:T(8,128)}, u32[]{:S(2)}) copy-start(s32[32,8]{0,1:T(8,128)} %param.18) | copy-start | bytes 3076
  0.7 5.8 %copy-start.4 = (bf16[32,8,4096]{2,1,0:T(8,128)(2,1)S(1)}, bf16[32,8,4096]{2,1,0:T(8,128)(2,1)}, u32[]{:S(2)}) copy-start(bf16[32,8,4096]{2,1,0:T(8,128)(2,1)} %angle_ref.1) | copy-start | bytes 6291460
  3.2 9.3 %collective-permute-start.1 = (bf16[1024,128]{1,0:T(8,128)(2,1)S(1)}, bf16[1024,128]{1,0:T(8,128)(2,1)S(1)}, u32[]{:S(2)}, u32[]{:S(2)}) collective-permute-start(bf16[1024,128]{1,0:T(8,128)(2,1)S(1)} %get-tuple-element.38.refs_0_.refs_4_), channel_id=1, source_target_pairs={{0,2},{1,3},{2,0},{3,1},{4,6},{5,7},{6,4},{7,5},{8,10},{9,11},{10,... | collective-permute-start | bytes 786440 | tf_op jit(solution)/shard_map/ppermute | solution.py:29
  6.2 6.3 %collective-permute-start = (bf16[1024,128]{1,0:T(8,128)(2,1)S(1)}, bf16[1024,128]{1,0:T(8,128)(2,1)S(1)}, u32[]{:S(2)}, u32[]{:S(2)}) collective-permute-start(bf16[1024,128]{1,0:T(8,128)(2,1)S(1)} %get-tuple-element.38.refs_0_.refs_4_), channel_id=1, source_target_pairs={{0,1},{1,0},{2,3},{3,2},{4,5},{5,4},{6,7},{7,6},{8,9},{9,8},{10,11... | collective-permute-start | bytes 786440 | tf_op jit(solution)/shard_map/ppermute | solution.py:29
  12.5 1.5 %collective-permute-start.2 = (bf16[1024,128]{1,0:T(8,128)(2,1)S(1)}, bf16[1024,128]{1,0:T(8,128)(2,1)S(1)}, u32[]{:S(2)}, u32[]{:S(2)}) collective-permute-start(bf16[1024,128]{1,0:T(8,128)(2,1)S(1)} %collective-permute-done.1.refs_6_), channel_id=1, source_target_pairs={{0,1},{1,0},{2,3},{3,2},{4,5},{5,4},{6,7},{7,6},{8,9},{9,8},{10,11... | collective-permute-start | bytes 786440 | tf_op jit(solution)/shard_map/ppermute | solution.py:29
  14.0 5.8 %copy-start.1 = (bf16[2048,512]{1,0:T(8,128)(2,1)S(1)}, bf16[2048,512]{1,0:T(8,128)(2,1)}, u32[]{:S(2)}) copy-start(bf16[2048,512]{1,0:T(8,128)(2,1)} %x_ref.3) | copy-start | bytes 6291460
  14.0 5.8 %copy-start.5 = (bf16[64,512]{1,0:T(8,128)(2,1)S(1)}, bf16[64,512]{1,0:T(8,128)(2,1)}, u32[]{:S(2)}) copy-start(bf16[64,512]{1,0:T(8,128)(2,1)} %up_ref.9) | copy-start | bytes 196612
  14.0 12.4 %copy-start.2 = (bf16[1,512,512]{2,1,0:T(8,128)(2,1)S(1)}, bf16[1,512,512]{2,1,0:T(8,128)(2,1)}, u32[]{:S(2)}) copy-start(bf16[1,512,512]{2,1,0:T(8,128)(2,1)} %param.14) | copy-start | bytes 1572868
  14.0 12.4 %copy-start.3 = (bf16[1,512,512]{2,1,0:T(8,128)(2,1)S(1)}, bf16[1,512,512]{2,1,0:T(8,128)(2,1)}, u32[]{:S(2)}) copy-start(bf16[1,512,512]{2,1,0:T(8,128)(2,1)} %param.15) | copy-start | bytes 1572868
  16.9 9.5 %copy-start = (bf16[2048,512]{1,0:T(8,128)(2,1)S(1)}, bf16[2048,512]{1,0:T(8,128)(2,1)}, u32[]{:S(2)}) copy-start(bf16[2048,512]{1,0:T(8,128)(2,1)} %ct_ref.5) | copy-start | bytes 6291460
  16.9 9.5 %collective-permute-start.3 = (bf16[512,128]{1,0:T(8,128)(2,1)S(1)}, bf16[512,128]{1,0:T(8,128)(2,1)S(1)}, u32[]{:S(2)}, u32[]{:S(2)}) collective-permute-start(bf16[512,128]{1,0:T(8,128)(2,1)S(1)} %get-tuple-element.44), channel_id=1, source_target_pairs={{0,16},{4,20},{8,24},{12,28},{16,0},{20,4},{24,8},{28,12},{1,17},{... | collective-permute-start | bytes 393224 | tf_op jit(solution)/shard_map/ppermute | solution.py:29
  26.4 9.9 %collective-permute-start.4 = (bf16[512,128]{1,0:T(8,128)(2,1)S(1)}, bf16[512,128]{1,0:T(8,128)(2,1)S(1)}, u32[]{:S(2)}, u32[]{:S(2)}) collective-permute-start(bf16[512,128]{1,0:T(8,128)(2,1)S(1)} %get-tuple-element.50), channel_id=1, source_target_pairs={{0,16},{4,20},{8,24},{12,28},{16,0},{20,4},{24,8},{28,12},{1,17},{... | collective-permute-start | bytes 393224 | tf_op jit(solution)/shard_map/ppermute | solution.py:29
  30.4 14.7 %collective-permute-start.5 = (bf16[512,128]{1,0:T(8,128)(2,1)S(1)}, bf16[512,128]{1,0:T(8,128)(2,1)S(1)}, u32[]{:S(2)}, u32[]{:S(2)}) collective-permute-start(bf16[512,128]{1,0:T(8,128)(2,1)S(1)} %get-tuple-element.63), channel_id=1, source_target_pairs={{0,16},{4,20},{8,24},{12,28},{16,0},{20,4},{24,8},{28,12},{1,17},{... | collective-permute-start | bytes 393224 | tf_op jit(solution)/shard_map/ppermute | solution.py:29
  38.9 7.1 %collective-permute-start.6 = (bf16[320,128]{1,0:T(8,128)(2,1)S(1)}, bf16[320,128]{1,0:T(8,128)(2,1)S(1)}, u32[]{:S(2)}, u32[]{:S(2)}) collective-permute-start(bf16[320,128]{1,0:T(8,128)(2,1)S(1)} %get-tuple-element.64), channel_id=1, source_target_pairs={{0,16},{4,20},{8,24},{12,28},{16,0},{20,4},{24,8},{28,12},{1,17},{... | collective-permute-start | bytes 245768 | tf_op jit(solution)/shard_map/ppermute | solution.py:29
  41.0 5.1 %collective-permute-start.7 = (bf16[192,128]{1,0:T(8,128)(2,1)S(1)}, bf16[192,128]{1,0:T(8,128)(2,1)S(1)}, u32[]{:S(2)}, u32[]{:S(2)}) collective-permute-start(bf16[192,128]{1,0:T(8,128)(2,1)S(1)} %get-tuple-element.65), channel_id=1, source_target_pairs={{0,16},{4,20},{8,24},{12,28},{16,0},{20,4},{24,8},{28,12},{1,17},{... | collective-permute-start | bytes 147464 | tf_op jit(solution)/shard_map/ppermute | solution.py:29
  46.1 12.1 %copy-start.6 = (bf16[512,64]{0,1:T(8,128)(2,1)S(1)}, bf16[512,64]{0,1:T(8,128)(2,1)}, u32[]{:S(2)}) copy-start(bf16[512,64]{0,1:T(8,128)(2,1)} %param.12) | copy-start | bytes 196612
  50.3 1.4 %collective-permute-start.12 = (bf16[512,128]{1,0:T(8,128)(2,1)S(1)}, bf16[512,128]{1,0:T(8,128)(2,1)S(1)}, u32[]{:S(2)}, u32[]{:S(2)}) collective-permute-start(bf16[512,128]{1,0:T(8,128)(2,1)S(1)} %get-tuple-element.73), channel_id=1, source_target_pairs={{0,1},{1,0},{2,3},{3,2},{4,5},{5,4},{6,7},{7,6},{8,9},{9,8},{10,11... | collective-permute-start | bytes 393224 | tf_op jit(solution)/shard_map/ppermute | solution.py:29
  50.3 9.2 %collective-permute-start.8 = (bf16[512,128]{1,0:T(8,128)(2,1)S(1)}, bf16[512,128]{1,0:T(8,128)(2,1)S(1)}, u32[]{:S(2)}, u32[]{:S(2)}) collective-permute-start(bf16[512,128]{1,0:T(8,128)(2,1)S(1)} %get-tuple-element.67), channel_id=1, source_target_pairs={{0,1},{1,0},{2,3},{3,2},{4,5},{5,4},{6,7},{7,6},{8,9},{9,8},{10,11... | collective-permute-start | bytes 393224 | tf_op jit(solution)/shard_map/ppermute | solution.py:29
  50.8 2.5 %collective-permute-start.9 = (bf16[512,128]{1,0:T(8,128)(2,1)S(1)}, bf16[512,128]{1,0:T(8,128)(2,1)S(1)}, u32[]{:S(2)}, u32[]{:S(2)}) collective-permute-start(bf16[512,128]{1,0:T(8,128)(2,1)S(1)} %get-tuple-element.69), channel_id=1, source_target_pairs={{0,1},{1,0},{2,3},{3,2},{4,5},{5,4},{6,7},{7,6},{8,9},{9,8},{10,11... | collective-permute-start | bytes 393224 | tf_op jit(solution)/shard_map/ppermute | solution.py:29
  50.9 3.0 %collective-permute-start.11 = (bf16[512,128]{1,0:T(8,128)(2,1)S(1)}, bf16[512,128]{1,0:T(8,128)(2,1)S(1)}, u32[]{:S(2)}, u32[]{:S(2)}) collective-permute-start(bf16[512,128]{1,0:T(8,128)(2,1)S(1)} %get-tuple-element.71), channel_id=1, source_target_pairs={{0,1},{1,0},{2,3},{3,2},{4,5},{5,4},{6,7},{7,6},{8,9},{9,8},{10,11... | collective-permute-start | bytes 393224 | tf_op jit(solution)/shard_map/ppermute | solution.py:29
  51.7 6.4 %collective-permute-start.13 = (bf16[512,128]{1,0:T(8,128)(2,1)S(1)}, bf16[512,128]{1,0:T(8,128)(2,1)S(1)}, u32[]{:S(2)}, u32[]{:S(2)}) collective-permute-start(bf16[512,128]{1,0:T(8,128)(2,1)S(1)} %add_convert_fusion), channel_id=1, source_target_pairs={{0,2},{1,3},{2,0},{3,1},{4,6},{5,7},{6,4},{7,5},{8,10},{9,11},{10,... | collective-permute-start | bytes 393224 | tf_op jit(solution)/shard_map/ppermute | solution.py:29
  53.3 6.8 %collective-permute-start.10 = (bf16[512,128]{1,0:T(8,128)(2,1)S(1)}, bf16[512,128]{1,0:T(8,128)(2,1)S(1)}, u32[]{:S(2)}, u32[]{:S(2)}) collective-permute-start(bf16[512,128]{1,0:T(8,128)(2,1)S(1)} %add_convert_fusion.1), channel_id=1, source_target_pairs={{0,2},{1,3},{2,0},{3,1},{4,6},{5,7},{6,4},{7,5},{8,10},{9,11},{10,... | collective-permute-start | bytes 393224 | tf_op jit(solution)/shard_map/ppermute | solution.py:29

commit v5 on v4

--- a/solution.py
+++ b/solution.py
@@ -129,11 +129,10 @@
         return carry
 
     lax.fori_loop(0, angle_ref.shape[0] // 2, pair, 0, unroll=2)
-    row = row_ref[...]
-    packed_rows = spot_ref.shape[0]
-    row = jnp.where(row < packed_rows, row, row - packed_rows)
-    tile = packed_rows // 8
-    for start in range(0, packed_rows, tile):
+    folded = spot_ref.shape[0]
+    row = lax.rem(row_ref[...], folded)
+    tile = folded // 4
+    for start in range(0, folded, tile):
         spot = lax.broadcasted_iota(jnp.int32, (tile, row.shape[1]), 0) + start
         spot_ref[start : start + tile, :] = (spot == row).astype(F32).astype(BF16)
 
@@ -153,7 +152,7 @@
         out_shape=[
             jax.ShapeDtypeStruct((blocks, block, slots * block), BF16),
             jax.ShapeDtypeStruct((blocks // 2, slots * block, lanes), BF16),
-            jax.ShapeDtypeStruct((edges // 2, edges), BF16),
+            jax.ShapeDtypeStruct((edges // 4, edges), BF16),
             jax.ShapeDtypeStruct((16, lanes), BF16),
         ],
         scratch_shapes=[
@@ -203,22 +202,26 @@
     lax.fori_loop(0, groups // 2, target, 0, unroll=True)
 
     place = place_ref[...].T
-    turned_half = place >= packed_rows
+    folded = packed_rows // 2
     spread = []
     wide_mask = left_lanes((2 * block, lanes))
+    lane_side = jnp.where(wide_mask, 1.0, 0.0)
     for m in range(groups):
         rows = trip_ref[m * block : (m + 1) * block, :].astype(F32)
         other = turn(rows)
         both = jnp.concatenate([jnp.where(mask, rows, other), jnp.where(mask, other, rows)], axis=0)
-        side = jnp.where(place[:, m : m + 1] < packed_rows, 1.0, 0.0)
-        lane_side = jnp.where(wide_mask, 1.0, 0.0)
-        spread.append(jnp.where(side == lane_side, both, 0.0).astype(BF16))
-    spread = jnp.concatenate(spread, axis=0)
+        column = place[:, m : m + 1]
+        side = jnp.where(column < packed_rows, 1.0, 0.0)
+        column = jnp.where(column < packed_rows, column, column - packed_rows)
+        both = jnp.where(side == lane_side, both, 0.0)
+        sides = [jnp.where(column < folded, both, 0.0), jnp.where(column < folded, 0.0, both)]
+        spread.append(jnp.concatenate(sides, axis=1).astype(BF16))
+    sent = dot(spot_ref[...], jnp.concatenate(spread, axis=0)).astype(BF16)
+    sent = jnp.concatenate([sent[:, :lanes], sent[:, lanes:]], axis=0)
     first = 0
-    for part, sent_ref in zip(parts, sent_refs):
-        rows = slice(first * block, (first + part) * block)
-        sent_ref[...] = dot(spot_ref[rows, :], spread).astype(BF16)
-        first += part
+    for sent_ref in sent_refs:
+        sent_ref[...] = sent[first : first + sent_ref.shape[0]]
+        first += sent_ref.shape[0]
 
 
 def triplet(index, spot, place, angles, pieces, after, block, slots, parts):
@@ -260,8 +263,10 @@
     return jnp.where(left_lanes(even.shape), even, odd)
 
 
-def gate_kernel(block, tile, x_ref, own_ref, up_ref, base_ref, slope_ref):
+def gate_kernel(block, tile, x_ref, own_ref, up_ref, wi_ref, wo_ref, base_ref, slope_ref, wi_half_ref, wo_half_ref):
     up = up_ref[...] * 0.5
+    wi_half_ref[...] = wi_ref[...] * 0.5
+    wo_half_ref[...] = wo_ref[...] * 0.5
     for start in range(0, x_ref.shape[0], tile):
         rows = own_ref[start // 2 : (start + tile) // 2, :]
         value, slope = gated(pre_up(rows, up, block))
@@ -270,7 +275,7 @@
         slope_ref[wide, :] = slope.astype(BF16)
 
 
-def gate(x, own, up, block):
+def gate(x, own, up, wi, wo, block):
     rows, width = x.shape
     return call(
         functools.partial(gate_kernel, block, 8 * block),
@@ -278,13 +283,15 @@
         8 * MIB,
         2 * rows * width * own.shape[1],
         8 * rows * width,
-        in_specs=[VMEM] * 3,
-        out_specs=[VMEM] * 2,
+        in_specs=[VMEM] * 5,
+        out_specs=[VMEM] * 4,
         out_shape=[
             jax.ShapeDtypeStruct((rows, width), F32),
             jax.ShapeDtypeStruct((rows, width), BF16),
+            jax.ShapeDtypeStruct(wi.shape, BF16),
+            jax.ShapeDtypeStruct(wo.shape, BF16),
         ],
-    )(x, own, up)
+    )(x, own, up, wi, wo)
 
 
 def layer_kernel(block, first, far_first, base_ref, ct_ref, far_ref, up_ref, wi_ref, wo_ref, *refs):
@@ -295,7 +302,7 @@
     far = far_ref[far_first * block : far_first * block + rows // 2, :]
     far_value, far_slope = gated(pre_up(far, up, block))
     hidden = base_ref[wide, :] + far_value * 0.5
-    wi, wo = wi_ref[...] * 0.5, wo_ref[...] * 0.5
+    wi, wo = wi_ref[...], wo_ref[...]
     in_value, in_slope = gated(dot(hidden.astype(BF16), wi))
     out_value, out_slope = gated(dot(in_value.astype(BF16), wo))
     held_ref[...] = ((hidden + out_value) * ROOT_HALF).astype(BF16)
@@ -399,18 +406,23 @@
             grad_ref[at : at + block, :] = both.astype(BF16)
     none = jnp.zeros((block, lanes), BF16)
 
-    def target(m, carry):
-        rows = grad_ref[pl.ds(pl.multiple_of(m * block, block), block), :]
-        pair = jnp.concatenate([jnp.where(mask, rows, none), jnp.where(mask, none, rows)], axis=0)
-        terms = dot(angle_ref[m], pair)
-        base = m * (2 * slots)
-        for s in range(slots):
-            term = terms[s * block : (s + 1) * block]
-            total_ref[index_ref[base + s]] += jnp.where(mask, term, 0.0)
-            total_ref[index_ref[base + slots + s]] += jnp.where(mask, 0.0, term)
+    def target(q, carry):
+        sides = []
+        for m in range(2):
+            rows = grad_ref[pl.ds(pl.multiple_of((2 * q + m) * block, block), block), :]
+            pair = jnp.concatenate([jnp.where(mask, rows, none), jnp.where(mask, none, rows)], axis=0)
+            sides.append(jnp.concatenate([jnp.zeros_like(pair)] * m + [pair] + [jnp.zeros_like(pair)] * (1 - m), axis=1))
+        matrix = jnp.concatenate([angle_ref[2 * q], angle_ref[2 * q + 1]], axis=1)
+        every = dot(matrix, jnp.concatenate(sides, axis=0))
+        for m in range(2):
+            base = (2 * q + m) * (2 * slots)
+            for s in range(slots):
+                term = every[s * block : (s + 1) * block, m * lanes : (m + 1) * lanes]
+                total_ref[index_ref[base + s]] += jnp.where(mask, term, 0.0)
+                total_ref[index_ref[base + slots + s]] += jnp.where(mask, 0.0, term)
         return carry
 
-    lax.fori_loop(0, groups, target, 0, unroll=True)
+    lax.fori_loop(0, groups // 2, target, 0, unroll=True)
 
     for piece in range(pieces):
         at = piece * groups
@@ -540,7 +552,7 @@
     pieces = [pieces[d] for d in range(lane_count)]
     trip_own, early, late = triplet(index, spot, place, angle_in, pieces, token, block, slots, sizes)
     early = swapped(early, "cluster", top_bit)
-    base, slope = gate(edge_feats, trip_own, up_weight, block)
+    base, slope, wi, wo = gate(edge_feats, trip_own, up_weight, inner_weight[0], outer_weight[0], block)
     early, late, base, slope = lax.optimization_barrier((early, late, base, slope))
     late = swapped(late, "cluster", top_bit)
     done, grads, far = [], [], []
@@ -550,8 +562,8 @@
             cotangent,
             late if first else early,
             up_weight,
-            inner_weight[0],
-            outer_weight[0],
+            wi,
+            wo,
             done,
             block,
             first,

time: 61.8 us -> 61.2 us (level)
  Pallas kernels: 27.4 us -> 26.3 us
  transfers between devices with their start and end apart: 14 -> 14, of which waited for: 8 -> 8; matrix products, arithmetic and copies ran while one was open for 1% -> 1% of each run, Pallas kernels for 27% -> 26%
where the time goes in v5:
time: 61.2 us; the launch traced here: 61.1 us
  Pallas kernels  26.3 us (43%)
  waiting for transfers between devices  18 us (29%)
  starting transfers between devices  15.4 us (25%)
  between operations  1.01 us (2%)
    ppermute x14, waiting for transfers between devices, swapped(): lax.ppermute(array, axis, [(i, i ^ bit) for i in range(lax.axis_size(axis...  18 us
    ppermute x14, starting transfers between devices, swapped(): lax.ppermute(array, axis, [(i, i ^ bit) for i in range(lax.axis_size(axis...  15.4 us
    pallas_call x3, Pallas kernels, layer(): call(functools.partial(layer_kernel, block, first, far_first), 'layer', 3...  8.24 us
    pallas_call x1, Pallas kernels, scatter(): call(functools.partial(scatter_kernel, block, slots, pieces, chunks), 'sc...  3.93 us
    pallas_call x1, Pallas kernels, ahead(): call(functools.partial(ahead_kernel, block, slots), 'ahead', 20 * MIB, 0,...  3.26 us
    pallas_call x2, Pallas kernels, last(): call(functools.partial(last_kernel, block, len(grads), len(terms), start)...  2.83 us
    pallas_call x1, Pallas kernels, triplet(): call(functools.partial(triplet_kernel, block, slots, count, halves, parts...  2.56 us
    pallas_call x1, Pallas kernels, down(): call(functools.partial(down_kernel, block), 'down', 12 * MIB, 2 * rows *...  2.48 us
  transfers between devices with their start and end apart: 14, of which 8 were waited for; matrix products, arithmetic and copies ran while one was open for 1% of the time, Pallas kernels for 26%

profile of v5, /device:TPU:0, one launch (start us, length us, event | category | flops | bytes accessed | tf_op | source)
XLA Modules:
  0.0 61.1 jit_solution(83492160873580442)
XLA Ops:
  0.6 0.0 copy-start.7
  0.6 0.0 copy-start.9
  0.7 0.0 copy-start.8
  0.7 0.0 copy-start.2
  0.7 2.5 %down.1 = (f32[1024,128]{1,0:T(8,128)S(1)}, bf16[1024,128]{1,0:T(8,128)(2,1)S(1)}) custom-call(bf16[2048,512]{1,0:T(8,128)(2,1)} %x_ref.3, bf16[64,512]{1,0:T(8,128)(2,1)} %bitcast.6), custom_call_target="tpu_custom_call" | custom-call | flops 268435456 | bytes 2097152 | tf_op jit(solution)/shard_map/down/pallas_call | solution.py:88
  3.2 3.0 %collective-permute-start.1 = (bf16[1024,128]{1,0:T(8,128)(2,1)S(1)}, bf16[1024,128]{1,0:T(8,128)(2,1)S(1)}, u32[]{:S(2)}, u32[]{:S(2)}) collective-permute-start(bf16[1024,128]{1,0:T(8,128)(2,1)S(1)} %get-tuple-element.40.refs_0_.refs_4_), channel_id=1, source_target_pairs={{0,2},{1,3},{2,0},{3,1},{4,6},{5,7},{6,4},{7,5},{8,10},{9,11},{10,... | collective-permute-start | bytes 786440 | tf_op jit(solution)/shard_map/ppermute | solution.py:29
  6.2 0.0 collective-permute-start
  6.2 0.0 copy-done.7
  6.3 0.1 copy.15
  6.4 0.1 reshape.14.refs_1_.refs_0_.index_ref
  6.5 3.3 %ahead.1 = (bf16[32,64,512]{2,1,0:T(8,128)(2,1)S(1)}, bf16[16,512,128]{2,1,0:T(8,128)(2,1)S(1)}, bf16[512,2048]{1,0:T(8,128)(2,1)S(1)}, bf16[16,128]{1,0:T(8,128)(2,1)S(1)}) custom-call(bf16[32,8,4096]{2,1,0:T(8,128)(2,1)S(1)} %copy-done.2, s32[1,2048]{1,0:T(1,128)S(1)} %bitcast.11, bf16[1024,128]{1,0:T(8,128)(2,1)S(1)} %get-tuple-element.40.refs_0_.refs_4_, ...), custom_call_target="tpu_custom_call" | custom-call | bytes 16777216 | tf_op jit(solution)/shard_map/ahead/pallas_call | solution.py:144
  9.8 2.7 %collective-permute-done.1.refs_6_ = bf16[1024,128]{1,0:T(8,128)(2,1)S(1)} collective-permute-done((bf16[1024,128]{1,0:T(8,128)(2,1)S(1)}, bf16[1024,128]{1,0:T(8,128)(2,1)S(1)}, u32[]{:S(2)}, u32[]{:S(2)}) %collective-permute-start.1) | collective-permute-done | bytes 262176 | tf_op jit(solution)/shard_map/ppermute | solution.py:29
  12.5 0.0 collective-permute-start.2
  12.5 0.0 collective-permute-done.refs_5_
  12.5 1.5 %collective-permute-done.2.refs_7_ = bf16[1024,128]{1,0:T(8,128)(2,1)S(1)} collective-permute-done((bf16[1024,128]{1,0:T(8,128)(2,1)S(1)}, bf16[1024,128]{1,0:T(8,128)(2,1)S(1)}, u32[]{:S(2)}, u32[]{:S(2)}) %collective-permute-start.2) | collective-permute-done | bytes 262176 | tf_op jit(solution)/shard_map/ppermute | solution.py:29
  14.0 2.6 %triplet.1 = (bf16[1024,128]{1,0:T(8,128)(2,1)S(1)}, bf16[512,128]{1,0:T(8,128)(2,1)S(1)}, bf16[512,128]{1,0:T(8,128)(2,1)S(1)}) custom-call(s32[256]{0:T(256)S(1)} %reshape.14.refs_1_.refs_0_.index_ref, bf16[512,2048]{1,0:T(8,128)(2,1)S(1)} %get-tuple-element.41.refs_1_, s32[16,128]{1,0:T(8,128)S(1)} %fusion.24.refs_2_.place_ref, ...), custom_call_target="tpu_custom_call" | custom-call | flops 134217728 | bytes 8388608 | tf_op jit(solution)/shard_map/triplet/pallas_call | solution.py:233
  16.6 0.0 copy-start
  16.6 2.9 %collective-permute-start.3 = (bf16[512,128]{1,0:T(8,128)(2,1)S(1)}, bf16[512,128]{1,0:T(8,128)(2,1)S(1)}, u32[]{:S(2)}, u32[]{:S(2)}) collective-permute-start(bf16[512,128]{1,0:T(8,128)(2,1)S(1)} %get-tuple-element.46), channel_id=1, source_target_pairs={{0,16},{4,20},{8,24},{12,28},{16,0},{20,4},{24,8},{28,12},{1,17},{... | collective-permute-start | bytes 393224 | tf_op jit(solution)/shard_map/ppermute | solution.py:29
  19.5 0.0 copy-done.3
  19.5 1.9 %gate.1 = (f32[2048,512]{1,0:T(8,128)S(1)}, bf16[2048,512]{1,0:T(8,128)(2,1)S(1)}, bf16[512,512]{1,0:T(8,128)(2,1)S(1)}, bf16[512,512]{1,0:T(8,128)(2,1)S(1)}) custom-call(bf16[2048,512]{1,0:T(8,128)(2,1)S(1)} %copy-done.1, bf16[1024,128]{1,0:T(8,128)(2,1)S(1)} %get-tuple-element.48.own_ref, bf16[64,512]{1,0:T(8,128)(2,1)S(1)} %copy-done.3, ...), custom_call_target="tpu_custom_call" | custom-call | flops 268435456 | bytes 8388608 | tf_op jit(solution)/shard_map/gate/pallas_call | solution.py:280
  21.4 4.7 %collective-permute-done.3.far_ref = bf16[512,128]{1,0:T(8,128)(2,1)S(1)} collective-permute-done((bf16[512,128]{1,0:T(8,128)(2,1)S(1)}, bf16[512,128]{1,0:T(8,128)(2,1)S(1)}, u32[]{:S(2)}, u32[]{:S(2)}) %collective-permute-start.3) | collective-permute-done | bytes 131104 | tf_op jit(solution)/shard_map/ppermute | solution.py:29
  26.1 0.0 collective-permute-start.4
  26.1 3.9 %layer.3 = (bf16[2048,512]{1,0:T(8,128)(2,1)}, bf16[1024,512]{1,0:T(8,128)(2,1)S(1)}, bf16[512,128]{1,0:T(8,128)(2,1)S(1)}) custom-call(f32[2048,512]{1,0:T(8,128)S(1)} %get-tuple-element.51.base_ref, bf16[2048,512]{1,0:T(8,128)(2,1)S(1)} %copy-done, bf16[512,128]{1,0:T(8,128)(2,1)S(1)} %collective-permute-done.3.far_ref, bf16[64,512]{1,0:T(8,128)(2,1)S(1)} %copy-done.3, ...), custom_call_target="tpu_custom_call" | custom-call | tf_op jit(solution)/shard_map/layer/pallas_call | solution.py:323
  30.0 3.0 %collective-permute-start.5 = (bf16[512,128]{1,0:T(8,128)(2,1)S(1)}, bf16[512,128]{1,0:T(8,128)(2,1)S(1)}, u32[]{:S(2)}, u32[]{:S(2)}) collective-permute-start(bf16[512,128]{1,0:T(8,128)(2,1)S(1)} %get-tuple-element.67), channel_id=1, source_target_pairs={{0,16},{4,20},{8,24},{12,28},{16,0},{20,4},{24,8},{28,12},{1,17},{... | collective-permute-start | bytes 393224 | tf_op jit(solution)/shard_map/ppermute | solution.py:29
  33.0 3.0 %collective-permute-done.4.far_ref = bf16[512,128]{1,0:T(8,128)(2,1)S(1)} collective-permute-done((bf16[512,128]{1,0:T(8,128)(2,1)S(1)}, bf16[512,128]{1,0:T(8,128)(2,1)S(1)}, u32[]{:S(2)}, u32[]{:S(2)}) %collective-permute-start.4) | collective-permute-done | bytes 131104 | tf_op jit(solution)/shard_map/ppermute | solution.py:29
  36.0 2.5 %layer.4 = (bf16[2048,512]{1,0:T(8,128)(2,1)}, bf16[640,512]{1,0:T(8,128)(2,1)S(1)}, bf16[320,128]{1,0:T(8,128)(2,1)S(1)}) custom-call(f32[2048,512]{1,0:T(8,128)S(1)} %get-tuple-element.51.base_ref, bf16[2048,512]{1,0:T(8,128)(2,1)S(1)} %copy-done, bf16[512,128]{1,0:T(8,128)(2,1)S(1)} %collective-permute-done.4.far_ref, ...), custom_call_target="tpu_custom_call", output_to_operand_aliasing={{0}: (6, {})} | custom-call | tf_op jit(solution)/shard_map/layer/pallas_call | solution.py:323
  38.6 0.1 collective-permute-start.6
  38.7 1.8 %layer.5 = (bf16[2048,512]{1,0:T(8,128)(2,1)}, bf16[384,512]{1,0:T(8,128)(2,1)S(1)}, bf16[192,128]{1,0:T(8,128)(2,1)S(1)}) custom-call(f32[2048,512]{1,0:T(8,128)S(1)} %get-tuple-element.51.base_ref, bf16[2048,512]{1,0:T(8,128)(2,1)S(1)} %copy-done, bf16[512,128]{1,0:T(8,128)(2,1)S(1)} %collective-permute-done.4.far_ref, ...), custom_call_target="tpu_custom_call", output_to_operand_aliasing={{0}: (6, {})} | custom-call | tf_op jit(solution)/shard_map/layer/pallas_call | solution.py:323
  40.5 3.2 %collective-permute-start.7 = (bf16[192,128]{1,0:T(8,128)(2,1)S(1)}, bf16[192,128]{1,0:T(8,128)(2,1)S(1)}, u32[]{:S(2)}, u32[]{:S(2)}) collective-permute-start(bf16[192,128]{1,0:T(8,128)(2,1)S(1)} %get-tuple-element.69), channel_id=1, source_target_pairs={{0,16},{4,20},{8,24},{12,28},{16,0},{20,4},{24,8},{28,12},{1,17},{... | collective-permute-start | bytes 147464 | tf_op jit(solution)/shard_map/ppermute | solution.py:29
  43.6 1.1 %near.1 = (f32[1024,128]{1,0:T(8,128)S(1)}, bf16[2048,512]{1,0:T(8,128)(2,1)S(1)}) custom-call(bf16[2048,512]{1,0:T(8,128)(2,1)S(1)} %get-tuple-element.62.slope_ref, bf16[64,512]{1,0:T(8,128)(2,1)S(1)} %copy-done.3, s32[16,128]{1,0:T(8,128)S(1)} %fusion.24.refs_2_.place_ref, bf16[1024,512]{1,0:T(8,128)(2,1)S(1)} %get-tuple-element.63.refs_0_, ...), custom_call_target="tpu_custom_call" | custom-call | flops 268435456 | bytes 4194304 | tf_op jit(solution)/shard_map/near/pallas_call | solution.py:364
  44.7 0.0 collective-permute-done.5.refs_0_
  44.8 0.9 %collective-permute-done.7.refs_2_ = bf16[192,128]{1,0:T(8,128)(2,1)S(1)} collective-permute-done((bf16[192,128]{1,0:T(8,128)(2,1)S(1)}, bf16[192,128]{1,0:T(8,128)(2,1)S(1)}, u32[]{:S(2)}, u32[]{:S(2)}) %collective-permute-start.7) | collective-permute-done | bytes 49184 | tf_op jit(solution)/shard_map/ppermute | solution.py:29
  45.7 0.0 collective-permute-done.6.refs_1_
  45.7 3.9 %scatter.1 = (f32[512,128]{1,0:T(8,128)S(1)}, f32[512,128]{1,0:T(8,128)S(1)}, bf16[512,128]{1,0:T(8,128)(2,1)S(1)}, bf16[512,128]{1,0:T(8,128)(2,1)S(1)}, f32[51...) custom-call(s32[256]{0:T(256)S(1)} %reshape.14.refs_1_.refs_0_.index_ref, ...), custom_call_target="tpu_custom_call" | custom-call | flops 134217728 | bytes 8388608 | tf_op jit(solution)/shard_map/scatter/pallas_call | solution.py:444
  49.6 0.1 collective-permute-start.12
  49.7 0.5 collective-permute-start.8
  50.2 0.1 collective-permute-start.9
  50.3 0.4 collective-permute-start.11
  50.7 0.3 collective-permute-done.12
  51.1 1.5 %collective-permute-start.13 = (bf16[512,128]{1,0:T(8,128)(2,1)S(1)}, bf16[512,128]{1,0:T(8,128)(2,1)S(1)}, u32[]{:S(2)}, u32[]{:S(2)}) collective-permute-start(bf16[512,128]{1,0:T(8,128)(2,1)S(1)} %add_convert_fusion), channel_id=1, source_target_pairs={{0,2},{1,3},{2,0},{3,1},{4,6},{5,7},{6,4},{7,5},{8,10},{9,11},{10,... | collective-permute-start | bytes 393224 | tf_op jit(solution)/shard_map/ppermute | solution.py:29
  52.6 0.0 collective-permute-done.9
  52.6 0.6 %collective-permute-start.10 = (bf16[512,128]{1,0:T(8,128)(2,1)S(1)}, bf16[512,128]{1,0:T(8,128)(2,1)S(1)}, u32[]{:S(2)}, u32[]{:S(2)}) collective-permute-start(bf16[512,128]{1,0:T(8,128)(2,1)S(1)} %add_convert_fusion.1), channel_id=1, source_target_pairs={{0,2},{1,3},{2,0},{3,1},{4,6},{5,7},{6,4},{7,5},{8,10},{9,11},{10,... | collective-permute-start | bytes 393224 | tf_op jit(solution)/shard_map/ppermute | solution.py:29
  53.3 0.0 collective-permute-done.11.refs_2_
  53.3 4.2 %collective-permute-done.13.refs_3_ = bf16[512,128]{1,0:T(8,128)(2,1)S(1)} collective-permute-done((bf16[512,128]{1,0:T(8,128)(2,1)S(1)}, bf16[512,128]{1,0:T(8,128)(2,1)S(1)}, u32[]{:S(2)}, u32[]{:S(2)}) %collective-permute-start.13) | collective-permute-done | bytes 131104 | tf_op jit(solution)/shard_map/ppermute | solution.py:29
  57.5 1.4 %last.2.refs_5_ = bf16[2048,512]{1,0:T(8,128)(2,1)} custom-call(f32[1024,128]{1,0:T(8,128)S(1)} %get-tuple-element.59.pre_ref, bf16[64,512]{1,0:T(8,128)(2,1)S(1)} %bitcast.7, bf16[1024,512]{1,0:T(8,128)(2,1)S(1)} %get-tuple-element.63.refs_0_, f32[512,128]{1,0:T(8,128)S(1)} %get-tuple-element.74.refs_1_, ...), custom_call_target="tpu_custom_call" | custom-call | tf_op jit(solution)/shard_map/last/pallas_call | solution.py:486
  58.9 0.0 collective-permute-done.8.refs_3_
  58.9 0.6 collective-permute-done.10.refs_4_
  59.5 1.4 %last.3 = bf16[2048,512]{1,0:T(8,128)(2,1)} custom-call(f32[1024,128]{1,0:T(8,128)S(1)} %get-tuple-element.59.pre_ref, bf16[64,512]{1,0:T(8,128)(2,1)S(1)} %bitcast.8, bf16[640,512]{1,0:T(8,128)(2,1)S(1)} %get-tuple-element.60.refs_1_.refs_0_, bf16[384,512]{1,0:T(8,128)(2,1)S(1)} %get-tuple-element.61.refs_2_.refs_1_, ...), custom_call_target="tpu_custom_call", output_to_operand_aliasing={{}: (7, {})} | custom-call | tf_op jit(solution)/shard_map/last/pallas_call | solution.py:486
  (20 shorter events, 0.2 us)
Async XLA Ops:
  0.6 5.6 %copy-start.7 = (s32[2048]{0:T(1024)S(1)}, s32[2048]{0:T(1024)}, u32[]{:S(2)}) copy-start(s32[2048]{0:T(1024)} %param.17) | copy-start | bytes 24580
  0.6 5.6 %copy-start.9 = (s32[32]{0:T(128)S(1)}, s32[32]{0:T(128)}, u32[]{:S(2)}) copy-start(s32[32]{0:T(128)} %param.19) | copy-start | bytes 388
  0.7 5.6 %copy-start.8 = (s32[32,8]{0,1:T(8,128)S(1)}, s32[32,8]{0,1:T(8,128)}, u32[]{:S(2)}) copy-start(s32[32,8]{0,1:T(8,128)} %param.18) | copy-start | bytes 3076
  0.7 5.8 %copy-start.2 = (bf16[32,8,4096]{2,1,0:T(8,128)(2,1)S(1)}, bf16[32,8,4096]{2,1,0:T(8,128)(2,1)}, u32[]{:S(2)}) copy-start(bf16[32,8,4096]{2,1,0:T(8,128)(2,1)} %angle_ref.1) | copy-start | bytes 6291460
  3.2 9.3 %collective-permute-start.1 = (bf16[1024,128]{1,0:T(8,128)(2,1)S(1)}, bf16[1024,128]{1,0:T(8,128)(2,1)S(1)}, u32[]{:S(2)}, u32[]{:S(2)}) collective-permute-start(bf16[1024,128]{1,0:T(8,128)(2,1)S(1)} %get-tuple-element.40.refs_0_.refs_4_), channel_id=1, source_target_pairs={{0,2},{1,3},{2,0},{3,1},{4,6},{5,7},{6,4},{7,5},{8,10},{9,11},{10,... | collective-permute-start | bytes 786440 | tf_op jit(solution)/shard_map/ppermute | solution.py:29
  6.2 6.3 %collective-permute-start = (bf16[1024,128]{1,0:T(8,128)(2,1)S(1)}, bf16[1024,128]{1,0:T(8,128)(2,1)S(1)}, u32[]{:S(2)}, u32[]{:S(2)}) collective-permute-start(bf16[1024,128]{1,0:T(8,128)(2,1)S(1)} %get-tuple-element.40.refs_0_.refs_4_), channel_id=1, source_target_pairs={{0,1},{1,0},{2,3},{3,2},{4,5},{5,4},{6,7},{7,6},{8,9},{9,8},{10,11... | collective-permute-start | bytes 786440 | tf_op jit(solution)/shard_map/ppermute | solution.py:29
  12.5 1.5 %collective-permute-start.2 = (bf16[1024,128]{1,0:T(8,128)(2,1)S(1)}, bf16[1024,128]{1,0:T(8,128)(2,1)S(1)}, u32[]{:S(2)}, u32[]{:S(2)}) collective-permute-start(bf16[1024,128]{1,0:T(8,128)(2,1)S(1)} %collective-permute-done.1.refs_6_), channel_id=1, source_target_pairs={{0,1},{1,0},{2,3},{3,2},{4,5},{5,4},{6,7},{7,6},{8,9},{9,8},{10,11... | collective-permute-start | bytes 786440 | tf_op jit(solution)/shard_map/ppermute | solution.py:29
  14.0 5.5 %copy-start.1 = (bf16[2048,512]{1,0:T(8,128)(2,1)S(1)}, bf16[2048,512]{1,0:T(8,128)(2,1)}, u32[]{:S(2)}) copy-start(bf16[2048,512]{1,0:T(8,128)(2,1)} %x_ref.3) | copy-start | bytes 6291460
  14.0 5.5 %copy-start.3 = (bf16[64,512]{1,0:T(8,128)(2,1)S(1)}, bf16[64,512]{1,0:T(8,128)(2,1)}, u32[]{:S(2)}) copy-start(bf16[64,512]{1,0:T(8,128)(2,1)} %up_ref.9) | copy-start | bytes 196612
  14.0 5.5 %copy-start.5 = (bf16[1,512,512]{2,1,0:T(8,128)(2,1)S(1)}, bf16[1,512,512]{2,1,0:T(8,128)(2,1)}, u32[]{:S(2)}) copy-start(bf16[1,512,512]{2,1,0:T(8,128)(2,1)} %param.14) | copy-start | bytes 1572868
  14.0 5.5 %copy-start.6 = (bf16[1,512,512]{2,1,0:T(8,128)(2,1)S(1)}, bf16[1,512,512]{2,1,0:T(8,128)(2,1)}, u32[]{:S(2)}) copy-start(bf16[1,512,512]{2,1,0:T(8,128)(2,1)} %param.15) | copy-start | bytes 1572868
  16.6 9.5 %copy-start = (bf16[2048,512]{1,0:T(8,128)(2,1)S(1)}, bf16[2048,512]{1,0:T(8,128)(2,1)}, u32[]{:S(2)}) copy-start(bf16[2048,512]{1,0:T(8,128)(2,1)} %ct_ref.5) | copy-start | bytes 6291460
  16.6 9.5 %collective-permute-start.3 = (bf16[512,128]{1,0:T(8,128)(2,1)S(1)}, bf16[512,128]{1,0:T(8,128)(2,1)S(1)}, u32[]{:S(2)}, u32[]{:S(2)}) collective-permute-start(bf16[512,128]{1,0:T(8,128)(2,1)S(1)} %get-tuple-element.46), channel_id=1, source_target_pairs={{0,16},{4,20},{8,24},{12,28},{16,0},{20,4},{24,8},{28,12},{1,17},{... | collective-permute-start | bytes 393224 | tf_op jit(solution)/shard_map/ppermute | solution.py:29
  26.1 9.9 %collective-permute-start.4 = (bf16[512,128]{1,0:T(8,128)(2,1)S(1)}, bf16[512,128]{1,0:T(8,128)(2,1)S(1)}, u32[]{:S(2)}, u32[]{:S(2)}) collective-permute-start(bf16[512,128]{1,0:T(8,128)(2,1)S(1)} %get-tuple-element.52), channel_id=1, source_target_pairs={{0,16},{4,20},{8,24},{12,28},{16,0},{20,4},{24,8},{28,12},{1,17},{... | collective-permute-start | bytes 393224 | tf_op jit(solution)/shard_map/ppermute | solution.py:29
  30.0 14.7 %collective-permute-start.5 = (bf16[512,128]{1,0:T(8,128)(2,1)S(1)}, bf16[512,128]{1,0:T(8,128)(2,1)S(1)}, u32[]{:S(2)}, u32[]{:S(2)}) collective-permute-start(bf16[512,128]{1,0:T(8,128)(2,1)S(1)} %get-tuple-element.67), channel_id=1, source_target_pairs={{0,16},{4,20},{8,24},{12,28},{16,0},{20,4},{24,8},{28,12},{1,17},{... | collective-permute-start | bytes 393224 | tf_op jit(solution)/shard_map/ppermute | solution.py:29
  38.6 7.1 %collective-permute-start.6 = (bf16[320,128]{1,0:T(8,128)(2,1)S(1)}, bf16[320,128]{1,0:T(8,128)(2,1)S(1)}, u32[]{:S(2)}, u32[]{:S(2)}) collective-permute-start(bf16[320,128]{1,0:T(8,128)(2,1)S(1)} %get-tuple-element.68), channel_id=1, source_target_pairs={{0,16},{4,20},{8,24},{12,28},{16,0},{20,4},{24,8},{28,12},{1,17},{... | collective-permute-start | bytes 245768 | tf_op jit(solution)/shard_map/ppermute | solution.py:29
  40.5 5.2 %collective-permute-start.7 = (bf16[192,128]{1,0:T(8,128)(2,1)S(1)}, bf16[192,128]{1,0:T(8,128)(2,1)S(1)}, u32[]{:S(2)}, u32[]{:S(2)}) collective-permute-start(bf16[192,128]{1,0:T(8,128)(2,1)S(1)} %get-tuple-element.69), channel_id=1, source_target_pairs={{0,16},{4,20},{8,24},{12,28},{16,0},{20,4},{24,8},{28,12},{1,17},{... | collective-permute-start | bytes 147464 | tf_op jit(solution)/shard_map/ppermute | solution.py:29
  45.7 11.8 %copy-start.4 = (bf16[512,64]{0,1:T(8,128)(2,1)S(1)}, bf16[512,64]{0,1:T(8,128)(2,1)}, u32[]{:S(2)}) copy-start(bf16[512,64]{0,1:T(8,128)(2,1)} %param.12) | copy-start | bytes 196612
  49.6 1.4 %collective-permute-start.12 = (bf16[512,128]{1,0:T(8,128)(2,1)S(1)}, bf16[512,128]{1,0:T(8,128)(2,1)S(1)}, u32[]{:S(2)}, u32[]{:S(2)}) collective-permute-start(bf16[512,128]{1,0:T(8,128)(2,1)S(1)} %get-tuple-element.77), channel_id=1, source_target_pairs={{0,1},{1,0},{2,3},{3,2},{4,5},{5,4},{6,7},{7,6},{8,9},{9,8},{10,11... | collective-permute-start | bytes 393224 | tf_op jit(solution)/shard_map/ppermute | solution.py:29
  49.7 9.2 %collective-permute-start.8 = (bf16[512,128]{1,0:T(8,128)(2,1)S(1)}, bf16[512,128]{1,0:T(8,128)(2,1)S(1)}, u32[]{:S(2)}, u32[]{:S(2)}) collective-permute-start(bf16[512,128]{1,0:T(8,128)(2,1)S(1)} %get-tuple-element.71), channel_id=1, source_target_pairs={{0,1},{1,0},{2,3},{3,2},{4,5},{5,4},{6,7},{7,6},{8,9},{9,8},{10,11... | collective-permute-start | bytes 393224 | tf_op jit(solution)/shard_map/ppermute | solution.py:29
  50.2 2.4 %collective-permute-start.9 = (bf16[512,128]{1,0:T(8,128)(2,1)S(1)}, bf16[512,128]{1,0:T(8,128)(2,1)S(1)}, u32[]{:S(2)}, u32[]{:S(2)}) collective-permute-start(bf16[512,128]{1,0:T(8,128)(2,1)S(1)} %get-tuple-element.73), channel_id=1, source_target_pairs={{0,1},{1,0},{2,3},{3,2},{4,5},{5,4},{6,7},{7,6},{8,9},{9,8},{10,11... | collective-permute-start | bytes 393224 | tf_op jit(solution)/shard_map/ppermute | solution.py:29
  50.3 3.0 %collective-permute-start.11 = (bf16[512,128]{1,0:T(8,128)(2,1)S(1)}, bf16[512,128]{1,0:T(8,128)(2,1)S(1)}, u32[]{:S(2)}, u32[]{:S(2)}) collective-permute-start(bf16[512,128]{1,0:T(8,128)(2,1)S(1)} %get-tuple-element.75), channel_id=1, source_target_pairs={{0,1},{1,0},{2,3},{3,2},{4,5},{5,4},{6,7},{7,6},{8,9},{9,8},{10,11... | collective-permute-start | bytes 393224 | tf_op jit(solution)/shard_map/ppermute | solution.py:29
  51.1 6.4 %collective-permute-start.13 = (bf16[512,128]{1,0:T(8,128)(2,1)S(1)}, bf16[512,128]{1,0:T(8,128)(2,1)S(1)}, u32[]{:S(2)}, u32[]{:S(2)}) collective-permute-start(bf16[512,128]{1,0:T(8,128)(2,1)S(1)} %add_convert_fusion), channel_id=1, source_target_pairs={{0,2},{1,3},{2,0},{3,1},{4,6},{5,7},{6,4},{7,5},{8,10},{9,11},{10,... | collective-permute-start | bytes 393224 | tf_op jit(solution)/shard_map/ppermute | solution.py:29
  52.6 6.9 %collective-permute-start.10 = (bf16[512,128]{1,0:T(8,128)(2,1)S(1)}, bf16[512,128]{1,0:T(8,128)(2,1)S(1)}, u32[]{:S(2)}, u32[]{:S(2)}) collective-permute-start(bf16[512,128]{1,0:T(8,128)(2,1)S(1)} %add_convert_fusion.1), channel_id=1, source_target_pairs={{0,2},{1,3},{2,0},{3,1},{4,6},{5,7},{6,4},{7,5},{8,10},{9,11},{10,... | collective-permute-start | bytes 393224 | tf_op jit(solution)/shard_map/ppermute | solution.py:29

commit v6 on v5

--- a/solution.py
+++ b/solution.py
@@ -104,7 +104,7 @@
 
 
 def ahead_kernel(block, slots, angle_ref, row_ref, *refs):
-    in_ref, out_ref, spot_ref, token_ref, rows_ref, pair_ref = refs[-6:]
+    in_ref, spot_ref, token_ref, rows_ref, pair_ref = refs[-5:]
     lanes = 2 * block
     half = block // 2
     mask = left_lanes((half, lanes))
@@ -124,8 +124,6 @@
             first, second = pair_ref[0, p], pair_ref[1, p]
             in_ref[2 * m, :, p * lanes : (p + 1) * lanes] = first.astype(BF16)
             in_ref[2 * m + 1, :, p * lanes : (p + 1) * lanes] = second.astype(BF16)
-            both = jnp.concatenate([first, second], axis=0)
-            out_ref[m, p * lanes : (p + 1) * lanes, :] = both.T.astype(BF16)
         return carry
 
     lax.fori_loop(0, angle_ref.shape[0] // 2, pair, 0, unroll=2)
@@ -148,10 +146,9 @@
         0,
         8 * angular.size * 2,
         in_specs=[VMEM, VMEM] + [ANY] * len(after),
-        out_specs=[VMEM] * 4,
+        out_specs=[VMEM] * 3,
         out_shape=[
             jax.ShapeDtypeStruct((blocks, block, slots * block), BF16),
-            jax.ShapeDtypeStruct((blocks // 2, slots * block, lanes), BF16),
             jax.ShapeDtypeStruct((edges // 4, edges), BF16),
             jax.ShapeDtypeStruct((16, lanes), BF16),
         ],
@@ -160,6 +157,47 @@
             pltpu.VMEM((2, slots // 2, block, lanes), F32),
         ],
     )(angular, row, *after)
+
+
+def beside_kernel(block, angle_ref, place_ref, *refs):
+    out_ref, spot_ref, token_ref = refs[-3:]
+    token_ref[...] = jnp.zeros(token_ref.shape, BF16)
+    lanes = 2 * block
+
+    def pair(m, carry):
+        both = jnp.concatenate([angle_ref[2 * m], angle_ref[2 * m + 1]], axis=0)
+        for p in range(both.shape[1] // lanes):
+            out_ref[m, p * lanes : (p + 1) * lanes, :] = both[:, p * lanes : (p + 1) * lanes].T
+        return carry
+
+    lax.fori_loop(0, out_ref.shape[0], pair, 0, unroll=2)
+    place = place_ref[...].T
+    folded = spot_ref.shape[1]
+    tile = 2 * block
+    for m in range(out_ref.shape[0]):
+        spot = lax.broadcasted_iota(jnp.int32, (tile, folded), 1)
+        column = lax.rem(place[:, m : m + 1], folded)
+        spot_ref[m * tile : (m + 1) * tile, :] = (spot == column).astype(F32).astype(BF16)
+
+
+def beside(angles, place, after, block):
+    blocks, _, width = angles.shape
+    lanes = 2 * block
+    edges = place.size
+    return call(
+        functools.partial(beside_kernel, block),
+        "beside",
+        16 * MIB,
+        0,
+        0,
+        in_specs=[VMEM] * 2 + [ANY],
+        out_specs=[VMEM] * 3,
+        out_shape=[
+            jax.ShapeDtypeStruct((blocks // 2, width, lanes), BF16),
+            jax.ShapeDtypeStruct((edges, edges // 4), BF16),
+            jax.ShapeDtypeStruct((16, lanes), BF16),
+        ],
+    )(angles, place, after)
 
 
 def triplet_kernel(block, slots, pieces, halves, parts, *refs):
@@ -263,7 +301,8 @@
     return jnp.where(left_lanes(even.shape), even, odd)
 
 
-def gate_kernel(block, tile, x_ref, own_ref, up_ref, wi_ref, wo_ref, base_ref, slope_ref, wi_half_ref, wo_half_ref):
+def gate_kernel(block, tile, x_ref, ct_ref, own_ref, up_ref, wi_ref, wo_ref, base_ref, slope_ref, *refs):
+    scaled_ref, wi_half_ref, wo_half_ref = refs
     up = up_ref[...] * 0.5
     wi_half_ref[...] = wi_ref[...] * 0.5
     wo_half_ref[...] = wo_ref[...] * 0.5
@@ -273,9 +312,10 @@
         wide = slice(start, start + tile)
         base_ref[wide, :] = x_ref[wide, :].astype(F32) * ROOT_HALF + value * 0.5
         slope_ref[wide, :] = slope.astype(BF16)
-
-
-def gate(x, own, up, wi, wo, block):
+        scaled_ref[wide, :] = ct_ref[wide, :].astype(F32) * (0.5 * ROOT_HALF)
+
+
+def gate(x, ct, own, up, wi, wo, block):
     rows, width = x.shape
     return call(
         functools.partial(gate_kernel, block, 8 * block),
@@ -283,18 +323,19 @@
         8 * MIB,
         2 * rows * width * own.shape[1],
         8 * rows * width,
-        in_specs=[VMEM] * 5,
-        out_specs=[VMEM] * 4,
+        in_specs=[VMEM] * 6,
+        out_specs=[VMEM] * 5,
         out_shape=[
             jax.ShapeDtypeStruct((rows, width), F32),
             jax.ShapeDtypeStruct((rows, width), BF16),
+            jax.ShapeDtypeStruct((rows, width), F32),
             jax.ShapeDtypeStruct(wi.shape, BF16),
             jax.ShapeDtypeStruct(wo.shape, BF16),
         ],
-    )(x, own, up, wi, wo)
-
-
-def layer_kernel(block, first, far_first, base_ref, ct_ref, far_ref, up_ref, wi_ref, wo_ref, *refs):
+    )(x, ct, own, up, wi, wo)
+
+
+def layer_kernel(block, first, far_first, base_ref, scaled_ref, far_ref, up_ref, wi_ref, wo_ref, *refs):
     out_ref, grad_ref, send_ref, held_ref, sem = refs[-5:]
     rows = grad_ref.shape[0]
     wide = slice(first * 2 * block, first * 2 * block + rows)
@@ -308,7 +349,7 @@
     held_ref[...] = ((hidden + out_value) * ROOT_HALF).astype(BF16)
     copy = pltpu.make_async_copy(held_ref, out_ref.at[wide, :], sem)
     copy.start()
-    scaled = ct_ref[wide, :].astype(F32) * (0.5 * ROOT_HALF)
+    scaled = scaled_ref[wide, :]
     grad_out = (scaled * out_slope).astype(BF16)
     grad_in = (dot_trans(grad_out, wo) * in_slope).astype(BF16)
     half_grad = scaled + dot_trans(grad_in, wi)
@@ -338,17 +379,8 @@
     )(base, ct, far, up, wi, wo, *before)
 
 
-def near_kernel(block, slope_ref, up_ref, place_ref, *refs):
-    near_ref, spot_ref = refs[-2:]
-    packed_rows = near_ref.shape[0]
-    place = place_ref[...].T
-    tile = 2 * block
-    for m in range(packed_rows // block):
-        column = place[:, m : m + 1]
-        folded = spot_ref.shape[1]
-        spot = lax.broadcasted_iota(jnp.int32, (tile, folded), 1)
-        column = lax.rem(column, folded)
-        spot_ref[m * tile : (m + 1) * tile, :] = (spot == column).astype(F32).astype(BF16)
+def near_kernel(block, slope_ref, up_ref, *refs):
+    near_ref = refs[-1]
     up = up_ref[...] * 0.5
     first = 0
     for grad_ref in refs[:-2]:
@@ -358,7 +390,7 @@
         first += rows
 
 
-def near_part(slope, up, place, grads, block):
+def near_part(slope, up, grads, after, block):
     rows, width = slope.shape
     lanes = 2 * up.shape[0]
     return call(
@@ -367,13 +399,10 @@
         8 * MIB,
         2 * rows * width * lanes,
         4 * rows * width,
-        in_specs=[VMEM] * (3 + len(grads)),
-        out_specs=[VMEM] * 2,
-        out_shape=[
-            jax.ShapeDtypeStruct((rows // 2, lanes), F32),
-            jax.ShapeDtypeStruct((rows, rows // 4), BF16),
-        ],
-    )(slope, up, place, *grads)
+        in_specs=[VMEM] * (2 + len(grads)) + [ANY],
+        out_specs=VMEM,
+        out_shape=jax.ShapeDtypeStruct((rows // 2, lanes), F32),
+    )(slope, up, *grads, after)
 
 
 def scatter_kernel(block, slots, pieces, chunks, index_ref, place_ref, spot_ref, angle_ref, near_ref, *refs):
@@ -531,12 +560,12 @@
     place_row = place.reshape(1, local_edges)
     place = place.reshape(groups, 2 * block)
 
-    cuts = [0, groups * 8 // 16, groups * 13 // 16, groups]
+    cuts = [0, groups * 9 // 16, groups * 13 // 16, groups]
     parts = [end - start for start, end in zip(cuts, cuts[1:])]
     sizes = [parts[0], groups - parts[0]]
 
     pre_down, *trip = down(edge_feats, down_trans, block, [groups])
-    angle_in, angle_out, spot, token = ahead(angular, place_row, [trip[0], index, place], block)
+    angle_in, spot, token = ahead(angular, place_row, [trip[0], index, place], block)
     pieces = {0: trip}
     bits = [1 << i for i in range(lane_count.bit_length() - 1)]
     for bit in reversed(bits):
@@ -552,14 +581,17 @@
     pieces = [pieces[d] for d in range(lane_count)]
     trip_own, early, late = triplet(index, spot, place, angle_in, pieces, token, block, slots, sizes)
     early = swapped(early, "cluster", top_bit)
-    base, slope, wi, wo = gate(edge_feats, trip_own, up_weight, inner_weight[0], outer_weight[0], block)
-    early, late, base, slope = lax.optimization_barrier((early, late, base, slope))
+    base, slope, scaled, wi, wo = gate(
+        edge_feats, cotangent, trip_own, up_weight, inner_weight[0], outer_weight[0], block
+    )
+    angle_out, spot, token = beside(angle_in, place, trip_own, block)
+    late, base, slope, token = lax.optimization_barrier((late, base, slope, token))
     late = swapped(late, "cluster", top_bit)
     done, grads, far = [], [], []
     for first, part in zip(cuts, parts):
         output, grad, sent = layer(
             base,
-            cotangent,
+            scaled,
             late if first else early,
             up_weight,
             wi,
@@ -573,7 +605,7 @@
         done = [output]
         grads.append(grad)
         far.append(swapped(sent, "cluster", top_bit))
-    near, spot = near_part(slope, up_weight, place, grads, block)
+    near = near_part(slope, up_weight, grads, token, block)
     types = [BF16 if d % 2 else F32 for d in range(lane_count)]
     sums = scatter(index, place, spot, angle_out, near, far, types, sizes, block, slots)
     sums = {d: sums[len(sizes) * d : len(sizes) * (d + 1)] for d in range(lane_count)}

time: 61.2 us -> 59.9 us (0.979)
  starting transfers between devices: 15.4 us -> 12.5 us
  Pallas kernels: 26.3 us -> 27.2 us
    ppermute x14, starting transfers between devices: 15.4 us -> 12.5 us  [swapped(): lax.ppermute(array, axis, [(i, i ^ bit) for i in range(lax.axis_size(axis...]
    pallas_call x0 -> x1, Pallas kernels: none -> 1.57 us  [beside(): call(functools.partial(beside_kernel, block), 'beside', 16 * MIB, 0, 0, i...]
    pallas_call x1, Pallas kernels: 3.26 us -> 2.53 us  [ahead(): call(functools.partial(ahead_kernel, block, slots), 'ahead', 20 * MIB, 0,...]
  transfers between devices with their start and end apart: 14 -> 14, of which waited for: 8 -> 8; matrix products, arithmetic and copies ran while one was open for 1% -> 1% of each run, Pallas kernels for 26% -> 28%
where the time goes in v6:
time: 59.9 us; the launch traced here: 59.3 us
  Pallas kernels  27.2 us (45%)
  waiting for transfers between devices  18.2 us (30%)
  starting transfers between devices  12.5 us (21%)
  between operations  1.07 us (2%)
    ppermute x14, waiting for transfers between devices, swapped(): lax.ppermute(array, axis, [(i, i ^ bit) for i in range(lax.axis_size(axis...  18.2 us
    ppermute x14, starting transfers between devices, swapped(): lax.ppermute(array, axis, [(i, i ^ bit) for i in range(lax.axis_size(axis...  12.5 us
    pallas_call x3, Pallas kernels, layer(): call(functools.partial(layer_kernel, block, first, far_first), 'layer', 3...  8.16 us
    pallas_call x1, Pallas kernels, scatter(): call(functools.partial(scatter_kernel, block, slots, pieces, chunks), 'sc...  4.09 us
    pallas_call x2, Pallas kernels, last(): call(functools.partial(last_kernel, block, len(grads), len(terms), start)...  2.86 us
    pallas_call x1, Pallas kernels, triplet(): call(functools.partial(triplet_kernel, block, slots, count, halves, parts...  2.55 us
    pallas_call x1, Pallas kernels, ahead(): call(functools.partial(ahead_kernel, block, slots), 'ahead', 20 * MIB, 0,...  2.53 us
    pallas_call x1, Pallas kernels, down(): call(functools.partial(down_kernel, block), 'down', 12 * MIB, 2 * rows *...  2.48 us
  transfers between devices with their start and end apart: 14, of which 8 were waited for; matrix products, arithmetic and copies ran while one was open for 1% of the time, Pallas kernels for 28%

profile of v6, /device:TPU:0, one launch (start us, length us, event | category | flops | bytes accessed | tf_op | source)
XLA Modules:
  0.0 59.3 jit_solution(9489114236074633506)
XLA Ops:
  0.6 0.0 copy-start.7
  0.6 0.0 copy-start.9
  0.7 0.0 copy-start.8
  0.7 0.0 copy-start.1
  0.7 2.5 %down.1 = (f32[1024,128]{1,0:T(8,128)S(1)}, bf16[1024,128]{1,0:T(8,128)(2,1)S(1)}) custom-call(bf16[2048,512]{1,0:T(8,128)(2,1)} %x_ref.3, bf16[64,512]{1,0:T(8,128)(2,1)} %bitcast.6), custom_call_target="tpu_custom_call" | custom-call | flops 268435456 | bytes 2097152 | tf_op jit(solution)/shard_map/down/pallas_call | solution.py:88
  3.2 3.0 %collective-permute-start.1 = (bf16[1024,128]{1,0:T(8,128)(2,1)S(1)}, bf16[1024,128]{1,0:T(8,128)(2,1)S(1)}, u32[]{:S(2)}, u32[]{:S(2)}) collective-permute-start(bf16[1024,128]{1,0:T(8,128)(2,1)S(1)} %get-tuple-element.41.refs_0_.refs_4_), channel_id=1, source_target_pairs={{0,2},{1,3},{2,0},{3,1},{4,6},{5,7},{6,4},{7,5},{8,10},{9,11},{10,... | collective-permute-start | bytes 786440 | tf_op jit(solution)/shard_map/ppermute | solution.py:29
  6.2 0.0 collective-permute-start
  6.3 0.1 copy.15
  6.4 0.1 reshape.14.refs_1_.refs_0_.index_ref
  6.5 2.5 %ahead.1 = (bf16[32,64,512]{2,1,0:T(8,128)(2,1)S(1)}, bf16[512,2048]{1,0:T(8,128)(2,1)S(1)}, bf16[16,128]{1,0:T(8,128)(2,1)S(1)}) custom-call(bf16[32,8,4096]{2,1,0:T(8,128)(2,1)S(1)} %copy-done.1, s32[1,2048]{1,0:T(1,128)S(1)} %bitcast.11, bf16[1024,128]{1,0:T(8,128)(2,1)S(1)} %get-tuple-element.41.refs_0_.refs_4_, ...), custom_call_target="tpu_custom_call" | custom-call | bytes 16777216 | tf_op jit(solution)/shard_map/ahead/pallas_call | solution.py:142
  9.1 3.4 %collective-permute-done.1.refs_6_ = bf16[1024,128]{1,0:T(8,128)(2,1)S(1)} collective-permute-done((bf16[1024,128]{1,0:T(8,128)(2,1)S(1)}, bf16[1024,128]{1,0:T(8,128)(2,1)S(1)}, u32[]{:S(2)}, u32[]{:S(2)}) %collective-permute-start.1) | collective-permute-done | bytes 262176 | tf_op jit(solution)/shard_map/ppermute | solution.py:29
  12.5 0.0 collective-permute-start.2
  12.5 0.0 collective-permute-done.refs_5_
  12.5 1.5 %collective-permute-done.2.refs_7_ = bf16[1024,128]{1,0:T(8,128)(2,1)S(1)} collective-permute-done((bf16[1024,128]{1,0:T(8,128)(2,1)S(1)}, bf16[1024,128]{1,0:T(8,128)(2,1)S(1)}, u32[]{:S(2)}, u32[]{:S(2)}) %collective-permute-start.2) | collective-permute-done | bytes 262176 | tf_op jit(solution)/shard_map/ppermute | solution.py:29
  14.0 2.5 %triplet.1 = (bf16[1024,128]{1,0:T(8,128)(2,1)S(1)}, bf16[576,128]{1,0:T(8,128)(2,1)S(1)}, bf16[448,128]{1,0:T(8,128)(2,1)S(1)}) custom-call(s32[256]{0:T(256)S(1)} %reshape.14.refs_1_.refs_0_.index_ref, bf16[512,2048]{1,0:T(8,128)(2,1)S(1)} %get-tuple-element.42.refs_1_, s32[16,128]{1,0:T(8,128)S(1)} %fusion.24.refs_2_.place_ref, ...), custom_call_target="tpu_custom_call" | custom-call | flops 134217728 | bytes 8388608 | tf_op jit(solution)/shard_map/triplet/pallas_call | solution.py:271
  16.6 0.0 copy-start
  16.6 0.0 copy-start.3
  16.6 2.9 %collective-permute-start.4 = (bf16[576,128]{1,0:T(8,128)(2,1)S(1)}, bf16[576,128]{1,0:T(8,128)(2,1)S(1)}, u32[]{:S(2)}, u32[]{:S(2)}) collective-permute-start(bf16[576,128]{1,0:T(8,128)(2,1)S(1)} %get-tuple-element.57), channel_id=1, source_target_pairs={{0,16},{4,20},{8,24},{12,28},{16,0},{20,4},{24,8},{28,12},{1,17},{... | collective-permute-start | bytes 442376 | tf_op jit(solution)/shard_map/ppermute | solution.py:29
  19.5 1.6 %beside.1 = (bf16[16,512,128]{2,1,0:T(8,128)(2,1)S(1)}, bf16[2048,512]{1,0:T(8,128)(2,1)S(1)}, bf16[16,128]{1,0:T(8,128)(2,1)S(1)}) custom-call(bf16[32,64,512]{2,1,0:T(8,128)(2,1)S(1)} %get-tuple-element.43.refs_3_.angle_ref, s32[16,128]{1,0:T(8,128)S(1)} %fusion.24.refs_2_.place_ref, bf16[1024,128]{1,0:T(8,128)(2,1)S(1)} %get-tuple-element.48.own_ref.refs_0_), custom_call_target="tpu_custom_call" | custom-call | tf_op jit(solution)/shard_map/beside/pallas_call | solution.py:187
  21.1 2.2 %gate.1 = (f32[2048,512]{1,0:T(8,128)S(1)}, bf16[2048,512]{1,0:T(8,128)(2,1)S(1)}, f32[2048,512]{1,0:T(8,128)S(1)}, bf16[512,512]{1,0:T(8,128)(2,1)S(1)}, bf16[512,512]{1,0:T(8,128)(2,1)S(1)}) custom-call(bf16[2048,512]{1,0:T(8,128)(2,1)S(1)} %copy-done, bf16[2048,512]{1,0:T(8,128)(2,1)S(1)} %copy-done.2, ...), custom_call_target="tpu_custom_call" | custom-call | flops 268435456 | bytes 8388608 | tf_op jit(solution)/shard_map/gate/pallas_call | solution.py:320
  23.4 0.2 collective-permute-start.3
  23.5 3.3 %collective-permute-done.4.far_ref = bf16[576,128]{1,0:T(8,128)(2,1)S(1)} collective-permute-done((bf16[576,128]{1,0:T(8,128)(2,1)S(1)}, bf16[576,128]{1,0:T(8,128)(2,1)S(1)}, u32[]{:S(2)}, u32[]{:S(2)}) %collective-permute-start.4) | collective-permute-done | bytes 147488 | tf_op jit(solution)/shard_map/ppermute | solution.py:29
  26.8 4.3 %layer.3 = (bf16[2048,512]{1,0:T(8,128)(2,1)}, bf16[1152,512]{1,0:T(8,128)(2,1)S(1)}, bf16[576,128]{1,0:T(8,128)(2,1)S(1)}) custom-call(f32[2048,512]{1,0:T(8,128)S(1)} %get-tuple-element.52.base_ref, f32[2048,512]{1,0:T(8,128)S(1)} %get-tuple-element.53.scaled_ref, bf16[576,128]{1,0:T(8,128)(2,1)S(1)} %collective-permute-done.4.far_ref, ...), custom_call_target="tpu_custom_call" | custom-call | tf_op jit(solution)/shard_map/layer/pallas_call | solution.py:364
  31.2 0.1 collective-permute-start.5
  31.2 0.5 collective-permute-done.3.far_ref
  31.7 2.1 %layer.4 = (bf16[2048,512]{1,0:T(8,128)(2,1)}, bf16[512,512]{1,0:T(8,128)(2,1)S(1)}, bf16[256,128]{1,0:T(8,128)(2,1)S(1)}) custom-call(f32[2048,512]{1,0:T(8,128)S(1)} %get-tuple-element.52.base_ref, f32[2048,512]{1,0:T(8,128)S(1)} %get-tuple-element.53.scaled_ref, ...), custom_call_target="tpu_custom_call", output_to_operand_aliasing={{0}: (6, {})} | custom-call | tf_op jit(solution)/shard_map/layer/pallas_call | solution.py:364
  33.8 2.5 %collective-permute-start.6 = (bf16[256,128]{1,0:T(8,128)(2,1)S(1)}, bf16[256,128]{1,0:T(8,128)(2,1)S(1)}, u32[]{:S(2)}, u32[]{:S(2)}) collective-permute-start(bf16[256,128]{1,0:T(8,128)(2,1)S(1)} %get-tuple-element.70), channel_id=1, source_target_pairs={{0,16},{4,20},{8,24},{12,28},{16,0},{20,4},{24,8},{28,12},{1,17},{... | collective-permute-start | bytes 196616 | tf_op jit(solution)/shard_map/ppermute | solution.py:29
  36.3 1.8 %layer.5 = (bf16[2048,512]{1,0:T(8,128)(2,1)}, bf16[384,512]{1,0:T(8,128)(2,1)S(1)}, bf16[192,128]{1,0:T(8,128)(2,1)S(1)}) custom-call(f32[2048,512]{1,0:T(8,128)S(1)} %get-tuple-element.52.base_ref, f32[2048,512]{1,0:T(8,128)S(1)} %get-tuple-element.53.scaled_ref, ...), custom_call_target="tpu_custom_call", output_to_operand_aliasing={{0}: (6, {})} | custom-call | tf_op jit(solution)/shard_map/layer/pallas_call | solution.py:364
  38.1 0.6 collective-permute-start.7
  38.6 0.7 %near.1.near_ref = f32[1024,128]{1,0:T(8,128)S(1)} custom-call(bf16[2048,512]{1,0:T(8,128)(2,1)S(1)} %get-tuple-element.66.slope_ref, bf16[64,512]{1,0:T(8,128)(2,1)S(1)} %copy-done.3, bf16[1152,512]{1,0:T(8,128)(2,1)S(1)} %get-tuple-element.67.refs_0_, bf16[512,512]{1,0:T(8,128)(2,1)S(1)} %get-tuple-element.62.refs_1_.refs_0_, ...), custom_call_target="tpu_custom_call" | custom-call | flops 268435456 | bytes 4194304 | tf_op jit(solution)/shard_map/near/pallas_call | solution.py:396
  39.4 4.5 %collective-permute-done.7.refs_2_ = bf16[192,128]{1,0:T(8,128)(2,1)S(1)} collective-permute-done((bf16[192,128]{1,0:T(8,128)(2,1)S(1)}, bf16[192,128]{1,0:T(8,128)(2,1)S(1)}, u32[]{:S(2)}, u32[]{:S(2)}) %collective-permute-start.7) | collective-permute-done | bytes 49184 | tf_op jit(solution)/shard_map/ppermute | solution.py:29
  43.8 0.0 collective-permute-done.6.refs_1_
  43.8 0.0 collective-permute-done.5.refs_0_
  43.8 4.1 %scatter.1 = (f32[576,128]{1,0:T(8,128)S(1)}, f32[448,128]{1,0:T(8,128)S(1)}, bf16[576,128]{1,0:T(8,128)(2,1)S(1)}, bf16[448,128]{1,0:T(8,128)(2,1)S(1)}, f32[57...) custom-call(s32[256]{0:T(256)S(1)} %reshape.14.refs_1_.refs_0_.index_ref, ...), custom_call_target="tpu_custom_call" | custom-call | flops 134217728 | bytes 8388608 | tf_op jit(solution)/shard_map/scatter/pallas_call | solution.py:473
  47.9 0.1 collective-permute-start.12
  48.0 0.5 collective-permute-start.8
  48.5 0.1 collective-permute-start.9
  48.6 0.4 collective-permute-start.11
  49.0 0.3 collective-permute-done.12
  49.4 1.6 %collective-permute-start.13 = (bf16[576,128]{1,0:T(8,128)(2,1)S(1)}, bf16[576,128]{1,0:T(8,128)(2,1)S(1)}, u32[]{:S(2)}, u32[]{:S(2)}) collective-permute-start(bf16[576,128]{1,0:T(8,128)(2,1)S(1)} %add_convert_fusion), channel_id=1, source_target_pairs={{0,2},{1,3},{2,0},{3,1},{4,6},{5,7},{6,4},{7,5},{8,10},{9,11},{10,... | collective-permute-start | bytes 442376 | tf_op jit(solution)/shard_map/ppermute | solution.py:29
  51.0 0.0 collective-permute-done.9
  51.0 0.6 %collective-permute-start.10 = (bf16[448,128]{1,0:T(8,128)(2,1)S(1)}, bf16[448,128]{1,0:T(8,128)(2,1)S(1)}, u32[]{:S(2)}, u32[]{:S(2)}) collective-permute-start(bf16[448,128]{1,0:T(8,128)(2,1)S(1)} %add_convert_fusion.1), channel_id=1, source_target_pairs={{0,2},{1,3},{2,0},{3,1},{4,6},{5,7},{6,4},{7,5},{8,10},{9,11},{10,... | collective-permute-start | bytes 344072 | tf_op jit(solution)/shard_map/ppermute | solution.py:29
  51.6 0.0 collective-permute-done.11.refs_2_
  51.6 4.6 %collective-permute-done.13.refs_3_ = bf16[576,128]{1,0:T(8,128)(2,1)S(1)} collective-permute-done((bf16[576,128]{1,0:T(8,128)(2,1)S(1)}, bf16[576,128]{1,0:T(8,128)(2,1)S(1)}, u32[]{:S(2)}, u32[]{:S(2)}) %collective-permute-start.13) | collective-permute-done | bytes 147488 | tf_op jit(solution)/shard_map/ppermute | solution.py:29
  56.2 1.5 %last.2.refs_5_ = bf16[2048,512]{1,0:T(8,128)(2,1)} custom-call(f32[1024,128]{1,0:T(8,128)S(1)} %get-tuple-element.61.pre_ref, bf16[64,512]{1,0:T(8,128)(2,1)S(1)} %bitcast.7, bf16[1152,512]{1,0:T(8,128)(2,1)S(1)} %get-tuple-element.67.refs_0_, f32[576,128]{1,0:T(8,128)S(1)} %get-tuple-element.76.refs_1_, ...), custom_call_target="tpu_custom_call" | custom-call | tf_op jit(solution)/shard_map/last/pallas_call | solution.py:515
  57.7 0.0 collective-permute-done.8.refs_3_
  57.7 0.1 collective-permute-done.10.refs_4_
  57.8 1.3 %last.3 = bf16[2048,512]{1,0:T(8,128)(2,1)} custom-call(f32[1024,128]{1,0:T(8,128)S(1)} %get-tuple-element.61.pre_ref, bf16[64,512]{1,0:T(8,128)(2,1)S(1)} %bitcast.8, bf16[512,512]{1,0:T(8,128)(2,1)S(1)} %get-tuple-element.62.refs_1_.refs_0_, bf16[384,512]{1,0:T(8,128)(2,1)S(1)} %get-tuple-element.63.refs_2_.refs_1_, ...), custom_call_target="tpu_custom_call", output_to_operand_aliasing={{}: (7, {})} | custom-call | tf_op jit(solution)/shard_map/last/pallas_call | solution.py:515
  (21 shorter events, 0.2 us)
Async XLA Ops:
  0.6 5.6 %copy-start.7 = (s32[2048]{0:T(1024)S(1)}, s32[2048]{0:T(1024)}, u32[]{:S(2)}) copy-start(s32[2048]{0:T(1024)} %param.17) | copy-start | bytes 24580
  0.6 5.6 %copy-start.9 = (s32[32]{0:T(128)S(1)}, s32[32]{0:T(128)}, u32[]{:S(2)}) copy-start(s32[32]{0:T(128)} %param.19) | copy-start | bytes 388
  0.7 5.6 %copy-start.8 = (s32[32,8]{0,1:T(8,128)S(1)}, s32[32,8]{0,1:T(8,128)}, u32[]{:S(2)}) copy-start(s32[32,8]{0,1:T(8,128)} %param.18) | copy-start | bytes 3076
  0.7 5.8 %copy-start.1 = (bf16[32,8,4096]{2,1,0:T(8,128)(2,1)S(1)}, bf16[32,8,4096]{2,1,0:T(8,128)(2,1)}, u32[]{:S(2)}) copy-start(bf16[32,8,4096]{2,1,0:T(8,128)(2,1)} %angle_ref.1) | copy-start | bytes 6291460
  3.2 9.3 %collective-permute-start.1 = (bf16[1024,128]{1,0:T(8,128)(2,1)S(1)}, bf16[1024,128]{1,0:T(8,128)(2,1)S(1)}, u32[]{:S(2)}, u32[]{:S(2)}) collective-permute-start(bf16[1024,128]{1,0:T(8,128)(2,1)S(1)} %get-tuple-element.41.refs_0_.refs_4_), channel_id=1, source_target_pairs={{0,2},{1,3},{2,0},{3,1},{4,6},{5,7},{6,4},{7,5},{8,10},{9,11},{10,... | collective-permute-start | bytes 786440 | tf_op jit(solution)/shard_map/ppermute | solution.py:29
  6.2 6.3 %collective-permute-start = (bf16[1024,128]{1,0:T(8,128)(2,1)S(1)}, bf16[1024,128]{1,0:T(8,128)(2,1)S(1)}, u32[]{:S(2)}, u32[]{:S(2)}) collective-permute-start(bf16[1024,128]{1,0:T(8,128)(2,1)S(1)} %get-tuple-element.41.refs_0_.refs_4_), channel_id=1, source_target_pairs={{0,1},{1,0},{2,3},{3,2},{4,5},{5,4},{6,7},{7,6},{8,9},{9,8},{10,11... | collective-permute-start | bytes 786440 | tf_op jit(solution)/shard_map/ppermute | solution.py:29
  12.5 1.5 %collective-permute-start.2 = (bf16[1024,128]{1,0:T(8,128)(2,1)S(1)}, bf16[1024,128]{1,0:T(8,128)(2,1)S(1)}, u32[]{:S(2)}, u32[]{:S(2)}) collective-permute-start(bf16[1024,128]{1,0:T(8,128)(2,1)S(1)} %collective-permute-done.1.refs_6_), channel_id=1, source_target_pairs={{0,1},{1,0},{2,3},{3,2},{4,5},{5,4},{6,7},{7,6},{8,9},{9,8},{10,11... | collective-permute-start | bytes 786440 | tf_op jit(solution)/shard_map/ppermute | solution.py:29
  14.0 7.1 %copy-start.2 = (bf16[2048,512]{1,0:T(8,128)(2,1)S(1)}, bf16[2048,512]{1,0:T(8,128)(2,1)}, u32[]{:S(2)}) copy-start(bf16[2048,512]{1,0:T(8,128)(2,1)} %ct_ref.1) | copy-start | bytes 6291460
  14.0 7.1 %copy-start.5 = (bf16[1,512,512]{2,1,0:T(8,128)(2,1)S(1)}, bf16[1,512,512]{2,1,0:T(8,128)(2,1)}, u32[]{:S(2)}) copy-start(bf16[1,512,512]{2,1,0:T(8,128)(2,1)} %param.14) | copy-start | bytes 1572868
  14.0 7.1 %copy-start.6 = (bf16[1,512,512]{2,1,0:T(8,128)(2,1)S(1)}, bf16[1,512,512]{2,1,0:T(8,128)(2,1)}, u32[]{:S(2)}) copy-start(bf16[1,512,512]{2,1,0:T(8,128)(2,1)} %param.15) | copy-start | bytes 1572868
  16.6 4.5 %copy-start = (bf16[2048,512]{1,0:T(8,128)(2,1)S(1)}, bf16[2048,512]{1,0:T(8,128)(2,1)}, u32[]{:S(2)}) copy-start(bf16[2048,512]{1,0:T(8,128)(2,1)} %x_ref.3) | copy-start | bytes 6291460
  16.6 4.5 %copy-start.3 = (bf16[64,512]{1,0:T(8,128)(2,1)S(1)}, bf16[64,512]{1,0:T(8,128)(2,1)}, u32[]{:S(2)}) copy-start(bf16[64,512]{1,0:T(8,128)(2,1)} %up_ref.9) | copy-start | bytes 196612
  16.6 10.2 %collective-permute-start.4 = (bf16[576,128]{1,0:T(8,128)(2,1)S(1)}, bf16[576,128]{1,0:T(8,128)(2,1)S(1)}, u32[]{:S(2)}, u32[]{:S(2)}) collective-permute-start(bf16[576,128]{1,0:T(8,128)(2,1)S(1)} %get-tuple-element.57), channel_id=1, source_target_pairs={{0,16},{4,20},{8,24},{12,28},{16,0},{20,4},{24,8},{28,12},{1,17},{... | collective-permute-start | bytes 442376 | tf_op jit(solution)/shard_map/ppermute | solution.py:29
  23.4 8.4 %collective-permute-start.3 = (bf16[448,128]{1,0:T(8,128)(2,1)S(1)}, bf16[448,128]{1,0:T(8,128)(2,1)S(1)}, u32[]{:S(2)}, u32[]{:S(2)}) collective-permute-start(bf16[448,128]{1,0:T(8,128)(2,1)S(1)} %get-tuple-element.54), channel_id=1, source_target_pairs={{0,16},{4,20},{8,24},{12,28},{16,0},{20,4},{24,8},{28,12},{1,17},{... | collective-permute-start | bytes 344072 | tf_op jit(solution)/shard_map/ppermute | solution.py:29
  31.2 12.7 %collective-permute-start.5 = (bf16[576,128]{1,0:T(8,128)(2,1)S(1)}, bf16[576,128]{1,0:T(8,128)(2,1)S(1)}, u32[]{:S(2)}, u32[]{:S(2)}) collective-permute-start(bf16[576,128]{1,0:T(8,128)(2,1)S(1)} %get-tuple-element.69), channel_id=1, source_target_pairs={{0,16},{4,20},{8,24},{12,28},{16,0},{20,4},{24,8},{28,12},{1,17},{... | collective-permute-start | bytes 442376 | tf_op jit(solution)/shard_map/ppermute | solution.py:29
  33.8 10.0 %collective-permute-start.6 = (bf16[256,128]{1,0:T(8,128)(2,1)S(1)}, bf16[256,128]{1,0:T(8,128)(2,1)S(1)}, u32[]{:S(2)}, u32[]{:S(2)}) collective-permute-start(bf16[256,128]{1,0:T(8,128)(2,1)S(1)} %get-tuple-element.70), channel_id=1, source_target_pairs={{0,16},{4,20},{8,24},{12,28},{16,0},{20,4},{24,8},{28,12},{1,17},{... | collective-permute-start | bytes 196616 | tf_op jit(solution)/shard_map/ppermute | solution.py:29
  38.1 5.8 %collective-permute-start.7 = (bf16[192,128]{1,0:T(8,128)(2,1)S(1)}, bf16[192,128]{1,0:T(8,128)(2,1)S(1)}, u32[]{:S(2)}, u32[]{:S(2)}) collective-permute-start(bf16[192,128]{1,0:T(8,128)(2,1)S(1)} %get-tuple-element.71), channel_id=1, source_target_pairs={{0,16},{4,20},{8,24},{12,28},{16,0},{20,4},{24,8},{28,12},{1,17},{... | collective-permute-start | bytes 147464 | tf_op jit(solution)/shard_map/ppermute | solution.py:29
  43.8 12.3 %copy-start.4 = (bf16[512,64]{0,1:T(8,128)(2,1)S(1)}, bf16[512,64]{0,1:T(8,128)(2,1)}, u32[]{:S(2)}) copy-start(bf16[512,64]{0,1:T(8,128)(2,1)} %param.12) | copy-start | bytes 196612
  47.9 1.4 %collective-permute-start.12 = (bf16[576,128]{1,0:T(8,128)(2,1)S(1)}, bf16[576,128]{1,0:T(8,128)(2,1)S(1)}, u32[]{:S(2)}, u32[]{:S(2)}) collective-permute-start(bf16[576,128]{1,0:T(8,128)(2,1)S(1)} %get-tuple-element.79), channel_id=1, source_target_pairs={{0,1},{1,0},{2,3},{3,2},{4,5},{5,4},{6,7},{7,6},{8,9},{9,8},{10,11... | collective-permute-start | bytes 442376 | tf_op jit(solution)/shard_map/ppermute | solution.py:29
  48.0 9.7 %collective-permute-start.8 = (bf16[448,128]{1,0:T(8,128)(2,1)S(1)}, bf16[448,128]{1,0:T(8,128)(2,1)S(1)}, u32[]{:S(2)}, u32[]{:S(2)}) collective-permute-start(bf16[448,128]{1,0:T(8,128)(2,1)S(1)} %get-tuple-element.73), channel_id=1, source_target_pairs={{0,1},{1,0},{2,3},{3,2},{4,5},{5,4},{6,7},{7,6},{8,9},{9,8},{10,11... | collective-permute-start | bytes 344072 | tf_op jit(solution)/shard_map/ppermute | solution.py:29
  48.5 2.5 %collective-permute-start.9 = (bf16[448,128]{1,0:T(8,128)(2,1)S(1)}, bf16[448,128]{1,0:T(8,128)(2,1)S(1)}, u32[]{:S(2)}, u32[]{:S(2)}) collective-permute-start(bf16[448,128]{1,0:T(8,128)(2,1)S(1)} %get-tuple-element.75), channel_id=1, source_target_pairs={{0,1},{1,0},{2,3},{3,2},{4,5},{5,4},{6,7},{7,6},{8,9},{9,8},{10,11... | collective-permute-start | bytes 344072 | tf_op jit(solution)/shard_map/ppermute | solution.py:29
  48.6 3.0 %collective-permute-start.11 = (bf16[576,128]{1,0:T(8,128)(2,1)S(1)}, bf16[576,128]{1,0:T(8,128)(2,1)S(1)}, u32[]{:S(2)}, u32[]{:S(2)}) collective-permute-start(bf16[576,128]{1,0:T(8,128)(2,1)S(1)} %get-tuple-element.77), channel_id=1, source_target_pairs={{0,1},{1,0},{2,3},{3,2},{4,5},{5,4},{6,7},{7,6},{8,9},{9,8},{10,11... | collective-permute-start | bytes 442376 | tf_op jit(solution)/shard_map/ppermute | solution.py:29
  49.4 6.8 %collective-permute-start.13 = (bf16[576,128]{1,0:T(8,128)(2,1)S(1)}, bf16[576,128]{1,0:T(8,128)(2,1)S(1)}, u32[]{:S(2)}, u32[]{:S(2)}) collective-permute-start(bf16[576,128]{1,0:T(8,128)(2,1)S(1)} %add_convert_fusion), channel_id=1, source_target_pairs={{0,2},{1,3},{2,0},{3,1},{4,6},{5,7},{6,4},{7,5},{8,10},{9,11},{10,... | collective-permute-start | bytes 442376 | tf_op jit(solution)/shard_map/ppermute | solution.py:29
  51.0 6.8 %collective-permute-start.10 = (bf16[448,128]{1,0:T(8,128)(2,1)S(1)}, bf16[448,128]{1,0:T(8,128)(2,1)S(1)}, u32[]{:S(2)}, u32[]{:S(2)}) collective-permute-start(bf16[448,128]{1,0:T(8,128)(2,1)S(1)} %add_convert_fusion.1), channel_id=1, source_target_pairs={{0,2},{1,3},{2,0},{3,1},{4,6},{5,7},{6,4},{7,5},{8,10},{9,11},{10,... | collective-permute-start | bytes 344072 | tf_op jit(solution)/shard_map/ppermute | solution.py:29

commit v7 on v6

--- a/solution.py
+++ b/solution.py
@@ -488,24 +488,26 @@
 
 def last_kernel(block, grads, terms, start, pre_ref, wt_ref, *refs):
     grad_refs, term_refs = refs[:grads], refs[grads : grads + terms]
-    out_ref, held_ref, sem = refs[-3:]
-    rows = held_ref.shape[0]
-    thin = slice(start // 2, (start + rows) // 2)
+    out_ref, held_ref, sems = refs[-3:]
+    groups = held_ref.shape[0] // (2 * block)
     left, right = padded(wt_ref[...])
-    total = term_refs[0][...].astype(F32)
-    for ref in term_refs[1:]:
-        total = total + ref[...].astype(F32)
-    _, slope = gated(pre_ref[thin, :] * 0.5)
-    grad = (total * (0.5 * slope)).astype(BF16)
-    both = join_pairs(dot(grad, left), dot(grad, right), block)
-    first = 0
-    for grad_ref in grad_refs:
-        here = slice(first, first + grad_ref.shape[0])
-        held_ref[here, :] = (grad_ref[...].astype(F32) + both[here]).astype(BF16)
-        first += grad_ref.shape[0]
-    copy = pltpu.make_async_copy(held_ref, out_ref.at[start : start + rows, :], sem)
-    copy.start()
-    copy.wait()
+    grad_rows = jnp.concatenate([grad_ref[...] for grad_ref in grad_refs], axis=0)
+    copies = []
+    for i, (low, high) in enumerate([(0, (groups + 1) // 2), ((groups + 1) // 2, groups)]):
+        thin = slice(low * block, high * block)
+        wide = slice(2 * low * block, 2 * high * block)
+        total = term_refs[0][thin, :].astype(F32)
+        for ref in term_refs[1:]:
+            total = total + ref[thin, :].astype(F32)
+        _, slope = gated(pre_ref[start // 2 + low * block : start // 2 + high * block, :] * 0.5)
+        grad = (total * (0.5 * slope)).astype(BF16)
+        both = join_pairs(dot(grad, left), dot(grad, right), block)
+        held_ref[wide, :] = (grad_rows[wide].astype(F32) + both).astype(BF16)
+        there = out_ref.at[start + 2 * low * block : start + 2 * high * block, :]
+        copies.append(pltpu.make_async_copy(held_ref.at[wide, :], there, sems.at[i]))
+        copies[-1].start()
+    for copy in copies:
+        copy.wait()
 
 
 def last(pre, grads, wt, terms, before, block, start):
@@ -521,7 +523,7 @@
         in_specs=[VMEM] * len(inputs) + [HBM] * len(before),
         out_specs=HBM,
         out_shape=jax.ShapeDtypeStruct((rows, width), BF16),
-        scratch_shapes=[pltpu.VMEM((here, width), BF16), pltpu.SemaphoreType.DMA(())],
+        scratch_shapes=[pltpu.VMEM((here, width), BF16), pltpu.SemaphoreType.DMA((2,))],
         input_output_aliases={len(inputs): 0} if before else {},
     )(*inputs, *before)
 

time: 59.9 us -> 59.9 us (level)
  no operation moved by 1% of the time
where the time goes in v7:
time: 59.9 us; the launch traced here: 59.2 us
  Pallas kernels  26.9 us (45%)
  waiting for transfers between devices  18.4 us (31%)
  starting transfers between devices  12.5 us (21%)
  between operations  1.07 us (2%)
    ppermute x14, waiting for transfers between devices, swapped(): lax.ppermute(array, axis, [(i, i ^ bit) for i in range(lax.axis_size(axis...  18.4 us
    ppermute x14, starting transfers between devices, swapped(): lax.ppermute(array, axis, [(i, i ^ bit) for i in range(lax.axis_size(axis...  12.5 us
    pallas_call x3, Pallas kernels, layer(): call(functools.partial(layer_kernel, block, first, far_first), 'layer', 3...  8.16 us
    pallas_call x1, Pallas kernels, scatter(): call(functools.partial(scatter_kernel, block, slots, pieces, chunks), 'sc...  4.02 us
    pallas_call x2, Pallas kernels, last(): call(functools.partial(last_kernel, block, len(grads), len(terms), start)...  2.61 us
    pallas_call x1, Pallas kernels, triplet(): call(functools.partial(triplet_kernel, block, slots, count, halves, parts...  2.55 us
    pallas_call x1, Pallas kernels, ahead(): call(functools.partial(ahead_kernel, block, slots), 'ahead', 20 * MIB, 0,...  2.53 us
    pallas_call x1, Pallas kernels, down(): call(functools.partial(down_kernel, block), 'down', 12 * MIB, 2 * rows *...  2.48 us
  transfers between devices with their start and end apart: 14, of which 8 were waited for; matrix products, arithmetic and copies ran while one was open for 1% of the time, Pallas kernels for 28%

profile of v7, /device:TPU:0, one launch (start us, length us, event | category | flops | bytes accessed | tf_op | source)
XLA Modules:
  0.0 59.2 jit_solution(1459381611182294077)
XLA Ops:
  0.6 0.0 copy-start.7
  0.6 0.0 copy-start.9
  0.7 0.0 copy-start.8
  0.7 2.5 %down.1 = (f32[1024,128]{1,0:T(8,128)S(1)}, bf16[1024,128]{1,0:T(8,128)(2,1)S(1)}) custom-call(bf16[2048,512]{1,0:T(8,128)(2,1)} %x_ref.3, bf16[64,512]{1,0:T(8,128)(2,1)} %bitcast.6), custom_call_target="tpu_custom_call" | custom-call | flops 268435456 | bytes 2097152 | tf_op jit(solution)/shard_map/down/pallas_call | solution.py:88
  3.2 3.0 %collective-permute-start.1 = (bf16[1024,128]{1,0:T(8,128)(2,1)S(1)}, bf16[1024,128]{1,0:T(8,128)(2,1)S(1)}, u32[]{:S(2)}, u32[]{:S(2)}) collective-permute-start(bf16[1024,128]{1,0:T(8,128)(2,1)S(1)} %get-tuple-element.41.refs_0_.refs_4_), channel_id=1, source_target_pairs={{0,2},{1,3},{2,0},{3,1},{4,6},{5,7},{6,4},{7,5},{8,10},{9,11},{10,... | collective-permute-start | bytes 786440 | tf_op jit(solution)/shard_map/ppermute | solution.py:29
  6.2 0.0 collective-permute-start
  6.3 0.1 copy.15
  6.4 0.1 reshape.14.refs_1_.refs_0_.index_ref
  6.5 2.5 %ahead.1 = (bf16[32,64,512]{2,1,0:T(8,128)(2,1)S(1)}, bf16[512,2048]{1,0:T(8,128)(2,1)S(1)}, bf16[16,128]{1,0:T(8,128)(2,1)S(1)}) custom-call(bf16[32,8,4096]{2,1,0:T(8,128)(2,1)S(1)} %copy-done.1, s32[1,2048]{1,0:T(1,128)S(1)} %bitcast.11, bf16[1024,128]{1,0:T(8,128)(2,1)S(1)} %get-tuple-element.41.refs_0_.refs_4_, ...), custom_call_target="tpu_custom_call" | custom-call | bytes 16777216 | tf_op jit(solution)/shard_map/ahead/pallas_call | solution.py:142
  9.1 3.4 %collective-permute-done.1.refs_6_ = bf16[1024,128]{1,0:T(8,128)(2,1)S(1)} collective-permute-done((bf16[1024,128]{1,0:T(8,128)(2,1)S(1)}, bf16[1024,128]{1,0:T(8,128)(2,1)S(1)}, u32[]{:S(2)}, u32[]{:S(2)}) %collective-permute-start.1) | collective-permute-done | bytes 262176 | tf_op jit(solution)/shard_map/ppermute | solution.py:29
  12.5 0.0 collective-permute-start.2
  12.5 0.0 collective-permute-done.refs_5_
  12.5 1.5 %collective-permute-done.2.refs_7_ = bf16[1024,128]{1,0:T(8,128)(2,1)S(1)} collective-permute-done((bf16[1024,128]{1,0:T(8,128)(2,1)S(1)}, bf16[1024,128]{1,0:T(8,128)(2,1)S(1)}, u32[]{:S(2)}, u32[]{:S(2)}) %collective-permute-start.2) | collective-permute-done | bytes 262176 | tf_op jit(solution)/shard_map/ppermute | solution.py:29
  14.0 2.5 %triplet.1 = (bf16[1024,128]{1,0:T(8,128)(2,1)S(1)}, bf16[576,128]{1,0:T(8,128)(2,1)S(1)}, bf16[448,128]{1,0:T(8,128)(2,1)S(1)}) custom-call(s32[256]{0:T(256)S(1)} %reshape.14.refs_1_.refs_0_.index_ref, bf16[512,2048]{1,0:T(8,128)(2,1)S(1)} %get-tuple-element.42.refs_1_, s32[16,128]{1,0:T(8,128)S(1)} %fusion.24.refs_2_.place_ref, ...), custom_call_target="tpu_custom_call" | custom-call | flops 134217728 | bytes 8388608 | tf_op jit(solution)/shard_map/triplet/pallas_call | solution.py:271
  16.6 0.0 copy-start
  16.6 0.0 copy-start.3
  16.6 2.9 %collective-permute-start.4 = (bf16[576,128]{1,0:T(8,128)(2,1)S(1)}, bf16[576,128]{1,0:T(8,128)(2,1)S(1)}, u32[]{:S(2)}, u32[]{:S(2)}) collective-permute-start(bf16[576,128]{1,0:T(8,128)(2,1)S(1)} %get-tuple-element.57), channel_id=1, source_target_pairs={{0,16},{4,20},{8,24},{12,28},{16,0},{20,4},{24,8},{28,12},{1,17},{... | collective-permute-start | bytes 442376 | tf_op jit(solution)/shard_map/ppermute | solution.py:29
  19.5 1.6 %beside.1 = (bf16[16,512,128]{2,1,0:T(8,128)(2,1)S(1)}, bf16[2048,512]{1,0:T(8,128)(2,1)S(1)}, bf16[16,128]{1,0:T(8,128)(2,1)S(1)}) custom-call(bf16[32,64,512]{2,1,0:T(8,128)(2,1)S(1)} %get-tuple-element.43.refs_3_.angle_ref, s32[16,128]{1,0:T(8,128)S(1)} %fusion.24.refs_2_.place_ref, bf16[1024,128]{1,0:T(8,128)(2,1)S(1)} %get-tuple-element.48.own_ref.refs_0_), custom_call_target="tpu_custom_call" | custom-call | tf_op jit(solution)/shard_map/beside/pallas_call | solution.py:187
  21.1 2.2 %gate.1 = (f32[2048,512]{1,0:T(8,128)S(1)}, bf16[2048,512]{1,0:T(8,128)(2,1)S(1)}, f32[2048,512]{1,0:T(8,128)S(1)}, bf16[512,512]{1,0:T(8,128)(2,1)S(1)}, bf16[512,512]{1,0:T(8,128)(2,1)S(1)}) custom-call(bf16[2048,512]{1,0:T(8,128)(2,1)S(1)} %copy-done, bf16[2048,512]{1,0:T(8,128)(2,1)S(1)} %copy-done.2, ...), custom_call_target="tpu_custom_call" | custom-call | flops 268435456 | bytes 8388608 | tf_op jit(solution)/shard_map/gate/pallas_call | solution.py:320
  23.4 0.2 collective-permute-start.3
  23.5 3.3 %collective-permute-done.4.far_ref = bf16[576,128]{1,0:T(8,128)(2,1)S(1)} collective-permute-done((bf16[576,128]{1,0:T(8,128)(2,1)S(1)}, bf16[576,128]{1,0:T(8,128)(2,1)S(1)}, u32[]{:S(2)}, u32[]{:S(2)}) %collective-permute-start.4) | collective-permute-done | bytes 147488 | tf_op jit(solution)/shard_map/ppermute | solution.py:29
  26.8 4.3 %layer.3 = (bf16[2048,512]{1,0:T(8,128)(2,1)}, bf16[1152,512]{1,0:T(8,128)(2,1)S(1)}, bf16[576,128]{1,0:T(8,128)(2,1)S(1)}) custom-call(f32[2048,512]{1,0:T(8,128)S(1)} %get-tuple-element.52.base_ref, f32[2048,512]{1,0:T(8,128)S(1)} %get-tuple-element.53.scaled_ref, bf16[576,128]{1,0:T(8,128)(2,1)S(1)} %collective-permute-done.4.far_ref, ...), custom_call_target="tpu_custom_call" | custom-call | tf_op jit(solution)/shard_map/layer/pallas_call | solution.py:364
  31.2 0.1 collective-permute-start.5
  31.2 0.5 collective-permute-done.3.far_ref
  31.7 2.1 %layer.4 = (bf16[2048,512]{1,0:T(8,128)(2,1)}, bf16[512,512]{1,0:T(8,128)(2,1)S(1)}, bf16[256,128]{1,0:T(8,128)(2,1)S(1)}) custom-call(f32[2048,512]{1,0:T(8,128)S(1)} %get-tuple-element.52.base_ref, f32[2048,512]{1,0:T(8,128)S(1)} %get-tuple-element.53.scaled_ref, ...), custom_call_target="tpu_custom_call", output_to_operand_aliasing={{0}: (6, {})} | custom-call | tf_op jit(solution)/shard_map/layer/pallas_call | solution.py:364
  33.8 2.5 %collective-permute-start.6 = (bf16[256,128]{1,0:T(8,128)(2,1)S(1)}, bf16[256,128]{1,0:T(8,128)(2,1)S(1)}, u32[]{:S(2)}, u32[]{:S(2)}) collective-permute-start(bf16[256,128]{1,0:T(8,128)(2,1)S(1)} %get-tuple-element.70), channel_id=1, source_target_pairs={{0,16},{4,20},{8,24},{12,28},{16,0},{20,4},{24,8},{28,12},{1,17},{... | collective-permute-start | bytes 196616 | tf_op jit(solution)/shard_map/ppermute | solution.py:29
  36.3 1.8 %layer.5 = (bf16[2048,512]{1,0:T(8,128)(2,1)}, bf16[384,512]{1,0:T(8,128)(2,1)S(1)}, bf16[192,128]{1,0:T(8,128)(2,1)S(1)}) custom-call(f32[2048,512]{1,0:T(8,128)S(1)} %get-tuple-element.52.base_ref, f32[2048,512]{1,0:T(8,128)S(1)} %get-tuple-element.53.scaled_ref, ...), custom_call_target="tpu_custom_call", output_to_operand_aliasing={{0}: (6, {})} | custom-call | tf_op jit(solution)/shard_map/layer/pallas_call | solution.py:364
  38.1 0.6 collective-permute-start.7
  38.6 0.7 %near.1.near_ref = f32[1024,128]{1,0:T(8,128)S(1)} custom-call(bf16[2048,512]{1,0:T(8,128)(2,1)S(1)} %get-tuple-element.66.slope_ref, bf16[64,512]{1,0:T(8,128)(2,1)S(1)} %copy-done.3, bf16[1152,512]{1,0:T(8,128)(2,1)S(1)} %get-tuple-element.67.refs_0_, bf16[512,512]{1,0:T(8,128)(2,1)S(1)} %get-tuple-element.62.refs_1_.refs_0_, ...), custom_call_target="tpu_custom_call" | custom-call | flops 268435456 | bytes 4194304 | tf_op jit(solution)/shard_map/near/pallas_call | solution.py:396
  39.4 4.5 %collective-permute-done.7.refs_2_ = bf16[192,128]{1,0:T(8,128)(2,1)S(1)} collective-permute-done((bf16[192,128]{1,0:T(8,128)(2,1)S(1)}, bf16[192,128]{1,0:T(8,128)(2,1)S(1)}, u32[]{:S(2)}, u32[]{:S(2)}) %collective-permute-start.7) | collective-permute-done | bytes 49184 | tf_op jit(solution)/shard_map/ppermute | solution.py:29
  43.8 0.0 collective-permute-done.6.refs_1_
  43.8 0.0 collective-permute-done.5.refs_0_
  43.8 4.0 %scatter.1 = (f32[576,128]{1,0:T(8,128)S(1)}, f32[448,128]{1,0:T(8,128)S(1)}, bf16[576,128]{1,0:T(8,128)(2,1)S(1)}, bf16[448,128]{1,0:T(8,128)(2,1)S(1)}, f32[57...) custom-call(s32[256]{0:T(256)S(1)} %reshape.14.refs_1_.refs_0_.index_ref, ...), custom_call_target="tpu_custom_call" | custom-call | flops 134217728 | bytes 8388608 | tf_op jit(solution)/shard_map/scatter/pallas_call | solution.py:473
  47.9 0.1 collective-permute-start.12
  47.9 0.5 collective-permute-start.8
  48.4 0.1 collective-permute-start.9
  48.5 0.4 collective-permute-start.11
  48.9 0.3 collective-permute-done.12
  49.3 1.7 %collective-permute-start.13 = (bf16[576,128]{1,0:T(8,128)(2,1)S(1)}, bf16[576,128]{1,0:T(8,128)(2,1)S(1)}, u32[]{:S(2)}, u32[]{:S(2)}) collective-permute-start(bf16[576,128]{1,0:T(8,128)(2,1)S(1)} %add_convert_fusion), channel_id=1, source_target_pairs={{0,2},{1,3},{2,0},{3,1},{4,6},{5,7},{6,4},{7,5},{8,10},{9,11},{10,... | collective-permute-start | bytes 442376 | tf_op jit(solution)/shard_map/ppermute | solution.py:29
  51.0 0.0 collective-permute-done.9
  51.0 0.5 collective-permute-start.10
  51.5 0.0 collective-permute-done.11.refs_2_
  51.5 4.6 %collective-permute-done.13.refs_3_ = bf16[576,128]{1,0:T(8,128)(2,1)S(1)} collective-permute-done((bf16[576,128]{1,0:T(8,128)(2,1)S(1)}, bf16[576,128]{1,0:T(8,128)(2,1)S(1)}, u32[]{:S(2)}, u32[]{:S(2)}) %collective-permute-start.13) | collective-permute-done | bytes 147488 | tf_op jit(solution)/shard_map/ppermute | solution.py:29
  56.1 0.0 copy-done.4
  56.1 1.4 %last.2.refs_5_ = bf16[2048,512]{1,0:T(8,128)(2,1)} custom-call(f32[1024,128]{1,0:T(8,128)S(1)} %get-tuple-element.61.pre_ref, bf16[64,512]{1,0:T(8,128)(2,1)S(1)} %bitcast.7, bf16[1152,512]{1,0:T(8,128)(2,1)S(1)} %get-tuple-element.67.refs_0_, f32[576,128]{1,0:T(8,128)S(1)} %get-tuple-element.76.refs_1_, ...), custom_call_target="tpu_custom_call" | custom-call | tf_op jit(solution)/shard_map/last/pallas_call | solution.py:517
  57.5 0.0 collective-permute-done.8.refs_3_
  57.5 0.3 collective-permute-done.10.refs_4_
  57.8 1.2 %last.3 = bf16[2048,512]{1,0:T(8,128)(2,1)} custom-call(f32[1024,128]{1,0:T(8,128)S(1)} %get-tuple-element.61.pre_ref, bf16[64,512]{1,0:T(8,128)(2,1)S(1)} %bitcast.8, bf16[512,512]{1,0:T(8,128)(2,1)S(1)} %get-tuple-element.62.refs_1_.refs_0_, bf16[384,512]{1,0:T(8,128)(2,1)S(1)} %get-tuple-element.63.refs_2_.refs_1_, ...), custom_call_target="tpu_custom_call", output_to_operand_aliasing={{}: (7, {})} | custom-call | tf_op jit(solution)/shard_map/last/pallas_call | solution.py:517
  (21 shorter events, 0.2 us)
Async XLA Ops:
  0.6 5.6 %copy-start.7 = (s32[2048]{0:T(1024)S(1)}, s32[2048]{0:T(1024)}, u32[]{:S(2)}) copy-start(s32[2048]{0:T(1024)} %param.17) | copy-start | bytes 24580
  0.6 5.6 %copy-start.9 = (s32[32]{0:T(128)S(1)}, s32[32]{0:T(128)}, u32[]{:S(2)}) copy-start(s32[32]{0:T(128)} %param.19) | copy-start | bytes 388
  0.7 5.6 %copy-start.8 = (s32[32,8]{0,1:T(8,128)S(1)}, s32[32,8]{0,1:T(8,128)}, u32[]{:S(2)}) copy-start(s32[32,8]{0,1:T(8,128)} %param.18) | copy-start | bytes 3076
  0.7 5.8 %copy-start.1 = (bf16[32,8,4096]{2,1,0:T(8,128)(2,1)S(1)}, bf16[32,8,4096]{2,1,0:T(8,128)(2,1)}, u32[]{:S(2)}) copy-start(bf16[32,8,4096]{2,1,0:T(8,128)(2,1)} %angle_ref.1) | copy-start | bytes 6291460
  3.2 9.3 %collective-permute-start.1 = (bf16[1024,128]{1,0:T(8,128)(2,1)S(1)}, bf16[1024,128]{1,0:T(8,128)(2,1)S(1)}, u32[]{:S(2)}, u32[]{:S(2)}) collective-permute-start(bf16[1024,128]{1,0:T(8,128)(2,1)S(1)} %get-tuple-element.41.refs_0_.refs_4_), channel_id=1, source_target_pairs={{0,2},{1,3},{2,0},{3,1},{4,6},{5,7},{6,4},{7,5},{8,10},{9,11},{10,... | collective-permute-start | bytes 786440 | tf_op jit(solution)/shard_map/ppermute | solution.py:29
  6.2 6.3 %collective-permute-start = (bf16[1024,128]{1,0:T(8,128)(2,1)S(1)}, bf16[1024,128]{1,0:T(8,128)(2,1)S(1)}, u32[]{:S(2)}, u32[]{:S(2)}) collective-permute-start(bf16[1024,128]{1,0:T(8,128)(2,1)S(1)} %get-tuple-element.41.refs_0_.refs_4_), channel_id=1, source_target_pairs={{0,1},{1,0},{2,3},{3,2},{4,5},{5,4},{6,7},{7,6},{8,9},{9,8},{10,11... | collective-permute-start | bytes 786440 | tf_op jit(solution)/shard_map/ppermute | solution.py:29
  12.5 1.5 %collective-permute-start.2 = (bf16[1024,128]{1,0:T(8,128)(2,1)S(1)}, bf16[1024,128]{1,0:T(8,128)(2,1)S(1)}, u32[]{:S(2)}, u32[]{:S(2)}) collective-permute-start(bf16[1024,128]{1,0:T(8,128)(2,1)S(1)} %collective-permute-done.1.refs_6_), channel_id=1, source_target_pairs={{0,1},{1,0},{2,3},{3,2},{4,5},{5,4},{6,7},{7,6},{8,9},{9,8},{10,11... | collective-permute-start | bytes 786440 | tf_op jit(solution)/shard_map/ppermute | solution.py:29
  14.0 7.1 %copy-start.2 = (bf16[2048,512]{1,0:T(8,128)(2,1)S(1)}, bf16[2048,512]{1,0:T(8,128)(2,1)}, u32[]{:S(2)}) copy-start(bf16[2048,512]{1,0:T(8,128)(2,1)} %ct_ref.1) | copy-start | bytes 6291460
  14.0 7.1 %copy-start.5 = (bf16[1,512,512]{2,1,0:T(8,128)(2,1)S(1)}, bf16[1,512,512]{2,1,0:T(8,128)(2,1)}, u32[]{:S(2)}) copy-start(bf16[1,512,512]{2,1,0:T(8,128)(2,1)} %param.14) | copy-start | bytes 1572868
  14.0 7.1 %copy-start.6 = (bf16[1,512,512]{2,1,0:T(8,128)(2,1)S(1)}, bf16[1,512,512]{2,1,0:T(8,128)(2,1)}, u32[]{:S(2)}) copy-start(bf16[1,512,512]{2,1,0:T(8,128)(2,1)} %param.15) | copy-start | bytes 1572868
  16.6 4.5 %copy-start = (bf16[2048,512]{1,0:T(8,128)(2,1)S(1)}, bf16[2048,512]{1,0:T(8,128)(2,1)}, u32[]{:S(2)}) copy-start(bf16[2048,512]{1,0:T(8,128)(2,1)} %x_ref.3) | copy-start | bytes 6291460
  16.6 4.5 %copy-start.3 = (bf16[64,512]{1,0:T(8,128)(2,1)S(1)}, bf16[64,512]{1,0:T(8,128)(2,1)}, u32[]{:S(2)}) copy-start(bf16[64,512]{1,0:T(8,128)(2,1)} %up_ref.9) | copy-start | bytes 196612
  16.6 10.2 %collective-permute-start.4 = (bf16[576,128]{1,0:T(8,128)(2,1)S(1)}, bf16[576,128]{1,0:T(8,128)(2,1)S(1)}, u32[]{:S(2)}, u32[]{:S(2)}) collective-permute-start(bf16[576,128]{1,0:T(8,128)(2,1)S(1)} %get-tuple-element.57), channel_id=1, source_target_pairs={{0,16},{4,20},{8,24},{12,28},{16,0},{20,4},{24,8},{28,12},{1,17},{... | collective-permute-start | bytes 442376 | tf_op jit(solution)/shard_map/ppermute | solution.py:29
  23.4 8.4 %collective-permute-start.3 = (bf16[448,128]{1,0:T(8,128)(2,1)S(1)}, bf16[448,128]{1,0:T(8,128)(2,1)S(1)}, u32[]{:S(2)}, u32[]{:S(2)}) collective-permute-start(bf16[448,128]{1,0:T(8,128)(2,1)S(1)} %get-tuple-element.54), channel_id=1, source_target_pairs={{0,16},{4,20},{8,24},{12,28},{16,0},{20,4},{24,8},{28,12},{1,17},{... | collective-permute-start | bytes 344072 | tf_op jit(solution)/shard_map/ppermute | solution.py:29
  31.2 12.7 %collective-permute-start.5 = (bf16[576,128]{1,0:T(8,128)(2,1)S(1)}, bf16[576,128]{1,0:T(8,128)(2,1)S(1)}, u32[]{:S(2)}, u32[]{:S(2)}) collective-permute-start(bf16[576,128]{1,0:T(8,128)(2,1)S(1)} %get-tuple-element.69), channel_id=1, source_target_pairs={{0,16},{4,20},{8,24},{12,28},{16,0},{20,4},{24,8},{28,12},{1,17},{... | collective-permute-start | bytes 442376 | tf_op jit(solution)/shard_map/ppermute | solution.py:29
  33.8 10.0 %collective-permute-start.6 = (bf16[256,128]{1,0:T(8,128)(2,1)S(1)}, bf16[256,128]{1,0:T(8,128)(2,1)S(1)}, u32[]{:S(2)}, u32[]{:S(2)}) collective-permute-start(bf16[256,128]{1,0:T(8,128)(2,1)S(1)} %get-tuple-element.70), channel_id=1, source_target_pairs={{0,16},{4,20},{8,24},{12,28},{16,0},{20,4},{24,8},{28,12},{1,17},{... | collective-permute-start | bytes 196616 | tf_op jit(solution)/shard_map/ppermute | solution.py:29
  38.1 5.8 %collective-permute-start.7 = (bf16[192,128]{1,0:T(8,128)(2,1)S(1)}, bf16[192,128]{1,0:T(8,128)(2,1)S(1)}, u32[]{:S(2)}, u32[]{:S(2)}) collective-permute-start(bf16[192,128]{1,0:T(8,128)(2,1)S(1)} %get-tuple-element.71), channel_id=1, source_target_pairs={{0,16},{4,20},{8,24},{12,28},{16,0},{20,4},{24,8},{28,12},{1,17},{... | collective-permute-start | bytes 147464 | tf_op jit(solution)/shard_map/ppermute | solution.py:29
  43.8 12.3 %copy-start.4 = (bf16[512,64]{0,1:T(8,128)(2,1)S(1)}, bf16[512,64]{0,1:T(8,128)(2,1)}, u32[]{:S(2)}) copy-start(bf16[512,64]{0,1:T(8,128)(2,1)} %param.12) | copy-start | bytes 196612
  47.9 1.4 %collective-permute-start.12 = (bf16[576,128]{1,0:T(8,128)(2,1)S(1)}, bf16[576,128]{1,0:T(8,128)(2,1)S(1)}, u32[]{:S(2)}, u32[]{:S(2)}) collective-permute-start(bf16[576,128]{1,0:T(8,128)(2,1)S(1)} %get-tuple-element.79), channel_id=1, source_target_pairs={{0,1},{1,0},{2,3},{3,2},{4,5},{5,4},{6,7},{7,6},{8,9},{9,8},{10,11... | collective-permute-start | bytes 442376 | tf_op jit(solution)/shard_map/ppermute | solution.py:29
  47.9 9.6 %collective-permute-start.8 = (bf16[448,128]{1,0:T(8,128)(2,1)S(1)}, bf16[448,128]{1,0:T(8,128)(2,1)S(1)}, u32[]{:S(2)}, u32[]{:S(2)}) collective-permute-start(bf16[448,128]{1,0:T(8,128)(2,1)S(1)} %get-tuple-element.73), channel_id=1, source_target_pairs={{0,1},{1,0},{2,3},{3,2},{4,5},{5,4},{6,7},{7,6},{8,9},{9,8},{10,11... | collective-permute-start | bytes 344072 | tf_op jit(solution)/shard_map/ppermute | solution.py:29
  48.4 2.6 %collective-permute-start.9 = (bf16[448,128]{1,0:T(8,128)(2,1)S(1)}, bf16[448,128]{1,0:T(8,128)(2,1)S(1)}, u32[]{:S(2)}, u32[]{:S(2)}) collective-permute-start(bf16[448,128]{1,0:T(8,128)(2,1)S(1)} %get-tuple-element.75), channel_id=1, source_target_pairs={{0,1},{1,0},{2,3},{3,2},{4,5},{5,4},{6,7},{7,6},{8,9},{9,8},{10,11... | collective-permute-start | bytes 344072 | tf_op jit(solution)/shard_map/ppermute | solution.py:29
  48.5 3.0 %collective-permute-start.11 = (bf16[576,128]{1,0:T(8,128)(2,1)S(1)}, bf16[576,128]{1,0:T(8,128)(2,1)S(1)}, u32[]{:S(2)}, u32[]{:S(2)}) collective-permute-start(bf16[576,128]{1,0:T(8,128)(2,1)S(1)} %get-tuple-element.77), channel_id=1, source_target_pairs={{0,1},{1,0},{2,3},{3,2},{4,5},{5,4},{6,7},{7,6},{8,9},{9,8},{10,11... | collective-permute-start | bytes 442376 | tf_op jit(solution)/shard_map/ppermute | solution.py:29
  49.3 6.8 %collective-permute-start.13 = (bf16[576,128]{1,0:T(8,128)(2,1)S(1)}, bf16[576,128]{1,0:T(8,128)(2,1)S(1)}, u32[]{:S(2)}, u32[]{:S(2)}) collective-permute-start(bf16[576,128]{1,0:T(8,128)(2,1)S(1)} %add_convert_fusion), channel_id=1, source_target_pairs={{0,2},{1,3},{2,0},{3,1},{4,6},{5,7},{6,4},{7,5},{8,10},{9,11},{10,... | collective-permute-start | bytes 442376 | tf_op jit(solution)/shard_map/ppermute | solution.py:29
  51.0 6.7 %collective-permute-start.10 = (bf16[448,128]{1,0:T(8,128)(2,1)S(1)}, bf16[448,128]{1,0:T(8,128)(2,1)S(1)}, u32[]{:S(2)}, u32[]{:S(2)}) collective-permute-start(bf16[448,128]{1,0:T(8,128)(2,1)S(1)} %add_convert_fusion.1), channel_id=1, source_target_pairs={{0,2},{1,3},{2,0},{3,1},{4,6},{5,7},{6,4},{7,5},{8,10},{9,11},{10,... | collective-permute-start | bytes 344072 | tf_op jit(solution)/shard_map/ppermute | solution.py:29
